TPU v7x, 512 devices: a whole 4x8x8 slice. The times are simulated.
512 devices in a mesh: dp: 32 (over x, z), group: 2 (over core), mp: 8 (over y).
Axes of the slice: x: 4, y: 8, z: 8, core: 2. Of those that a mesh axis runs over, the one named last changes fastest.
Arguments:
- teacher_rows: bfloat16 [20480, 5120], P('dp', ('group', 'mp')), may hold values from -500 to 500
- teacher_gain: bfloat16 [5120], P(('group', 'mp')), may hold values from 0.099609375 to 1.8984375
- teacher_head: bfloat16 [6144, 5120], P(('group', 'mp'), 'dp'), may hold values from -3 to 3
- student_rows: bfloat16 [20480, 2048], P('dp'), may hold values from -500 to 500
- student_gain: bfloat16 [2048], replicated, may hold values from 0.099609375 to 1.8984375
- student_head: bfloat16 [6144, 2048], P(('group', 'mp'), 'dp'), may hold values from -3 to 3
- lengths: int32 [32], P('dp'), may hold values from 384 to 640, as said below
Outputs:
- head_update: bfloat16 [6144, 2048], P(('group', 'mp'), 'dp')
- row_update: bfloat16 [20480, 2048], P(('dp', 'group', 'mp'))
Inputs may be any that keep to these rules, and one draw needn't show every extreme that they name: `lengths`: the first sequence has exactly 384 tokens and the last exactly 640.
All inputs are finite; a program needn't handle non-finite values.
Results may differ from a plain program's by a relative error of at most 0.023.
Values may be sent and summed in bfloat16 or wider, within the bound.
No kernel may reach another device: no remote copies, remote signals or barrier semaphores. Data moves between devices by JAX's collectives and lax.ppermute only.
A program may use at most 64 MiB of HBM per device.

v0:
```python
import jax
import jax.numpy as jnp
from jax import lax
from jax.sharding import PartitionSpec as P

DT = 5120
LMAX = 640


epsilon = 1e-06


def normalize(rows, gain):
    values = rows.astype(jnp.float32)
    mean_square = jnp.mean(values * values, axis=-1, keepdims=True)
    return (values * lax.rsqrt(mean_square + epsilon) * gain.astype(jnp.float32)).astype(
        jnp.bfloat16
    )


def against(rows, weights):
    return lax.dot_general(
        rows, weights, (((1,), (1,)), ((), ())), preferred_element_type=jnp.float32
    )


def body(
    teacher_rows, teacher_gain, teacher_head, student_rows, student_gain, student_head, lengths
):
    head_teacher, head_student = (
        lax.all_gather(teacher_head, "dp", axis=1, tiled=True),
        lax.all_gather(student_head, "dp", axis=1, tiled=True),
    )
    student_normed = normalize(student_rows, student_gain)
    tokens = student_rows.shape[0]
    values = teacher_rows.astype(jnp.float32)
    squares = lax.psum(jnp.sum(values * values, axis=1), ("group", "mp"))
    scale = lax.rsqrt(squares / DT + epsilon)
    teacher_normed = (values * scale[:, None] * teacher_gain.astype(jnp.float32)).astype(
        jnp.bfloat16
    )
    teacher_logits = against(
        lax.all_gather(teacher_normed, ("group", "mp"), axis=1, tiled=True), head_teacher
    )
    student_logits = against(student_normed, head_student)
    teacher_top, student_top = lax.pmax(
        (jnp.max(teacher_logits, axis=1), jnp.max(student_logits, axis=1)), ("group", "mp")
    )
    teacher_sum, student_sum = lax.psum(
        (
            jnp.sum(jnp.exp(teacher_logits - teacher_top[:, None]), axis=1),
            jnp.sum(jnp.exp(student_logits - student_top[:, None]), axis=1),
        ),
        ("group", "mp"),
    )
    teacher_lse = teacher_top + jnp.log(teacher_sum)
    student_lse = student_top + jnp.log(student_sum)
    position = jnp.arange(tokens, dtype=jnp.int32) % LMAX
    live = (position < jnp.repeat(lengths, LMAX, total_repeat_length=tokens)).astype(jnp.float32)
    teacher_prob = jnp.exp(teacher_logits - teacher_lse[:, None])
    student_prob = jnp.exp(student_logits - student_lse[:, None])
    logit_grad = (live[:, None] * (student_prob - teacher_prob)).astype(jnp.bfloat16)
    head_grad = (
        lax.psum_scatter(
            lax.dot_general(
                student_normed,
                logit_grad,
                (((0,), (0,)), ((), ())),
                preferred_element_type=jnp.float32,
            ).astype(jnp.bfloat16),
            "dp",
            scatter_dimension=0,
            tiled=True,
        )
        .astype(jnp.float32)
        .T
    )
    rows = lax.slice_in_dim(
        logit_grad,
        0,
        tokens // lax.axis_size(("group", "mp")) * lax.axis_size(("group", "mp")),
        axis=0,
    )
    row_grad = lax.psum_scatter(
        jnp.dot(rows, head_student, preferred_element_type=jnp.float32).astype(jnp.bfloat16),
        ("group", "mp"),
        scatter_dimension=0,
        tiled=True,
    ).astype(jnp.float32)
    devices = lax.axis_size(("dp", "group", "mp"))
    head_square, row_square = lax.psum(
        (jnp.sum(head_grad * head_grad), jnp.sum(row_grad * row_grad)), ("dp", "group", "mp")
    )
    head_update = head_grad * lax.rsqrt(head_square / (head_grad.size * devices) + epsilon)
    row_update = row_grad * lax.rsqrt(row_square / (row_grad.size * devices) + epsilon)
    return (head_update.astype(jnp.bfloat16), row_update.astype(jnp.bfloat16))


def solution(mesh):
    placed = (
        P("dp", ("group", "mp")),
        P(("group", "mp")),
        P(("group", "mp"), "dp"),
        P("dp", None),
        P(),
        P(("group", "mp"), "dp"),
        P("dp"),
    )
    return jax.shard_map(
        body,
        mesh=mesh,
        in_specs=placed,
        out_specs=(P(("group", "mp"), "dp"), P(("dp", "group", "mp"), None)),
        check_vma=False,
    )
```

profile of v0, /device:TPU:1, one launch (start us, length us, event | category | flops | bytes accessed | tf_op | source)
XLA Modules:
  0.0 709.9 jit_solution(17062500374979216916)
XLA Ops:
  7.2 0.0 all-gather.4.cloned.1.call-start
  7.2 0.7 all-gather.4.cloned.1.call-update
  7.9 0.0 all-gather.8.cloned.1.call-start
  7.9 0.7 all-gather.8.cloned.1.call-update
  8.6 0.0 all-gather.6.cloned.1.call-start
  8.7 0.7 convert_element_type.54
  9.4 1.1 fusion.3
  10.5 29.6 %psum.36 = f32[640]{0:T(1024)S(1)} all-reduce(f32[640]{0:T(1024)S(1)} %fusion.3), channel_id=1, replica_groups=mesh['dp'=32,'group'=2,'mp'=8] {'group','mp'}, use_global_device_ids=true, to_apply=%region_6.0 | all-reduce | flops 640 | bytes 5120 | tf_op jit(solution)/shard_map/psum | solution.py:37
  40.1 1.9 fusion.5
  41.9 0.0 all-gather.6.cloned.1.call-update
  42.0 0.0 reduce-scatter.3.cloned.1.call-start
  42.0 0.7 convert_element_type.50
  43.4 2.3 fusion
  45.7 50.5 %all-gather.4.cloned.1.call-done = bf16[384,2048]{0,1:T(8,128)(2,1)} async-done(((bf16[384,64]{0,1:T(8,128)(2,1)}), bf16[384,2048]{0,1:T(8,128)(2,1)}) %all-gather.4.cloned.1.call-update) | async-done | bytes 1572880 | tf_op jit(solution)/shard_map/all_gather | solution.py:32
  96.2 3.8 fusion.16
  100.0 84.1 %all-gather.8.cloned.1.call-done = bf16[384,5120]{0,1:T(8,128)(2,1)} async-done(((bf16[384,160]{0,1:T(8,128)(2,1)}), bf16[384,5120]{0,1:T(8,128)(2,1)}) %all-gather.8.cloned.1.call-update) | async-done | bytes 3932176 | tf_op jit(solution)/shard_map/all_gather | solution.py:31
  184.1 52.3 %all-gather.6.cloned.1.call-done = bf16[640,5120]{0,1:T(8,128)(2,1)} async-done(((bf16[640,320]{0,1:T(8,128)(2,1)}), bf16[640,5120]{0,1:T(8,128)(2,1)}) %all-gather.6.cloned.1.call-update) | async-done | bytes 6553616 | tf_op jit(solution)/shard_map/all_gather | solution.py:43
  236.4 7.3 %fusion.15 = (f32[640]{0:T(1024)S(1)}, f32[640,384]{0,1:T(8,128)S(1)}) fusion(bf16[640,5120]{0,1:T(8,128)(2,1)} %all-gather.6.cloned.1.call-done, bf16[384,5120]{0,1:T(8,128)(2,1)} %all-gather.8.cloned.1.call-done), kind=kOutput, calls=%fused_computation.31 | convolution fusion | flops 2516827648 | bytes 11471360 | tf_op jit(solution)/shard_map/dot_general | solution.py:22
  243.7 28.1 %all-reduce.2 = (f32[640]{0:T(1024)S(1)}, f32[640]{0:T(1024)S(1)}) all-reduce(f32[640]{0:T(1024)S(1)} %get-tuple-element.32, f32[640]{0:T(1024)S(1)} %get-tuple-element.34), channel_id=1, replica_groups=mesh['dp'=32,'group'=2,'mp'=8] {'group','mp'}, use_global_device_ids=true, to_apply=%region_8.0 | all-reduce | flops 1280 | bytes 10240 | tf_op jit(solution)/shard_map/pmax | solution.py:46
  271.8 0.3 exponential_reduce_fusion
  272.1 27.6 %all-reduce.1 = (f32[640]{0:T(1024)S(1)}, f32[640]{0:T(1024)S(1)}) all-reduce(f32[640]{0:T(1024)S(1)} %get-tuple-element.36, f32[640]{0:T(1024)S(1)} %get-tuple-element.37), channel_id=1, replica_groups=mesh['dp'=32,'group'=2,'mp'=8] {'group','mp'}, use_global_device_ids=true, to_apply=%region_10.0 | all-reduce | flops 1280 | bytes 10240 | tf_op jit(solution)/shard_map/psum | solution.py:49
  299.7 0.3 multiply_convert_fusion
  300.0 0.0 copy-start
  300.0 4.8 convolution_convert_fusion.1
  304.8 0.0 reduce-scatter.3.cloned.1.call-update
  304.8 0.0 reduce-scatter.5.cloned.1.call-start
  304.9 0.0 copy-done
  304.9 3.1 convolution_convert_fusion
  308.0 0.0 reduce-scatter.5.cloned.1.call-update
  308.0 215.2 %reduce-scatter.3.cloned.1.call-done = bf16[64,384]{1,0:T(8,128)(2,1)} async-done(((bf16[2048,384]{1,0:T(8,128)(2,1)}), bf16[64,384]{1,0:T(8,128)(2,1)}) %reduce-scatter.3.cloned.1.call-update) | async-done | bytes 49168 | tf_op jit(solution)/shard_map/reduce_scatter | solution.py:64
  523.2 1.4 fusion.11
  524.6 73.6 %reduce-scatter.5.cloned.1.call-done = bf16[40,2048]{1,0:T(8,128)(2,1)} async-done(((bf16[640,2048]{1,0:T(8,128)(2,1)}), bf16[40,2048]{1,0:T(8,128)(2,1)}) %reduce-scatter.5.cloned.1.call-update) | async-done | bytes 163856 | tf_op jit(solution)/shard_map/reduce_scatter | solution.py:84
  598.2 1.6 fusion.9
  599.8 99.1 %all-reduce = (f32[]{:T(128)}, f32[]{:T(128)}) all-reduce(f32[]{:T(128)} %fusion.11, f32[]{:T(128)} %fusion.9), channel_id=1, replica_groups=mesh['dp'=32,'group'=2,'mp'=8] {'dp','group','mp'}, use_global_device_ids=true, to_apply=%region_13.14 | all-reduce | flops 2 | bytes 16 | tf_op jit(solution)/shard_map/psum | solution.py:91
  700.3 1.4 fusion.13
  701.7 1.6 fusion.10
  (5 shorter events, 0.0 us)
Async XLA Ops:
  7.2 89.1 %all-gather.4.cloned.1.call-start = ((), (), s32[]{:S(2)}) async-start(), calls=%async_computation.2 | async-start | bytes 1622016 | tf_op jit(solution)/shard_map/all_gather | solution.py:32
  7.9 176.2 %all-gather.8.cloned.1.call-start = ((), (), s32[]{:S(2)}) async-start(), calls=%async_computation.4 | async-start | bytes 4055040 | tf_op jit(solution)/shard_map/all_gather | solution.py:31
  8.6 227.8 %all-gather.6.cloned.1.call-start = ((), (), s32[]{:S(2)}) async-start(), calls=%async_computation.3 | async-start | bytes 6963200 | tf_op jit(solution)/shard_map/all_gather | solution.py:43
  42.0 481.2 %reduce-scatter.3.cloned.1.call-start = ((), (), s32[]{:S(2)}) async-start(), calls=%async_computation.5 | async-start | bytes 1622016 | tf_op jit(solution)/shard_map/reduce_scatter | solution.py:64
  300.0 4.9 copy-start
  304.8 293.4 %reduce-scatter.5.cloned.1.call-start = ((), (), s32[]{:S(2)}) async-start(), calls=%async_computation.6 | async-start | bytes 2785280 | tf_op jit(solution)/shard_map/reduce_scatter | solution.py:84
Sparse Core Ops, SparseCore 0:
  11.2 85.0 all-gather.3
  99.4 84.6 all-gather.7
  186.2 50.1 all-gather.5
  305.0 218.1 reduce-scatter.2
  525.8 72.2 reduce-scatter.4
where the time goes:
time: 710 us
  waiting for transfers between devices  477 us (67%)
  blocking collectives  184 us (26%)
  matrix products  18.9 us (3%)
  between operations  15.9 us (2%)
  other arithmetic  13.4 us (2%)
    reduce_scatter x1, waiting for transfers between devices, body(): lax.psum_scatter(lax.dot_general(student_normed, logit_grad, (((0,), (0,)...  215 us
    psum x1, blocking collectives, body(): lax.psum((jnp.sum(head_grad * head_grad), jnp.sum(row_grad * row_grad)),...  99.1 us
    all_gather x1, waiting for transfers between devices, body(): lax.all_gather(teacher_head, 'dp', axis=1, tiled=True)  84.1 us
    reduce_scatter x1, waiting for transfers between devices, body(): lax.psum_scatter(jnp.dot(rows, head_student, preferred_element_type=jnp.f...  73.6 us
    all_gather x1, waiting for transfers between devices, body(): lax.all_gather(teacher_normed, ('group', 'mp'), axis=1, tiled=True)  52.3 us
    all_gather x1, waiting for transfers between devices, body(): lax.all_gather(student_head, 'dp', axis=1, tiled=True)  50.5 us
    psum x1, blocking collectives, body(): squares = lax.psum(jnp.sum(values * values, axis=1), ('group', 'mp'))  29.6 us
    pmax x1, blocking collectives, body(): lax.pmax((jnp.max(teacher_logits, axis=1), jnp.max(student_logits, axis=1...  28.1 us
  transfers between devices with their start and end apart: 5, of which 5 were waited for; matrix products, arithmetic and copies ran while one was open for 2% of the time, Pallas kernels for 0%

commit v1 on v0

v1 whole, which is shorter than its diff:
```python
import jax
import jax.numpy as jnp
from jax import lax
from jax.sharding import Mesh, PartitionSpec as P

F32 = jnp.float32
BF16 = jnp.bfloat16
DT = 5120
NX, NZ, NC, NY = 4, 8, 2, 8
epsilon = 1e-06


def split3(values):
    high = values.astype(BF16)
    rest = values - high.astype(F32)
    middle = rest.astype(BF16)
    low = (rest - middle.astype(F32)).astype(BF16)
    return high, middle, low


def normalize(rows, gain):
    values = rows.astype(F32)
    mean_square = jnp.mean(values * values, axis=-1, keepdims=True)
    return (values * lax.rsqrt(mean_square + epsilon) * gain.astype(F32)).astype(BF16)


def shifted(values, axis, size, by):
    return lax.ppermute(values, axis, [(i, (i + by) % size) for i in range(size)])


def body(
    teacher_rows, teacher_gain, teacher_head, student_rows, student_gain, student_head, lengths
):
    tokens = student_rows.shape[0]
    ft, fs = teacher_head.shape[1], student_head.shape[1]
    vocab = teacher_head.shape[0]
    z = lax.axis_index("z")
    c = lax.axis_index("core")

    block = teacher_rows.T
    wide = block.shape[0]
    values = block.astype(F32)
    scaled = (values * teacher_gain.astype(F32)[:, None]).astype(BF16)
    squares = jnp.stack(split3(jnp.sum(values * values, axis=0)), axis=0)
    sent = jnp.concatenate([scaled, jnp.pad(squares, ((0, 13), (0, 0)))], axis=0)
    rows = lax.all_gather(sent, ("core", "y"), axis=0, tiled=False)

    heads = jnp.concatenate([student_head.T, teacher_head.T], axis=0)
    own = lax.all_gather(heads, "x", axis=0, tiled=False)
    student_w = jnp.zeros((NX, NZ, fs, vocab), BF16)
    teacher_w = jnp.zeros((NX, NZ, ft, vocab), BF16)

    def place(ws, part, at):
        s, t = ws
        s = lax.dynamic_update_slice(s, part[:, None, :fs], (0, at, 0, 0))
        t = lax.dynamic_update_slice(t, part[:, None, fs:], (0, at, 0, 0))
        return s, t

    ws = place((student_w, teacher_w), own, z)
    right = left = own
    for step in range(1, NZ // 2 + 1):
        right = shifted(right, "z", NZ, 1)
        if step < NZ // 2:
            left = shifted(left, "z", NZ, -1)
        ws = place(ws, right, (z - step) % NZ)
        if step < NZ // 2:
            ws = place(ws, left, (z + step) % NZ)
    student_w = ws[0].reshape(NX * NZ * fs, vocab)
    teacher_w = ws[1].reshape(NC * NY, wide, vocab)

    student_normed = normalize(student_rows, student_gain)
    student_logits = jnp.dot(student_normed, student_w, preferred_element_type=F32)
    total = jnp.sum(rows[:, wide : wide + 3].astype(F32), axis=(0, 1))
    scale = lax.rsqrt(total / DT + epsilon)
    teacher_logits = (
        lax.dot_general(
            rows[:, :wide],
            teacher_w,
            (((0, 1), (0, 1)), ((), ())),
            preferred_element_type=F32,
        )
        * scale[:, None]
    )

    tops = [jnp.max(v, axis=1) for v in (teacher_logits, student_logits)]
    sums = [
        jnp.sum(jnp.exp(v - top[:, None]), axis=1)
        for v, top in zip((teacher_logits, student_logits), tops)
    ]
    stats = jnp.stack(tops + sums, axis=0)
    stats = jnp.broadcast_to(stats[None], (NC * NY,) + stats.shape)
    stats = lax.all_to_all(stats, ("core", "y"), 0, 0, tiled=True)
    top = jnp.max(stats[:, :2], axis=0)
    lse = top + jnp.log(jnp.sum(stats[:, 2:] * jnp.exp(stats[:, :2] - top), axis=0))
    live = (jnp.arange(tokens, dtype=jnp.int32) < lengths[0]).astype(F32)
    logit_grad = (
        live[:, None]
        * (jnp.exp(student_logits - lse[1][:, None]) - jnp.exp(teacher_logits - lse[0][:, None]))
    ).astype(BF16)

    row_part = lax.dot_general(
        logit_grad, student_w, (((1,), (1,)), ((), ())), preferred_element_type=F32
    )
    half = tokens // NC
    mine = lax.dynamic_slice_in_dim(row_part, c * half, half, 0)
    other = lax.dynamic_slice_in_dim(row_part, (1 - c) * half, half, 0).astype(BF16)
    mine = (mine + lax.ppermute(other, "core", [(0, 1), (1, 0)]).astype(F32)).astype(BF16)
    row_grad = lax.psum_scatter(mine, "y", scatter_dimension=0, tiled=True).astype(F32)

    head_part = lax.dot_general(
        student_normed, logit_grad, (((0,), (0,)), ((), ())), preferred_element_type=F32
    ).astype(BF16)
    head_part = lax.all_to_all(head_part.reshape(NX, NZ * fs, vocab), "x", 0, 0, tiled=True)
    head_part = jnp.sum(head_part.astype(F32), axis=0).astype(BF16)
    head_part = lax.all_to_all(head_part.reshape(NZ, fs, vocab), "z", 0, 0, tiled=True)
    head_grad = jnp.sum(head_part.astype(F32), axis=0)

    devices = NX * NZ * NC * NY
    squares = jnp.stack([jnp.sum(head_grad * head_grad), jnp.sum(row_grad * row_grad)])
    squares = jnp.broadcast_to(squares[None, :, None], (devices, 2, 64)).reshape(devices, 128)
    squares = lax.all_to_all(squares, ("x", "z", "core", "y"), 0, 0, tiled=True)
    squares = jnp.sum(squares, axis=0)
    head_update = head_grad * lax.rsqrt(squares[0] / (head_grad.size * devices) + epsilon)
    row_update = row_grad * lax.rsqrt(squares[64] / (row_grad.size * devices) + epsilon)
    return (head_update.astype(BF16).T, row_update.astype(BF16))


def solution(mesh):
    mesh = Mesh(mesh.devices.reshape(NX, NZ, NC, NY), ("x", "z", "core", "y"))
    dp, mp = ("x", "z"), ("core", "y")
    placed = (P(dp, mp), P(mp), P(mp, dp), P(dp, None), P(), P(mp, dp), P(dp))
    return jax.shard_map(
        body,
        mesh=mesh,
        in_specs=placed,
        out_specs=(P(mp, dp), P(dp + mp, None)),
        check_vma=False,
    )
```

time: 710 us -> 232 us (0.33)
  waiting for transfers between devices: 477 us -> 47.2 us
  blocking collectives: 184 us -> 78.6 us
  starting transfers between devices: 0.2 us -> 44.4 us
  local copies, waits for them, and re-layouts: 0.01 us -> 12.1 us
    reduce_scatter x2 -> x1, waiting for transfers between devices: 289 us -> 0.01 us  [body(): lax.psum_scatter(mine, 'y', scatter_dimension=0, tiled=True).astype(F32)]
    all_gather x3 -> x1, waiting for transfers between devices: 187 us -> 0.01 us  [body(): rows = lax.all_gather(sent, ('core', 'y'), axis=0, tiled=False)]
    psum x3 -> x0, blocking collectives: 156 us -> none  [the longest x1 99.1 us: body(): lax.psum((jnp.sum(head_grad * head_grad), jnp.sum(row_grad * row_grad)),...]
    all_to_all x0 -> x3, blocking collectives: none -> 67.2 us  [the longest x1 28.7 us: body(): squares = lax.all_to_all(squares, ('x', 'z', 'core', 'y'), 0, 0, tiled=True)]
    ppermute x0 -> x8, waiting for transfers between devices: none -> 40.1 us  [the longest x7 37.1 us: shifted(): lax.ppermute(values, axis, [(i, (i + by) % size) for i in range(size)])]
    ppermute x0 -> x8, starting transfers between devices: none -> 31.7 us  [the longest x7 28.8 us: shifted(): lax.ppermute(values, axis, [(i, (i + by) % size) for i in range(size)])]
    pmax x1 -> x0, blocking collectives: 28.1 us -> none  [body(): lax.pmax((jnp.max(teacher_logits, axis=1), jnp.max(student_logits, axis=1...]
    all_to_all x0 -> x1, starting transfers between devices: none -> 12.5 us  [body(): stats = lax.all_to_all(stats, ('core', 'y'), 0, 0, tiled=True)]
  transfers between devices with their start and end apart: 5 -> 11, of which waited for: 5 -> 6; matrix products, arithmetic and copies ran while one was open for 2% -> 6% of each run, Pallas kernels for 0% -> 0%
where the time goes in v1:
time: 232 us; the launch traced here: 231 us
  blocking collectives  78.6 us (34%)
  waiting for transfers between devices  47.2 us (20%)
  starting transfers between devices  44.4 us (19%)
  other arithmetic  19.7 us (8%)
  between operations  16.7 us (7%)
  matrix products  12.4 us (5%)
  local copies, waits for them, and re-layouts  12.1 us (5%)
    ppermute x7, waiting for transfers between devices, shifted(): lax.ppermute(values, axis, [(i, (i + by) % size) for i in range(size)])  37.1 us
    ppermute x7, starting transfers between devices, shifted(): lax.ppermute(values, axis, [(i, (i + by) % size) for i in range(size)])  28.8 us
    all_to_all x1, blocking collectives, body(): squares = lax.all_to_all(squares, ('x', 'z', 'core', 'y'), 0, 0, tiled=True)  28.7 us
    all_to_all x1, blocking collectives, body(): lax.all_to_all(head_part.reshape(NX, NZ * fs, vocab), 'x', 0, 0, tiled=True)  22.8 us
    all_to_all x1, blocking collectives, body(): lax.all_to_all(head_part.reshape(NZ, fs, vocab), 'z', 0, 0, tiled=True)  15.7 us
    all_to_all x1, starting transfers between devices, body(): stats = lax.all_to_all(stats, ('core', 'y'), 0, 0, tiled=True)  12.5 us
    all_gather x1, blocking collectives, body(): own = lax.all_gather(heads, 'x', axis=0, tiled=False)  11.4 us
    dot_general x1, matrix products, body(): lax.dot_general(rows[:, :wide], teacher_w, (((0, 1), (0, 1)), ((), ())),...  7.26 us
  transfers between devices with their start and end apart: 11, of which 6 were waited for; matrix products, arithmetic and copies ran while one was open for 6% of the time, Pallas kernels for 0%

profile of v1, /device:TPU:1, one launch (start us, length us, event | category | flops | bytes accessed | tf_op | source)
XLA Modules:
  0.0 231.0 jit_solution(10598037016983039830)
XLA Ops:
  7.2 0.0 all-gather.4.cloned.1.call-start
  7.2 0.7 convert_element_type.138
  7.9 1.1 fusion.24
  9.1 0.8 pad_maximum_fusion
  9.9 0.9 pad_maximum_fusion.1
  10.8 11.4 %all-gather = bf16[896,384]{1,0:T(8,128)(2,1)S(1)} all-gather(bf16[224,384]{1,0:T(8,128)(2,1)S(1)} %pad_maximum_fusion.1), channel_id=2, replica_groups=mesh['x'=4,'z'=8,'core'=2,'y'=8] {'x'}, dimensions={0}, use_global_device_ids=true | all-gather | bytes 860160 | tf_op jit(solution)/shard_map/all_gather | solution.py:49
  22.2 5.3 %collective-permute-start = (bf16[4,224,384]{2,1,0:T(8,128)(2,1)S(1)}, bf16[4,224,384]{2,1,0:T(8,128)(2,1)}, u32[]{:S(2)}, u32[]{:S(2)}) collective-permute-start(bf16[4,224,384]{2,1,0:T(8,128)(2,1)S(1)} %bitcast.110), channel_id=1, source_target_pairs={{0,16},{16,32},{32,48},{48,64},{64,80},{80,96},{96,112},{112,0},{1... | collective-permute-start | bytes 2064392 | tf_op jit(solution)/shard_map/ppermute | solution.py:28
  27.5 8.6 %collective-permute-start.1 = (bf16[4,224,384]{2,1,0:T(8,128)(2,1)S(1)}, bf16[4,224,384]{2,1,0:T(8,128)(2,1)S(1)}, u32[]{:S(2)}, u32[]{:S(2)}) collective-permute-start(bf16[4,224,384]{2,1,0:T(8,128)(2,1)S(1)} %bitcast.111), channel_id=1, source_target_pairs={{0,112},{16,0},{32,16},{48,32},{64,48},{80,64},{96,80},{112,96},{1... | collective-permute-start | bytes 2064392 | tf_op jit(solution)/shard_map/ppermute | solution.py:28
  36.3 2.4 %fusion.2 = f32[640]{0:T(1024)S(1)} fusion(bf16[640,2048]{1,0:T(8,128)(2,1)} %param.10), kind=kLoop, calls=%fused_computation.4 | loop fusion | flops 3931520 | bytes 2624000 | tf_op jit(solution)/shard_map/reduce_sum | solution.py:23
  38.7 0.2 broadcast_in_dim.78
  39.0 0.5 broadcast_in_dim.87
  39.5 0.1 fusion.23
  39.6 8.2 %collective-permute-done = bf16[4,224,384]{2,1,0:T(8,128)(2,1)} collective-permute-done((bf16[4,224,384]{2,1,0:T(8,128)(2,1)S(1)}, bf16[4,224,384]{2,1,0:T(8,128)(2,1)}, u32[]{:S(2)}, u32[]{:S(2)}) %collective-permute-start) | collective-permute-done | bytes 688160 | tf_op jit(solution)/shard_map/ppermute | solution.py:28
  47.8 1.9 collective-permute-start.2
  49.7 4.6 %collective-permute-start.3 = (bf16[4,224,384]{2,1,0:T(8,128)(2,1)S(1)}, bf16[4,224,384]{2,1,0:T(8,128)(2,1)S(1)}, u32[]{:S(2)}, u32[]{:S(2)}) collective-permute-start(bf16[4,224,384]{2,1,0:T(8,128)(2,1)S(1)} %collective-permute-done.1), channel_id=1, source_target_pairs={{0,112},{16,0},{32,16},{48,32},{64,48},{80,64},{96,80},{112,96},{1... | collective-permute-start | bytes 2064392 | tf_op jit(solution)/shard_map/ppermute | solution.py:28
  54.3 1.0 fusion.33
  55.3 1.1 fusion.22
  56.5 0.1 fusion.21
  56.5 8.7 %collective-permute-done.2 = bf16[4,224,384]{2,1,0:T(8,128)(2,1)S(1)} collective-permute-done((bf16[4,224,384]{2,1,0:T(8,128)(2,1)}, bf16[4,224,384]{2,1,0:T(8,128)(2,1)S(1)}, u32[]{:S(2)}, u32[]{:S(2)}) %collective-permute-start.2) | collective-permute-done | bytes 688160 | tf_op jit(solution)/shard_map/ppermute | solution.py:28
  65.2 1.9 collective-permute-start.4
  67.2 4.6 %collective-permute-start.5 = (bf16[4,224,384]{2,1,0:T(8,128)(2,1)S(1)}, bf16[4,224,384]{2,1,0:T(8,128)(2,1)S(1)}, u32[]{:S(2)}, u32[]{:S(2)}) collective-permute-start(bf16[4,224,384]{2,1,0:T(8,128)(2,1)S(1)} %collective-permute-done.3), channel_id=1, source_target_pairs={{0,112},{16,0},{32,16},{48,32},{64,48},{80,64},{96,80},{112,96},{1... | collective-permute-start | bytes 2064392 | tf_op jit(solution)/shard_map/ppermute | solution.py:28
  71.7 0.1 fusion.20
  71.9 0.1 fusion.19
  72.0 9.5 %collective-permute-done.4 = bf16[4,224,384]{2,1,0:T(8,128)(2,1)S(1)} collective-permute-done((bf16[4,224,384]{2,1,0:T(8,128)(2,1)S(1)}, bf16[4,224,384]{2,1,0:T(8,128)(2,1)S(1)}, u32[]{:S(2)}, u32[]{:S(2)}) %collective-permute-start.4) | collective-permute-done | bytes 688160 | tf_op jit(solution)/shard_map/ppermute | solution.py:28
  81.5 1.9 collective-permute-start.6
  83.4 0.1 fusion.18
  83.5 0.1 fusion.17
  83.7 2.5 %copy.42 = bf16[4,8,160,384]{3,2,1,0:T(8,128)(2,1)} copy(bf16[4,8,160,384]{3,2,0,1:T(8,128)(2,1)S(1)} %fusion.17) | data formatting | bytes 7864320 | tf_op jit(solution)/shard_map/dynamic_update_slice | solution.py:56
  86.2 10.7 %collective-permute-done.6 = bf16[4,224,384]{2,1,0:T(8,128)(2,1)S(1)} collective-permute-done((bf16[4,224,384]{2,1,0:T(8,128)(2,1)S(1)}, bf16[4,224,384]{2,1,0:T(8,128)(2,1)S(1)}, u32[]{:S(2)}, u32[]{:S(2)}) %collective-permute-start.6) | collective-permute-done | bytes 688160 | tf_op jit(solution)/shard_map/ppermute | solution.py:28
  97.0 1.7 fusion.45
  98.7 0.2 exponential_reduce_fusion
  98.8 0.9 fusion.16
  99.7 1.0 convert_reduce_fusion.1
  100.7 7.3 %fusion.46 = (f32[640]{0:T(1024)S(1)}, f32[640,384]{0,1:T(8,128)S(1)}) fusion(f32[640]{0:T(1024)S(1)} %add_rsqrt_fusion, bf16[16,320,384]{2,1,0:T(8,128)(2,1)} %bitcast.31, bf16[16,336,640]{2,1,0:T(8,128)(2,1)} %bitcast.120), kind=kOutput, calls=%fused_computation.88 | convolution fusion | flops 2517073408 | bytes 11473920 | tf_op jit(solution)/shard_map/dot_general | solution.py:76
  108.0 0.2 exponential_reduce_fusion.1
  108.2 0.7 broadcast_in_dim.96
  108.9 12.5 %all-to-all-start = ((f32[16,4,640]{2,1,0:T(4,128)}), f32[16,4,640]{2,1,0:T(4,128)}, u32[]{:S(2)}, u32[]{:S(2)}) async-start(f32[16,4,640]{2,1,0:T(4,128)} %broadcast_in_dim.96), calls=%async_computation | async-start | bytes 327680 | tf_op jit(solution)/shard_map/all_to_all | solution.py:92
  121.3 0.2 reduce-scatter.2.cloned.1.call-start
  122.2 7.0 %all-to-all-done = f32[16,4,640]{2,1,0:T(4,128)} async-done(((f32[16,4,640]{2,1,0:T(4,128)}), f32[16,4,640]{2,1,0:T(4,128)}, u32[]{:S(2)}, u32[]{:S(2)}) %all-to-all-start) | async-done | bytes 163872 | tf_op jit(solution)/shard_map/all_to_all | solution.py:92
  129.3 1.0 slice_reduce_fusion
  130.2 1.1 fusion.35
  131.4 0.3 multiply_convert_fusion
  131.7 1.6 fusion.47
  133.3 2.3 copy-done
  135.6 1.3 dynamic-slice_convert_fusion
  136.9 2.9 %collective-permute-start.7 = (bf16[320,2048]{1,0:T(8,128)(2,1)}, bf16[320,2048]{1,0:T(8,128)(2,1)}, u32[]{:S(2)}, u32[]{:S(2)}) collective-permute-start(bf16[320,2048]{1,0:T(8,128)(2,1)} %dynamic-slice_convert_fusion), channel_id=1, source_target_pairs={{0,8},{8,0},{1,9},{9,1},{2,10},{10,2},{3,11},{11,3},{4,12},{12,4},... | collective-permute-start | bytes 3932168 | tf_op jit(solution)/shard_map/ppermute | solution.py:107
  139.8 2.9 %collective-permute-done.7 = bf16[320,2048]{1,0:T(8,128)(2,1)} collective-permute-done((bf16[320,2048]{1,0:T(8,128)(2,1)}, bf16[320,2048]{1,0:T(8,128)(2,1)}, u32[]{:S(2)}, u32[]{:S(2)}) %collective-permute-start.7) | collective-permute-done | bytes 1310752 | tf_op jit(solution)/shard_map/ppermute | solution.py:107
  142.8 3.6 %add_convert_fusion = bf16[320,2048]{1,0:T(8,128)(2,1)} fusion(bf16[320,2048]{1,0:T(8,128)(2,1)} %collective-permute-done.7, f32[640,2048]{1,0:T(8,128)} %copy-done, s32[]{:T(128)S(6)} %select_n.84), kind=kLoop, calls=%fused_computation.8 | loop fusion | flops 1966080 | bytes 5242884 | tf_op jit(solution)/shard_map/convert_element_type | solution.py:107
  146.4 1.8 convolution_convert_fusion
  148.3 22.8 %all_to_all.21 = bf16[4,512,384]{2,1,0:T(8,128)(2,1)S(1)} all-to-all(bf16[4,512,384]{2,1,0:T(8,128)(2,1)S(1)} %bitcast.114), channel_id=1, replica_groups=mesh['x'=4,'z'=8,'core'=2,'y'=8] {'x'}, dimensions={0} | all-to-all | bytes 3145728 | tf_op jit(solution)/shard_map/all_to_all | solution.py:113
  171.1 0.4 reduce_sum.111
  171.5 15.7 %all_to_all.22 = bf16[8,64,384]{2,1,0:T(8,128)(2,1)S(1)} all-to-all(bf16[8,64,384]{2,1,0:T(8,128)(2,1)S(1)} %bitcast.115), channel_id=1, replica_groups=mesh['x'=4,'z'=8,'core'=2,'y'=8] {'z'}, dimensions={0} | all-to-all | bytes 786432 | tf_op jit(solution)/shard_map/all_to_all | solution.py:115
  187.2 0.1 convert_reduce_fusion
  187.3 0.6 multiply_reduce_fusion
  187.9 1.6 fusion.25
  189.5 1.4 pad_maximum_fusion.3
  190.9 0.1 broadcast_in_dim.97
  191.0 0.1 broadcast_in_dim.98
  191.1 0.1 broadcast_in_dim.99
  191.2 28.7 %all_to_all.23 = f32[512,1,128]{2,1,0:T(1,128)S(1)} all-to-all(f32[512,1,128]{2,1,0:T(1,128)S(1)} %broadcast_in_dim.99), channel_id=1, replica_groups=mesh['x'=4,'z'=8,'core'=2,'y'=8] {'x','z','core','y'}, dimensions={0} | all-to-all | bytes 524288 | tf_op jit(solution)/shard_map/all_to_all | solution.py:121
  219.9 0.1 reduce_sum.115
  220.0 0.6 fusion.44
  221.9 0.6 fusion.36
  222.5 1.6 fusion.26
  (43 shorter events, 0.5 us)
Async XLA Ops:
  7.2 29.1 %copy-start.5 = (bf16[2048]{0:T(1024)(128)(2,1)S(1)}, bf16[2048]{0:T(1024)(128)(2,1)}, u32[]{:S(2)}) copy-start(bf16[2048]{0:T(1024)(128)(2,1)} %param.11) | copy-start | bytes 12292
  7.2 92.5 %all-gather.4.cloned.1.call-start = ((), (), s32[]{:S(2)}) async-start(), calls=%async_computation.6 | async-start | bytes 7311360 | tf_op jit(solution)/shard_map/all_gather | solution.py:46
  22.2 25.5 %collective-permute-start = (bf16[4,224,384]{2,1,0:T(8,128)(2,1)S(1)}, bf16[4,224,384]{2,1,0:T(8,128)(2,1)}, u32[]{:S(2)}, u32[]{:S(2)}) collective-permute-start(bf16[4,224,384]{2,1,0:T(8,128)(2,1)S(1)} %bitcast.110), channel_id=1, source_target_pairs={{0,16},{16,32},{32,48},{48,64},{64,80},{80,96},{96,112},{112,0},{1... | collective-permute-start | bytes 2064392 | tf_op jit(solution)/shard_map/ppermute | solution.py:28
  27.5 22.2 %collective-permute-start.1 = (bf16[4,224,384]{2,1,0:T(8,128)(2,1)S(1)}, bf16[4,224,384]{2,1,0:T(8,128)(2,1)S(1)}, u32[]{:S(2)}, u32[]{:S(2)}) collective-permute-start(bf16[4,224,384]{2,1,0:T(8,128)(2,1)S(1)} %bitcast.111), channel_id=1, source_target_pairs={{0,112},{16,0},{32,16},{48,32},{64,48},{80,64},{96,80},{112,96},{1... | collective-permute-start | bytes 2064392 | tf_op jit(solution)/shard_map/ppermute | solution.py:28
  38.7 58.2 %copy-start.6 = (f32[640]{0:T(1024)}, f32[640]{0:T(1024)S(1)}, u32[]{:S(2)}) copy-start(f32[640]{0:T(1024)S(1)} %add_rsqrt_fusion.1) | copy-start | bytes 7684
  47.8 17.4 %collective-permute-start.2 = (bf16[4,224,384]{2,1,0:T(8,128)(2,1)}, bf16[4,224,384]{2,1,0:T(8,128)(2,1)S(1)}, u32[]{:S(2)}, u32[]{:S(2)}) collective-permute-start(bf16[4,224,384]{2,1,0:T(8,128)(2,1)} %collective-permute-done), channel_id=1, source_target_pairs={{0,16},{16,32},{32,48},{48,64},{64,80},{80,96},{96,112},{112,0},{1... | collective-permute-start | bytes 2064392 | tf_op jit(solution)/shard_map/ppermute | solution.py:28
  49.7 17.4 %collective-permute-start.3 = (bf16[4,224,384]{2,1,0:T(8,128)(2,1)S(1)}, bf16[4,224,384]{2,1,0:T(8,128)(2,1)S(1)}, u32[]{:S(2)}, u32[]{:S(2)}) collective-permute-start(bf16[4,224,384]{2,1,0:T(8,128)(2,1)S(1)} %collective-permute-done.1), channel_id=1, source_target_pairs={{0,112},{16,0},{32,16},{48,32},{64,48},{80,64},{96,80},{112,96},{1... | collective-permute-start | bytes 2064392 | tf_op jit(solution)/shard_map/ppermute | solution.py:28
  65.2 16.3 %collective-permute-start.4 = (bf16[4,224,384]{2,1,0:T(8,128)(2,1)S(1)}, bf16[4,224,384]{2,1,0:T(8,128)(2,1)S(1)}, u32[]{:S(2)}, u32[]{:S(2)}) collective-permute-start(bf16[4,224,384]{2,1,0:T(8,128)(2,1)S(1)} %collective-permute-done.2), channel_id=1, source_target_pairs={{0,16},{16,32},{32,48},{48,64},{64,80},{80,96},{96,112},{112,0},{1... | collective-permute-start | bytes 2064392 | tf_op jit(solution)/shard_map/ppermute | solution.py:28
  67.2 16.4 %collective-permute-start.5 = (bf16[4,224,384]{2,1,0:T(8,128)(2,1)S(1)}, bf16[4,224,384]{2,1,0:T(8,128)(2,1)S(1)}, u32[]{:S(2)}, u32[]{:S(2)}) collective-permute-start(bf16[4,224,384]{2,1,0:T(8,128)(2,1)S(1)} %collective-permute-done.3), channel_id=1, source_target_pairs={{0,112},{16,0},{32,16},{48,32},{64,48},{80,64},{96,80},{112,96},{1... | collective-permute-start | bytes 2064392 | tf_op jit(solution)/shard_map/ppermute | solution.py:28
  81.5 15.4 %collective-permute-start.6 = (bf16[4,224,384]{2,1,0:T(8,128)(2,1)S(1)}, bf16[4,224,384]{2,1,0:T(8,128)(2,1)S(1)}, u32[]{:S(2)}, u32[]{:S(2)}) collective-permute-start(bf16[4,224,384]{2,1,0:T(8,128)(2,1)S(1)} %collective-permute-done.4), channel_id=1, source_target_pairs={{0,16},{16,32},{32,48},{48,64},{64,80},{80,96},{96,112},{112,0},{1... | collective-permute-start | bytes 2064392 | tf_op jit(solution)/shard_map/ppermute | solution.py:28
  83.6 13.3 %copy-start.1 = (bf16[640,2048]{1,0:T(8,128)(2,1)S(1)}, bf16[640,2048]{1,0:T(8,128)(2,1)}, u32[]{:S(2)}) copy-start(bf16[640,2048]{1,0:T(8,128)(2,1)} %param.10) | copy-start | bytes 7864324
  108.9 20.4 %all-to-all-start = ((f32[16,4,640]{2,1,0:T(4,128)}), f32[16,4,640]{2,1,0:T(4,128)}, u32[]{:S(2)}, u32[]{:S(2)}) async-start(f32[16,4,640]{2,1,0:T(4,128)} %broadcast_in_dim.96), calls=%async_computation | async-start | bytes 327680 | tf_op jit(solution)/shard_map/all_to_all | solution.py:92
  121.3 66.6 %reduce-scatter.2.cloned.1.call-start = ((), (), s32[]{:S(2)}) async-start(), calls=%async_computation.5 | async-start | bytes 1474560 | tf_op jit(solution)/shard_map/reduce_scatter | solution.py:108
  131.7 1.6 copy-start.3
  133.3 2.3 %copy-start = (f32[640,2048]{1,0:T(8,128)}, f32[640,2048]{1,0:T(8,128)S(1)}, u32[]{:S(2)}) copy-start(f32[640,2048]{1,0:T(8,128)S(1)} %fusion.47) | copy-start | bytes 15728644
  136.9 5.9 %collective-permute-start.7 = (bf16[320,2048]{1,0:T(8,128)(2,1)}, bf16[320,2048]{1,0:T(8,128)(2,1)}, u32[]{:S(2)}, u32[]{:S(2)}) collective-permute-start(bf16[320,2048]{1,0:T(8,128)(2,1)} %dynamic-slice_convert_fusion), channel_id=1, source_target_pairs={{0,8},{8,0},{1,9},{9,1},{2,10},{10,2},{3,11},{11,3},{4,12},{12,4},... | collective-permute-start | bytes 3932168 | tf_op jit(solution)/shard_map/ppermute | solution.py:107
  139.8 6.6 %copy-start.2 = (bf16[640,2048]{1,0:T(8,128)(2,1)S(1)}, bf16[640,2048]{1,0:T(8,128)(2,1)}, u32[]{:S(2)}) copy-start(bf16[640,2048]{1,0:T(8,128)(2,1)} %param.10) | copy-start | bytes 7864324
  139.8 6.6 %copy-start.4 = (bf16[640,384]{0,1:T(8,128)(2,1)S(1)}, bf16[640,384]{0,1:T(8,128)(2,1)}, u32[]{:S(2)}) copy-start(bf16[640,384]{0,1:T(8,128)(2,1)} %copy-done.3) | copy-start | bytes 1474564
  139.8 6.6 %copy-start.7 = (f32[640]{0:T(1024)S(1)}, f32[640]{0:T(1024)}, u32[]{:S(2)}) copy-start(f32[640]{0:T(1024)} %copy-done.6) | copy-start | bytes 7684
Sparse Core Ops, SparseCore 0:
  10.1 57.0 all-gather.3
  146.5 30.3 reduce-scatter.1

commit v2 on v1

--- a/solution.py
+++ b/solution.py
@@ -34,7 +34,7 @@
     tokens = student_rows.shape[0]
     ft, fs = teacher_head.shape[1], student_head.shape[1]
     vocab = teacher_head.shape[0]
-    z = lax.axis_index("z")
+    x, z = lax.axis_index("x"), lax.axis_index("z")
     c = lax.axis_index("core")
 
     block = teacher_rows.T
@@ -45,26 +45,40 @@
     sent = jnp.concatenate([scaled, jnp.pad(squares, ((0, 13), (0, 0)))], axis=0)
     rows = lax.all_gather(sent, ("core", "y"), axis=0, tiled=False)
 
-    heads = jnp.concatenate([student_head.T, teacher_head.T], axis=0)
-    own = lax.all_gather(heads, "x", axis=0, tiled=False)
+    first = ft * 2 // 5
+    part_a = jnp.concatenate([student_head.T, teacher_head.T[:first]], axis=0)
+    part_b = teacher_head.T[first:]
+    own_a = lax.all_gather(part_a, "x", axis=0, tiled=False)
+    own_b = lax.all_gather(part_b, "z", axis=0, tiled=False)
     student_w = jnp.zeros((NX, NZ, fs, vocab), BF16)
     teacher_w = jnp.zeros((NX, NZ, ft, vocab), BF16)
 
-    def place(ws, part, at):
+    def place_a(ws, part, at):
         s, t = ws
         s = lax.dynamic_update_slice(s, part[:, None, :fs], (0, at, 0, 0))
         t = lax.dynamic_update_slice(t, part[:, None, fs:], (0, at, 0, 0))
         return s, t
 
-    ws = place((student_w, teacher_w), own, z)
-    right = left = own
+    def place_b(ws, part, at):
+        s, t = ws
+        return s, lax.dynamic_update_slice(t, part[None], (at, 0, first, 0))
+
+    ws = place_b(place_a((student_w, teacher_w), own_a, z), own_b, x)
+    right_b = shifted(own_b, "x", NX, 1)
+    left_b = shifted(own_b, "x", NX, -1)
+    far_b = shifted(right_b, "x", NX, 1)
+    right = left = own_a
     for step in range(1, NZ // 2 + 1):
         right = shifted(right, "z", NZ, 1)
         if step < NZ // 2:
             left = shifted(left, "z", NZ, -1)
-        ws = place(ws, right, (z - step) % NZ)
+        ws = place_a(ws, right, (z - step) % NZ)
         if step < NZ // 2:
-            ws = place(ws, left, (z + step) % NZ)
+            ws = place_a(ws, left, (z + step) % NZ)
+        if step == 1:
+            ws = place_b(place_b(ws, right_b, (x - 1) % NX), left_b, (x + 1) % NX)
+        if step == 3:
+            ws = place_b(ws, far_b, (x + 2) % NX)
     student_w = ws[0].reshape(NX * NZ * fs, vocab)
     teacher_w = ws[1].reshape(NC * NY, wide, vocab)
 
@@ -98,13 +112,18 @@
         * (jnp.exp(student_logits - lse[1][:, None]) - jnp.exp(teacher_logits - lse[0][:, None]))
     ).astype(BF16)
 
-    row_part = lax.dot_general(
-        logit_grad, student_w, (((1,), (1,)), ((), ())), preferred_element_type=F32
-    )
     half = tokens // NC
-    mine = lax.dynamic_slice_in_dim(row_part, c * half, half, 0)
-    other = lax.dynamic_slice_in_dim(row_part, (1 - c) * half, half, 0).astype(BF16)
-    mine = (mine + lax.ppermute(other, "core", [(0, 1), (1, 0)]).astype(F32)).astype(BF16)
+
+    def row_half(which):
+        return lax.dot_general(
+            lax.dynamic_slice_in_dim(logit_grad, which * half, half, 0),
+            student_w,
+            (((1,), (1,)), ((), ())),
+            preferred_element_type=F32,
+        )
+
+    other = lax.ppermute(row_half(1 - c).astype(BF16), "core", [(0, 1), (1, 0)])
+    mine = (row_half(c) + other.astype(F32)).astype(BF16)
     row_grad = lax.psum_scatter(mine, "y", scatter_dimension=0, tiled=True).astype(F32)
 
     head_part = lax.dot_general(

time: 232 us -> 260 us (1.12)
  waiting for transfers between devices: 47.2 us -> 20.8 us
  blocking collectives: 78.6 us -> 104 us
  local copies, waits for them, and re-layouts: 12.1 us -> 25.6 us
  starting transfers between devices: 44.4 us -> 57.5 us
  matrix products: 12.4 us -> 18.8 us
  other arithmetic: 19.7 us -> 15.4 us
    ppermute x7 -> x10, waiting for transfers between devices: 37.1 us -> 10.8 us  [shifted(): lax.ppermute(values, axis, [(i, (i + by) % size) for i in range(size)])]
    all_gather x1 -> x2, blocking collectives: 11.4 us -> 34.9 us  [the longest x1 23.4 us: body(): own_b = lax.all_gather(part_b, 'z', axis=0, tiled=False)]
    dynamic_update_slice x17 -> x20, local copies, waits for them, and re-layouts: 6.18 us -> 19.3 us  [the longest x5 8.52 us: place_b(): return (s, lax.dynamic_update_slice(t, part[None], (at, 0, first, 0)))]
    ppermute x7 -> x10, starting transfers between devices: 28.8 us -> 36.8 us  [shifted(): lax.ppermute(values, axis, [(i, (i + by) % size) for i in range(size)])]
    all_to_all x1, starting transfers between devices: 12.5 us -> 17.5 us  [body(): stats = lax.all_to_all(stats, ('core', 'y'), 0, 0, tiled=True)]
    dot_general x1 -> x2, matrix products: 1.59 us -> 5.77 us  [row_half(): lax.dot_general(lax.dynamic_slice_in_dim(logit_grad, which * half, half,...]
    convert_element_type x1 -> x0, other arithmetic: 3.62 us -> none  [body(): (mine + lax.ppermute(other, 'core', [(0, 1), (1, 0)]).astype(F32)).astype...]
  transfers between devices with their start and end apart: 11 -> 14, of which waited for: 6 -> 5; matrix products, arithmetic and copies ran while one was open for 6% -> 12% of each run, Pallas kernels for 0% -> 0%
where the time goes in v2:
time: 260 us; the launch traced here: 258 us
  blocking collectives  104 us (40%)
  starting transfers between devices  57.5 us (22%)
  local copies, waits for them, and re-layouts  25.6 us (10%)
  waiting for transfers between devices  20.8 us (8%)
  matrix products  18.8 us (7%)
  between operations  16.7 us (6%)
  other arithmetic  15.4 us (6%)
    ppermute x10, starting transfers between devices, shifted(): lax.ppermute(values, axis, [(i, (i + by) % size) for i in range(size)])  36.8 us
    all_to_all x1, blocking collectives, body(): squares = lax.all_to_all(squares, ('x', 'z', 'core', 'y'), 0, 0, tiled=True)  29.7 us
    all_to_all x1, blocking collectives, body(): lax.all_to_all(head_part.reshape(NX, NZ * fs, vocab), 'x', 0, 0, tiled=True)  23.9 us
    all_gather x1, blocking collectives, body(): own_b = lax.all_gather(part_b, 'z', axis=0, tiled=False)  23.4 us
    all_to_all x1, starting transfers between devices, body(): stats = lax.all_to_all(stats, ('core', 'y'), 0, 0, tiled=True)  17.5 us
    all_to_all x1, blocking collectives, body(): lax.all_to_all(head_part.reshape(NZ, fs, vocab), 'z', 0, 0, tiled=True)  15.1 us
    all_gather x1, blocking collectives, body(): own_a = lax.all_gather(part_a, 'x', axis=0, tiled=False)  11.6 us
    ppermute x10, waiting for transfers between devices, shifted(): lax.ppermute(values, axis, [(i, (i + by) % size) for i in range(size)])  10.8 us
  transfers between devices with their start and end apart: 14, of which 5 were waited for; matrix products, arithmetic and copies ran while one was open for 12% of the time, Pallas kernels for 0%

profile of v2, /device:TPU:1, one launch (start us, length us, event | category | flops | bytes accessed | tf_op | source)
XLA Modules:
  0.0 258.5 jit_solution(6298449183415528546)
XLA Ops:
  7.2 0.7 convert_element_type.138
  7.9 1.3 fusion.17
  9.2 0.8 pad_maximum_fusion
  10.0 0.8 slice.105
  10.9 0.8 pad_maximum_fusion.1
  11.7 11.6 %all-gather = bf16[512,384]{1,0:T(8,128)(2,1)} all-gather(bf16[128,384]{1,0:T(8,128)(2,1)S(1)} %pad_maximum_fusion.1), channel_id=2, replica_groups=mesh['x'=4,'z'=8,'core'=2,'y'=8] {'x'}, dimensions={0}, use_global_device_ids=true | all-gather | bytes 491520 | tf_op jit(solution)/shard_map/all_gather | solution.py:51
  23.2 4.8 %collective-permute-start = (bf16[4,128,384]{2,1,0:T(8,128)(2,1)}, bf16[4,128,384]{2,1,0:T(8,128)(2,1)}, u32[]{:S(2)}, u32[]{:S(2)}) collective-permute-start(bf16[4,128,384]{2,1,0:T(8,128)(2,1)} %bitcast.3), channel_id=1, source_target_pairs={{0,16},{16,32},{32,48},{48,64},{64,80},{80,96},{96,112},{112,0},{1... | collective-permute-start | bytes 1179656 | tf_op jit(solution)/shard_map/ppermute | solution.py:28
  28.0 8.6 %collective-permute-start.1 = (bf16[4,128,384]{2,1,0:T(8,128)(2,1)}, bf16[4,128,384]{2,1,0:T(8,128)(2,1)}, u32[]{:S(2)}, u32[]{:S(2)}) collective-permute-start(bf16[4,128,384]{2,1,0:T(8,128)(2,1)} %bitcast.3), channel_id=1, source_target_pairs={{0,112},{16,0},{32,16},{48,32},{64,48},{80,64},{96,80},{112,96},{1... | collective-permute-start | bytes 1179656 | tf_op jit(solution)/shard_map/ppermute | solution.py:28
  36.6 0.9 slice.116
  37.5 23.4 %all-gather.2 = bf16[768,384]{1,0:T(8,128)(2,1)S(1)} all-gather(bf16[96,384]{1,0:T(8,128)(2,1)S(1)} %slice.116), channel_id=4, replica_groups=mesh['x'=4,'z'=8,'core'=2,'y'=8] {'z'}, dimensions={0}, use_global_device_ids=true | all-gather | bytes 663552 | tf_op jit(solution)/shard_map/all_gather | solution.py:52
  60.8 1.9 collective-permute-start.7
  62.8 4.6 %collective-permute-start.8 = (bf16[8,96,384]{2,1,0:T(8,128)(2,1)S(1)}, bf16[8,96,384]{2,1,0:T(8,128)(2,1)}, u32[]{:S(2)}, u32[]{:S(2)}) collective-permute-start(bf16[8,96,384]{2,1,0:T(8,128)(2,1)S(1)} %bitcast.127), channel_id=1, source_target_pairs={{0,384},{128,0},{256,128},{384,256},{1,385},{129,1},{257,129},{385... | collective-permute-start | bytes 1769480 | tf_op jit(solution)/shard_map/ppermute | solution.py:28
  67.3 2.4 broadcast_in_dim.99
  69.8 1.6 fusion.29
  71.4 0.6 fusion.2
  72.3 0.9 constant_dynamic-update-slice_fusion
  73.5 1.0 fusion.37
  74.4 3.4 %collective-permute-start.2 = (bf16[4,128,384]{2,1,0:T(8,128)(2,1)}, bf16[4,128,384]{2,1,0:T(8,128)(2,1)S(1)}, u32[]{:S(2)}, u32[]{:S(2)}) collective-permute-start(bf16[4,128,384]{2,1,0:T(8,128)(2,1)} %collective-permute-done), channel_id=1, source_target_pairs={{0,16},{16,32},{32,48},{48,64},{64,80},{80,96},{96,112},{112,0},{1... | collective-permute-start | bytes 1179656 | tf_op jit(solution)/shard_map/ppermute | solution.py:28
  77.9 3.1 %collective-permute-start.3 = (bf16[4,128,384]{2,1,0:T(8,128)(2,1)}, bf16[4,128,384]{2,1,0:T(8,128)(2,1)S(1)}, u32[]{:S(2)}, u32[]{:S(2)}) collective-permute-start(bf16[4,128,384]{2,1,0:T(8,128)(2,1)} %collective-permute-done.1), channel_id=1, source_target_pairs={{0,112},{16,0},{32,16},{48,32},{64,48},{80,64},{96,80},{112,96},{1... | collective-permute-start | bytes 1179656 | tf_op jit(solution)/shard_map/ppermute | solution.py:28
  81.0 1.6 fusion.28
  82.6 1.0 fusion.36
  83.6 1.6 fusion.27
  85.2 1.0 fusion.35
  86.2 1.9 collective-permute-start.9
  88.1 2.0 bitcast_dynamic-update-slice_fusion.1
  90.1 2.0 bitcast_dynamic-update-slice_fusion
  92.1 2.2 collective-permute-start.4
  94.3 4.3 %collective-permute-start.5 = (bf16[4,128,384]{2,1,0:T(8,128)(2,1)S(1)}, bf16[4,128,384]{2,1,0:T(8,128)(2,1)S(1)}, u32[]{:S(2)}, u32[]{:S(2)}) collective-permute-start(bf16[4,128,384]{2,1,0:T(8,128)(2,1)S(1)} %collective-permute-done.3), channel_id=1, source_target_pairs={{0,112},{16,0},{32,16},{48,32},{64,48},{80,64},{96,80},{112,96},{1... | collective-permute-start | bytes 1179656 | tf_op jit(solution)/shard_map/ppermute | solution.py:28
  98.6 0.7 fusion.26
  99.3 0.7 fusion.25
  100.1 2.0 collective-permute-done.4
  102.1 0.7 fusion.24
  102.8 0.5 collective-permute-done.5
  103.3 0.7 fusion.23
  104.0 0.9 bitcast_dynamic-update-slice_fusion.2
  104.9 2.7 %copy.51 = bf16[4,8,160,384]{3,2,1,0:T(8,128)(2,1)S(1)} copy(bf16[4,8,160,384]{3,2,0,1:T(8,128)(2,1)} %bitcast_dynamic-update-slice_fusion.2) | data formatting | bytes 7864320 | tf_op jit(solution)/shard_map/dynamic_update_slice | solution.py:64
  107.6 2.1 collective-permute-start.6
  109.8 8.3 %collective-permute-done.6 = bf16[4,128,384]{2,1,0:T(8,128)(2,1)S(1)} collective-permute-done((bf16[4,128,384]{2,1,0:T(8,128)(2,1)S(1)}, bf16[4,128,384]{2,1,0:T(8,128)(2,1)S(1)}, u32[]{:S(2)}, u32[]{:S(2)}) %collective-permute-start.6) | collective-permute-done | bytes 393248 | tf_op jit(solution)/shard_map/ppermute | solution.py:28
  118.2 1.6 fusion.50
  120.2 0.3 exponential_reduce_fusion
  120.5 1.0 convert_reduce_fusion.1
  121.5 7.7 %fusion.51 = (f32[640]{0:T(1024)S(1)}, f32[640,384]{1,0:T(8,128)S(1)}) fusion(f32[640]{0:T(1024)S(1)} %add_rsqrt_fusion, bf16[16,320,384]{2,1,0:T(8,128)(2,1)} %bitcast.125, bf16[16,336,640]{2,1,0:T(8,128)(2,1)} %bitcast.136), kind=kOutput, calls=%fused_computation.97 | convolution fusion | flops 2517073408 | bytes 11473920 | tf_op jit(solution)/shard_map/dot_general | solution.py:90
  129.2 0.3 exponential_reduce_fusion.1
  129.5 0.7 broadcast_in_dim.112
  130.2 17.5 %all-to-all-start = ((f32[16,4,640]{2,1,0:T(4,128)}), f32[16,4,640]{2,1,0:T(4,128)}, u32[]{:S(2)}, u32[]{:S(2)}) async-start(f32[16,4,640]{2,1,0:T(4,128)} %broadcast_in_dim.112), calls=%async_computation | async-start | bytes 327680 | tf_op jit(solution)/shard_map/all_to_all | solution.py:106
  148.4 7.2 %all-to-all-done = f32[16,4,640]{2,1,0:T(4,128)} async-done(((f32[16,4,640]{2,1,0:T(4,128)}), f32[16,4,640]{2,1,0:T(4,128)}, u32[]{:S(2)}, u32[]{:S(2)}) %all-to-all-start) | async-done | bytes 163872 | tf_op jit(solution)/shard_map/all_to_all | solution.py:106
  155.6 1.0 slice_reduce_fusion
  156.6 1.1 fusion.38
  157.7 1.2 multiply_convert_fusion
  158.9 2.9 %convolution_convert_fusion.1 = bf16[320,2048]{1,0:T(8,128)(2,1)} fusion(bf16[2048,384]{1,0:T(8,128)(2,1)S(1)} %bitcast.123, bf16[640,384]{1,0:T(8,128)(2,1)} %multiply_convert_fusion, s32[]{:T(128)S(6)} %select_n.116), kind=kOutput, calls=%fused_computation.10 | convolution fusion | flops 503971840 | bytes 3129348 | tf_op jit(solution)/shard_map/dot_general | solution.py:118
  161.8 3.1 %collective-permute-start.10 = (bf16[320,2048]{1,0:T(8,128)(2,1)}, bf16[320,2048]{1,0:T(8,128)(2,1)S(1)}, u32[]{:S(2)}, u32[]{:S(2)}) collective-permute-start(bf16[320,2048]{1,0:T(8,128)(2,1)} %convolution_convert_fusion.1), channel_id=1, source_target_pairs={{0,8},{8,0},{1,9},{9,1},{2,10},{10,2},{3,11},{11,3},{4,12},{12,4},... | collective-permute-start | bytes 3932168 | tf_op jit(solution)/shard_map/ppermute | solution.py:125
  164.9 2.7 %collective-permute-done.10 = bf16[320,2048]{1,0:T(8,128)(2,1)S(1)} collective-permute-done((bf16[320,2048]{1,0:T(8,128)(2,1)}, bf16[320,2048]{1,0:T(8,128)(2,1)S(1)}, u32[]{:S(2)}, u32[]{:S(2)}) %collective-permute-start.10) | collective-permute-done | bytes 1310752 | tf_op jit(solution)/shard_map/ppermute | solution.py:125
  167.6 2.9 %fusion.5 = bf16[320,2048]{1,0:T(8,128)(2,1)} fusion(bf16[2048,384]{1,0:T(8,128)(2,1)S(1)} %bitcast.124, bf16[320,2048]{1,0:T(8,128)(2,1)S(1)} %collective-permute-done.10, bf16[640,384]{1,0:T(8,128)(2,1)} %multiply_convert_fusion, s32[]{:T(128)S(6)} %select_n.115), kind=kOutput, calls=%fused_computation.9 | convolution fusion | flops 505282560 | bytes 4440068 | tf_op jit(solution)/shard_map/dot_general | solution.py:118
  170.5 3.7 %convolution_convert_fusion = bf16[2048,384]{1,0:T(8,128)(2,1)S(1)} fusion(bf16[640,384]{1,0:T(8,128)(2,1)} %multiply_convert_fusion, bf16[640,2048]{1,0:T(8,128)(2,1)} %param.10, f32[2048]{0:T(1024)S(1)} %convert_element_type.134, f32[640]{0:T(1024)S(1)} %copy-done.5), kind=kOutput, calls=%fused_computation.8 | convolution fusion | flops 1012662272 | bytes 4696576 | tf_op jit(solution)/shard_map/dot_general | solution.py:129
  174.2 23.9 %all_to_all.21 = bf16[4,512,384]{2,1,0:T(8,128)(2,1)S(1)} all-to-all(bf16[4,512,384]{2,1,0:T(8,128)(2,1)S(1)} %bitcast.129), channel_id=1, replica_groups=mesh['x'=4,'z'=8,'core'=2,'y'=8] {'x'}, dimensions={0} | all-to-all | bytes 3145728 | tf_op jit(solution)/shard_map/all_to_all | solution.py:132
  198.1 0.4 reduce_sum.111
  198.5 15.1 %all_to_all.22 = bf16[8,64,384]{2,1,0:T(8,128)(2,1)S(1)} all-to-all(bf16[8,64,384]{2,1,0:T(8,128)(2,1)S(1)} %bitcast.130), channel_id=1, replica_groups=mesh['x'=4,'z'=8,'core'=2,'y'=8] {'z'}, dimensions={0} | all-to-all | bytes 786432 | tf_op jit(solution)/shard_map/all_to_all | solution.py:134
  213.7 0.6 multiply_reduce_fusion
  214.3 1.6 fusion.18
  216.0 1.4 pad_maximum_fusion.3
  217.6 29.7 %all_to_all.23 = f32[512,1,128]{2,1,0:T(1,128)S(1)} all-to-all(f32[512,1,128]{2,1,0:T(1,128)S(1)} %broadcast_in_dim.115), channel_id=1, replica_groups=mesh['x'=4,'z'=8,'core'=2,'y'=8] {'x','z','core','y'}, dimensions={0} | all-to-all | bytes 524288 | tf_op jit(solution)/shard_map/all_to_all | solution.py:140
  247.4 0.6 fusion.49
  249.4 0.6 fusion.39
  250.0 1.6 fusion.19
  (50 shorter events, 1.4 us)
Async XLA Ops:
  7.2 113.4 %all-gather.5.cloned.1.call-start = ((), (), s32[]{:S(2)}) async-start(), calls=%async_computation.6 | async-start | bytes 7311360 | tf_op jit(solution)/shard_map/all_gather | solution.py:46
  7.9 63.5 %copy-start.1 = (bf16[640,2048]{1,0:T(8,128)(2,1)S(1)}, bf16[640,2048]{1,0:T(8,128)(2,1)}, u32[]{:S(2)}) copy-start(bf16[640,2048]{1,0:T(8,128)(2,1)} %param.10) | copy-start | bytes 7864324
  23.2 51.2 %collective-permute-start = (bf16[4,128,384]{2,1,0:T(8,128)(2,1)}, bf16[4,128,384]{2,1,0:T(8,128)(2,1)}, u32[]{:S(2)}, u32[]{:S(2)}) collective-permute-start(bf16[4,128,384]{2,1,0:T(8,128)(2,1)} %bitcast.3), channel_id=1, source_target_pairs={{0,16},{16,32},{32,48},{48,64},{64,80},{80,96},{96,112},{112,0},{1... | collective-permute-start | bytes 1179656 | tf_op jit(solution)/shard_map/ppermute | solution.py:28
  28.0 49.9 %collective-permute-start.1 = (bf16[4,128,384]{2,1,0:T(8,128)(2,1)}, bf16[4,128,384]{2,1,0:T(8,128)(2,1)}, u32[]{:S(2)}, u32[]{:S(2)}) collective-permute-start(bf16[4,128,384]{2,1,0:T(8,128)(2,1)} %bitcast.3), channel_id=1, source_target_pairs={{0,112},{16,0},{32,16},{48,32},{64,48},{80,64},{96,80},{112,96},{1... | collective-permute-start | bytes 1179656 | tf_op jit(solution)/shard_map/ppermute | solution.py:28
  37.5 34.7 %copy-start.3 = (bf16[2048]{0:T(1024)(128)(2,1)S(1)}, bf16[2048]{0:T(1024)(128)(2,1)}, u32[]{:S(2)}) copy-start(bf16[2048]{0:T(1024)(128)(2,1)} %param.11) | copy-start | bytes 12292
  60.8 25.4 %collective-permute-start.7 = (bf16[8,96,384]{2,1,0:T(8,128)(2,1)S(1)}, bf16[8,96,384]{2,1,0:T(8,128)(2,1)}, u32[]{:S(2)}, u32[]{:S(2)}) collective-permute-start(bf16[8,96,384]{2,1,0:T(8,128)(2,1)S(1)} %bitcast.126), channel_id=1, source_target_pairs={{0,128},{128,256},{256,384},{384,0},{1,129},{129,257},{257,385},{3... | collective-permute-start | bytes 1769480 | tf_op jit(solution)/shard_map/ppermute | solution.py:28
  62.8 27.4 %collective-permute-start.8 = (bf16[8,96,384]{2,1,0:T(8,128)(2,1)S(1)}, bf16[8,96,384]{2,1,0:T(8,128)(2,1)}, u32[]{:S(2)}, u32[]{:S(2)}) collective-permute-start(bf16[8,96,384]{2,1,0:T(8,128)(2,1)S(1)} %bitcast.127), channel_id=1, source_target_pairs={{0,384},{128,0},{256,128},{384,256},{1,385},{129,1},{257,129},{385... | collective-permute-start | bytes 1769480 | tf_op jit(solution)/shard_map/ppermute | solution.py:28
  72.0 46.2 %copy-start.4 = (f32[640]{0:T(1024)}, f32[640]{0:T(1024)S(1)}, u32[]{:S(2)}) copy-start(f32[640]{0:T(1024)S(1)} %add_rsqrt_fusion.1) | copy-start | bytes 7684
  74.4 17.6 %collective-permute-start.2 = (bf16[4,128,384]{2,1,0:T(8,128)(2,1)}, bf16[4,128,384]{2,1,0:T(8,128)(2,1)S(1)}, u32[]{:S(2)}, u32[]{:S(2)}) collective-permute-start(bf16[4,128,384]{2,1,0:T(8,128)(2,1)} %collective-permute-done), channel_id=1, source_target_pairs={{0,16},{16,32},{32,48},{48,64},{64,80},{80,96},{96,112},{112,0},{1... | collective-permute-start | bytes 1179656 | tf_op jit(solution)/shard_map/ppermute | solution.py:28
  77.9 16.4 %collective-permute-start.3 = (bf16[4,128,384]{2,1,0:T(8,128)(2,1)}, bf16[4,128,384]{2,1,0:T(8,128)(2,1)S(1)}, u32[]{:S(2)}, u32[]{:S(2)}) collective-permute-start(bf16[4,128,384]{2,1,0:T(8,128)(2,1)} %collective-permute-done.1), channel_id=1, source_target_pairs={{0,112},{16,0},{32,16},{48,32},{64,48},{80,64},{96,80},{112,96},{1... | collective-permute-start | bytes 1179656 | tf_op jit(solution)/shard_map/ppermute | solution.py:28
  86.2 17.8 %collective-permute-start.9 = (bf16[8,96,384]{2,1,0:T(8,128)(2,1)}, bf16[8,96,384]{2,1,0:T(8,128)(2,1)S(1)}, u32[]{:S(2)}, u32[]{:S(2)}) collective-permute-start(bf16[8,96,384]{2,1,0:T(8,128)(2,1)} %collective-permute-done.7), channel_id=1, source_target_pairs={{0,128},{128,256},{256,384},{384,0},{1,129},{129,257},{257,385},{3... | collective-permute-start | bytes 1769480 | tf_op jit(solution)/shard_map/ppermute | solution.py:28
  92.1 10.0 %collective-permute-start.4 = (bf16[4,128,384]{2,1,0:T(8,128)(2,1)S(1)}, bf16[4,128,384]{2,1,0:T(8,128)(2,1)S(1)}, u32[]{:S(2)}, u32[]{:S(2)}) collective-permute-start(bf16[4,128,384]{2,1,0:T(8,128)(2,1)S(1)} %collective-permute-done.2), channel_id=1, source_target_pairs={{0,16},{16,32},{32,48},{48,64},{64,80},{80,96},{96,112},{112,0},{1... | collective-permute-start | bytes 1179656 | tf_op jit(solution)/shard_map/ppermute | solution.py:28
  94.3 9.0 %collective-permute-start.5 = (bf16[4,128,384]{2,1,0:T(8,128)(2,1)S(1)}, bf16[4,128,384]{2,1,0:T(8,128)(2,1)S(1)}, u32[]{:S(2)}, u32[]{:S(2)}) collective-permute-start(bf16[4,128,384]{2,1,0:T(8,128)(2,1)S(1)} %collective-permute-done.3), channel_id=1, source_target_pairs={{0,112},{16,0},{32,16},{48,32},{64,48},{80,64},{96,80},{112,96},{1... | collective-permute-start | bytes 1179656 | tf_op jit(solution)/shard_map/ppermute | solution.py:28
  104.9 13.4 %copy-start.2 = (bf16[640,2048]{1,0:T(8,128)(2,1)S(1)}, bf16[640,2048]{1,0:T(8,128)(2,1)}, u32[]{:S(2)}) copy-start(bf16[640,2048]{1,0:T(8,128)(2,1)} %param.10) | copy-start | bytes 7864324
  107.6 10.5 %collective-permute-start.6 = (bf16[4,128,384]{2,1,0:T(8,128)(2,1)S(1)}, bf16[4,128,384]{2,1,0:T(8,128)(2,1)S(1)}, u32[]{:S(2)}, u32[]{:S(2)}) collective-permute-start(bf16[4,128,384]{2,1,0:T(8,128)(2,1)S(1)} %collective-permute-done.4), channel_id=1, source_target_pairs={{0,16},{16,32},{32,48},{48,64},{64,80},{80,96},{96,112},{112,0},{1... | collective-permute-start | bytes 1179656 | tf_op jit(solution)/shard_map/ppermute | solution.py:28
  118.2 2.0 copy-start
  130.2 25.4 %all-to-all-start = ((f32[16,4,640]{2,1,0:T(4,128)}), f32[16,4,640]{2,1,0:T(4,128)}, u32[]{:S(2)}, u32[]{:S(2)}) async-start(f32[16,4,640]{2,1,0:T(4,128)} %broadcast_in_dim.112), calls=%async_computation | async-start | bytes 327680 | tf_op jit(solution)/shard_map/all_to_all | solution.py:106
  147.7 66.7 %reduce-scatter.2.cloned.1.call-start = ((), (), s32[]{:S(2)}) async-start(), calls=%async_computation.5 | async-start | bytes 1474560 | tf_op jit(solution)/shard_map/reduce_scatter | solution.py:127
  158.9 11.6 %copy-start.5 = (f32[640]{0:T(1024)S(1)}, f32[640]{0:T(1024)}, u32[]{:S(2)}) copy-start(f32[640]{0:T(1024)} %copy-done.4) | copy-start | bytes 7684
  161.8 5.8 %collective-permute-start.10 = (bf16[320,2048]{1,0:T(8,128)(2,1)}, bf16[320,2048]{1,0:T(8,128)(2,1)S(1)}, u32[]{:S(2)}, u32[]{:S(2)}) collective-permute-start(bf16[320,2048]{1,0:T(8,128)(2,1)} %convolution_convert_fusion.1), channel_id=1, source_target_pairs={{0,8},{8,0},{1,9},{9,1},{2,10},{10,2},{3,11},{11,3},{4,12},{12,4},... | collective-permute-start | bytes 3932168 | tf_op jit(solution)/shard_map/ppermute | solution.py:125
Sparse Core Ops, SparseCore 0:
  10.2 57.0 all-gather.4
  170.6 32.4 reduce-scatter.1

commit v3 on v1

v3 whole, which is shorter than its diff:
```python
import jax
import jax.numpy as jnp
from jax import lax
from jax.experimental import pallas as pl
from jax.experimental.pallas import tpu as pltpu
from jax.sharding import Mesh, PartitionSpec as P

F32 = jnp.float32
BF16 = jnp.bfloat16
DT = 5120
NX, NZ, NC, NY = 4, 8, 2, 8
epsilon = 1e-06
HEAD_ROWS = 16
ANY = pl.BlockSpec(memory_space=pl.ANY)
VMEM = pl.BlockSpec(memory_space=pltpu.VMEM)
SMEM = pl.BlockSpec(memory_space=pltpu.SMEM)


def split3(values):
    high = values.astype(BF16)
    rest = values - high.astype(F32)
    middle = rest.astype(BF16)
    low = (rest - middle.astype(F32)).astype(BF16)
    return high, middle, low


def normalize(rows, gain):
    values = rows.astype(F32)
    mean_square = jnp.mean(values * values, axis=-1, keepdims=True)
    return (values * lax.rsqrt(mean_square + epsilon) * gain.astype(F32)).astype(BF16)


def shifted(values, axis, size, by):
    return lax.ppermute(values, axis, [(i, (i + by) % size) for i in range(size)])


def against(left, right, dims):
    return lax.dot_general(left, right, (dims, ((), ())), preferred_element_type=F32)


def logits_kernel(offsets, wide, fs, z_ref, rows_ref, *refs):
    blocks, refs = refs[: len(offsets)], refs[len(offsets) :]
    normed_ref, student_ref, teacher_ref, lse_ref, weights_ref = refs[:5]
    rows, squares, weights, row_sems, square_sem, student_sems, teacher_sems = refs[5:]
    z = z_ref[0]
    parts = rows_ref.shape[0]
    student_copies, teacher_copies, row_copies = [], [], []
    for k, (block, offset) in enumerate(zip(blocks, offsets)):
        at = lax.rem(z + offset + NZ, NZ)
        student_copies.append(
            pltpu.make_async_copy(
                block.at[:, pl.ds(0, fs)], weights_ref.at[:, at], student_sems.at[k]
            )
        )
        teacher_copies.append(
            pltpu.make_async_copy(
                block.at[:, pl.ds(fs, weights.shape[2])], weights.at[:, at], teacher_sems.at[k]
            )
        )
    for k in range(parts):
        row_copies.append(
            pltpu.make_async_copy(
                rows_ref.at[k, pl.ds(0, wide)], rows.at[pl.ds(k * wide, wide)], row_sems.at[k]
            )
        )
    square_copy = pltpu.make_async_copy(
        rows_ref.at[:, pl.ds(wide, HEAD_ROWS)], squares, square_sem
    )
    for copy in student_copies + teacher_copies + [square_copy] + row_copies:
        copy.start()

    vocab = weights.shape[3]
    for copy in student_copies:
        copy.wait()
    step = NZ * fs
    total = None
    for k in range(NX):
        part = against(
            weights_ref[k].reshape(step, vocab),
            normed_ref[pl.ds(k * step, step), :],
            ((0,), (0,)),
        )
        total = part if total is None else total + part
    student_ref[...] = total
    top = jnp.max(total, axis=0, keepdims=True)
    student_lse = top + jnp.log(jnp.sum(jnp.exp(total - top), axis=0, keepdims=True))

    for copy in teacher_copies:
        copy.wait()
    step = NZ * weights.shape[2]
    total = None
    for k in range(NX):
        for copy in row_copies[k * parts // NX : (k + 1) * parts // NX]:
            copy.wait()
        part = against(
            weights[k].reshape(step, vocab), rows[pl.ds(k * step, step), :], ((0,), (0,))
        )
        total = part if total is None else total + part
    square_copy.wait()
    square = jnp.sum(jnp.sum(squares[...].astype(F32), axis=0), axis=0, keepdims=True)
    total = total * lax.rsqrt(square / DT + epsilon)
    teacher_ref[...] = total
    top = jnp.max(total, axis=0, keepdims=True)
    teacher_lse = top + jnp.log(jnp.sum(jnp.exp(total - top), axis=0, keepdims=True))
    both = jnp.concatenate([teacher_lse, student_lse], axis=0)
    lse_ref[...] = jnp.broadcast_to(both[None], lse_ref.shape)


def logits(z, rows, blocks, offsets, normed, wide, fs):
    vocab = blocks[0].shape[2]
    ft = blocks[0].shape[1] - fs
    parts, _, tokens = rows.shape
    dma = pltpu.SemaphoreType.DMA
    flops = 2 * vocab * tokens * (parts * wide + normed.shape[0])

    def kernel(*refs):
        logits_kernel(offsets, wide, fs, *refs)

    return pl.pallas_call(
        kernel,
        out_shape=(
            jax.ShapeDtypeStruct((vocab, tokens), F32),
            jax.ShapeDtypeStruct((vocab, tokens), F32),
            jax.ShapeDtypeStruct((NC * NY, 2, tokens), F32),
            jax.ShapeDtypeStruct((NX, NZ, fs, vocab), BF16),
        ),
        in_specs=[SMEM, ANY] + [ANY] * len(blocks) + [VMEM],
        out_specs=(VMEM, VMEM, VMEM, VMEM),
        scratch_shapes=[
            pltpu.VMEM((parts * wide, tokens), BF16),
            pltpu.VMEM((parts, HEAD_ROWS, tokens), BF16),
            pltpu.VMEM((NX, NZ, ft, vocab), BF16),
            dma((parts,)),
            dma(()),
            dma((len(blocks),)),
            dma((len(blocks),)),
        ],
        compiler_params=pltpu.CompilerParams(vmem_limit_bytes=40 << 20),
        cost_estimate=pl.CostEstimate(
            flops=flops, bytes_accessed=20 << 20, transcendentals=2 * vocab * tokens
        ),
    )(z, rows, *blocks, normed)


def grad_kernel(
    which_ref, student_ref, teacher_ref, lse_ref, weights_ref, grad_ref, other_ref, mine_ref, turned
):
    tokens = student_ref.shape[1]
    lses = lse_ref[...]
    top = jnp.max(lses, axis=0)
    lse = top + jnp.log(jnp.sum(jnp.exp(lses - top[None]), axis=0))
    position = lax.broadcasted_iota(jnp.int32, (1, tokens), 1)
    live = (position < which_ref[1]).astype(F32)
    grad = live * (
        jnp.exp(student_ref[...] - lse[1:2]) - jnp.exp(teacher_ref[...] - lse[0:1])
    )
    grad_ref[...] = grad.astype(BF16)
    turned[...] = grad.T.astype(BF16)
    half = tokens // NC
    core = which_ref[0]
    mine = turned[pl.ds(pl.multiple_of(core * half, half), half), :]
    other = turned[pl.ds(pl.multiple_of((1 - core) * half, half), half), :]
    width = weights_ref.shape[0] // NX
    for k in range(NX):
        columns = pl.ds(k * width, width)
        block = weights_ref[columns, :]
        other_ref[:, columns] = against(other, block, ((1,), (1,))).astype(BF16)
        mine_ref[:, columns] = against(mine, block, ((1,), (1,)))


def gradient(which, student, teacher, lse, weights):
    vocab, tokens = student.shape
    features = weights.shape[0]
    half = tokens // NC
    return pl.pallas_call(
        grad_kernel,
        out_shape=(
            jax.ShapeDtypeStruct((vocab, tokens), BF16),
            jax.ShapeDtypeStruct((half, features), BF16),
            jax.ShapeDtypeStruct((half, features), F32),
        ),
        in_specs=[SMEM, VMEM, VMEM, VMEM, VMEM],
        out_specs=(VMEM, VMEM, VMEM),
        scratch_shapes=[pltpu.VMEM((tokens, vocab), BF16)],
        compiler_params=pltpu.CompilerParams(vmem_limit_bytes=40 << 20),
        cost_estimate=pl.CostEstimate(
            flops=2 * vocab * tokens * features,
            bytes_accessed=10 << 20,
            transcendentals=2 * vocab * tokens,
        ),
    )(which, student, teacher, lse, weights)


def body(
    teacher_rows, teacher_gain, teacher_head, student_rows, student_gain, student_head, lengths
):
    fs = student_head.shape[1]
    vocab = teacher_head.shape[0]
    z = lax.axis_index("z")
    c = lax.axis_index("core")

    heads = jnp.concatenate([student_head.T, teacher_head.T], axis=0)
    own = lax.all_gather(heads, "x", axis=0, tiled=False)
    blocks, offsets = [own], [0]
    right = left = own
    for step in range(1, NZ // 2 + 1):
        right = shifted(right, "z", NZ, 1)
        blocks.append(right)
        offsets.append(-step)
        if step < NZ // 2:
            left = shifted(left, "z", NZ, -1)
            blocks.append(left)
            offsets.append(step)

    teacher_rows, _ = lax.optimization_barrier((teacher_rows, own))
    block = teacher_rows.T
    wide = block.shape[0]
    values = block.astype(F32)
    scaled = (values * teacher_gain.astype(F32)[:, None]).astype(BF16)
    squares = jnp.stack(split3(jnp.sum(values * values, axis=0)), axis=0)
    sent = jnp.concatenate([scaled, jnp.pad(squares, ((0, HEAD_ROWS - 3), (0, 0)))], axis=0)
    rows = lax.all_gather(sent, ("core", "y"), axis=0, tiled=False)

    normed = normalize(student_rows, student_gain).T
    student_logits, teacher_logits, lse, student_w = logits(
        z[None], rows, blocks, offsets, normed, wide, fs
    )
    student_w = student_w.reshape(NX * NZ * fs, vocab)

    lse = lax.all_to_all(lse, ("core", "y"), 0, 0, tiled=True)
    which = jnp.stack([c, lengths[0]])
    logit_grad, other, mine = gradient(which, student_logits, teacher_logits, lse, student_w)

    other = lax.ppermute(other, "core", [(0, 1), (1, 0)])
    mine = (mine + other.astype(F32)).astype(BF16)
    row_grad = lax.psum_scatter(mine, "y", scatter_dimension=0, tiled=True).astype(F32)

    head_part = against(normed, logit_grad, ((1,), (1,))).astype(BF16)
    head_part = lax.all_to_all(head_part.reshape(NX, NZ * fs, vocab), "x", 0, 0, tiled=True)
    head_part = jnp.sum(head_part.astype(F32), axis=0).astype(BF16)
    head_part = lax.all_to_all(head_part.reshape(NZ, fs, vocab), "z", 0, 0, tiled=True)
    head_grad = jnp.sum(head_part.astype(F32), axis=0)

    devices = NX * NZ * NC * NY
    squares = jnp.stack([jnp.sum(head_grad * head_grad), jnp.sum(row_grad * row_grad)])
    squares = jnp.broadcast_to(squares[None, :, None], (devices, 2, 64)).reshape(devices, 128)
    squares = lax.all_to_all(squares, ("x", "z", "core", "y"), 0, 0, tiled=True)
    squares = jnp.sum(squares, axis=0)
    head_update = head_grad * lax.rsqrt(squares[0] / (head_grad.size * devices) + epsilon)
    row_update = row_grad * lax.rsqrt(squares[64] / (row_grad.size * devices) + epsilon)
    return (head_update.astype(BF16).T, row_update.astype(BF16))


def solution(mesh):
    mesh = Mesh(mesh.devices.reshape(NX, NZ, NC, NY), ("x", "z", "core", "y"))
    dp, mp = ("x", "z"), ("core", "y")
    placed = (P(dp, mp), P(mp), P(mp, dp), P(dp, None), P(), P(mp, dp), P(dp))
    return jax.shard_map(
        body,
        mesh=mesh,
        in_specs=placed,
        out_specs=(P(mp, dp), P(dp + mp, None)),
        check_vma=False,
    )
```

time: 232 us -> 233 us (level)
  Pallas kernels: 0 us -> 12.4 us
  matrix products: 12.4 us -> 1.72 us
  local copies, waits for them, and re-layouts: 12.1 us -> 17.1 us
  other arithmetic: 19.7 us -> 16.3 us
  waiting for transfers between devices: 47.2 us -> 44.8 us
    unnamed x16 -> x29, local copies, waits for them, and re-layouts: 2.34 us -> 16.2 us
    pallas_call x0 -> x2, Pallas kernels: none -> 12.4 us  [the longest x1 9.91 us: logits(): pl.pallas_call(kernel, out_shape=(jax.ShapeDtypeStruct((vocab, tokens), F...]
    dot_general x4 -> x1, matrix products: 12.4 us -> 1.72 us  [against(): lax.dot_general(left, right, (dims, ((), ())), preferred_element_type=F32)]
    dynamic_update_slice x17 -> x0, local copies, waits for them, and re-layouts: 6.18 us -> none  [the longest x9 4.95 us: place(): t = lax.dynamic_update_slice(t, part[:, None, fs:], (0, at, 0, 0))]
    convert_element_type x3 -> x1, other arithmetic: 3.91 us -> 1.47 us  [body(): mine = (mine + other.astype(F32)).astype(BF16)]
    transpose x0 -> x1, other arithmetic: none -> 2.41 us  [body(): normed = normalize(student_rows, student_gain).T]
    reduce_sum x4 -> x0, other arithmetic: 2.4 us -> none  [the longest x1 1.09 us: body(): jnp.sum(stats[:, 2:] * jnp.exp(stats[:, :2] - top), axis=0)]
  transfers between devices with their start and end apart: 11 -> 11, of which waited for: 6 -> 7; matrix products, arithmetic and copies ran while one was open for 6% -> 5% of each run, Pallas kernels for 0% -> 0%
where the time goes in v3:
time: 233 us; the launch traced here: 232 us
  blocking collectives  78.1 us (34%)
  starting transfers between devices  44.9 us (19%)
  waiting for transfers between devices  44.8 us (19%)
  local copies, waits for them, and re-layouts  17.1 us (7%)
  other arithmetic  16.3 us (7%)
  between operations  16.3 us (7%)
  Pallas kernels  12.4 us (5%)
    ppermute x7, waiting for transfers between devices, shifted(): lax.ppermute(values, axis, [(i, (i + by) % size) for i in range(size)])  35.8 us
    ppermute x7, starting transfers between devices, shifted(): lax.ppermute(values, axis, [(i, (i + by) % size) for i in range(size)])  28.8 us
    all_to_all x1, blocking collectives, body(): squares = lax.all_to_all(squares, ('x', 'z', 'core', 'y'), 0, 0, tiled=True)  28.7 us
    all_to_all x1, blocking collectives, body(): lax.all_to_all(head_part.reshape(NX, NZ * fs, vocab), 'x', 0, 0, tiled=True)  22.8 us
    unnamed x29, local copies, waits for them, and re-layouts  16.2 us
    all_to_all x1, blocking collectives, body(): lax.all_to_all(head_part.reshape(NZ, fs, vocab), 'z', 0, 0, tiled=True)  15.3 us
    all_to_all x1, starting transfers between devices, body(): lse = lax.all_to_all(lse, ('core', 'y'), 0, 0, tiled=True)  13 us
    all_gather x1, blocking collectives, body(): own = lax.all_gather(heads, 'x', axis=0, tiled=False)  11.4 us
  transfers between devices with their start and end apart: 11, of which 7 were waited for; matrix products, arithmetic and copies ran while one was open for 5% of the time, Pallas kernels for 0%

profile of v3, /device:TPU:1, one launch (start us, length us, event | category | flops | bytes accessed | tf_op | source)
XLA Modules:
  0.0 231.6 jit_solution(17211517656602240778)
XLA Ops:
  7.2 0.0 all-gather.4.cloned.1.call-start
  7.2 0.7 convert_element_type.121
  7.9 0.9 pad_maximum_fusion.1
  8.8 11.4 %all-gather = bf16[896,384]{1,0:T(8,128)(2,1)S(1)} all-gather(bf16[224,384]{1,0:T(8,128)(2,1)S(1)} %pad_maximum_fusion.1), channel_id=2, replica_groups=mesh['x'=4,'z'=8,'core'=2,'y'=8] {'x'}, dimensions={0}, use_global_device_ids=true | all-gather | bytes 860160 | tf_op jit(solution)/shard_map/all_gather | solution.py:203
  20.2 1.1 fusion.7
  21.4 0.8 pad_maximum_fusion
  22.2 0.0 all-gather.4.cloned.1.call-update
  22.2 5.3 %collective-permute-start = (bf16[4,224,384]{2,1,0:T(8,128)(2,1)S(1)}, bf16[4,224,384]{2,1,0:T(8,128)(2,1)S(1)}, u32[]{:S(2)}, u32[]{:S(2)}) collective-permute-start(bf16[4,224,384]{2,1,0:T(8,128)(2,1)S(1)} %bitcast.21), channel_id=1, source_target_pairs={{0,16},{16,32},{32,48},{48,64},{64,80},{80,96},{96,112},{112,0},{1... | collective-permute-start | bytes 2064392 | tf_op jit(solution)/shard_map/ppermute | solution.py:34
  27.6 8.6 %collective-permute-start.1 = (bf16[4,224,384]{2,1,0:T(8,128)(2,1)S(1)}, bf16[4,224,384]{2,1,0:T(8,128)(2,1)S(1)}, u32[]{:S(2)}, u32[]{:S(2)}) collective-permute-start(bf16[4,224,384]{2,1,0:T(8,128)(2,1)S(1)} %bitcast.22), channel_id=1, source_target_pairs={{0,112},{16,0},{32,16},{48,32},{64,48},{80,64},{96,80},{112,96},{1... | collective-permute-start | bytes 2064392 | tf_op jit(solution)/shard_map/ppermute | solution.py:34
  36.1 11.5 %collective-permute-done.refs_3_ = bf16[4,224,384]{2,1,0:T(8,128)(2,1)S(1)} collective-permute-done((bf16[4,224,384]{2,1,0:T(8,128)(2,1)S(1)}, bf16[4,224,384]{2,1,0:T(8,128)(2,1)S(1)}, u32[]{:S(2)}, u32[]{:S(2)}) %collective-permute-start) | collective-permute-done | bytes 688160 | tf_op jit(solution)/shard_map/ppermute | solution.py:34
  47.7 1.9 collective-permute-start.2
  49.6 0.0 copy-start
  49.6 0.8 copy-done
  50.5 0.0 collective-permute-done.1.refs_4_
  50.5 4.6 %collective-permute-start.3 = (bf16[4,224,384]{2,1,0:T(8,128)(2,1)S(1)}, bf16[4,224,384]{2,1,0:T(8,128)(2,1)}, u32[]{:S(2)}, u32[]{:S(2)}) collective-permute-start(bf16[4,224,384]{2,1,0:T(8,128)(2,1)S(1)} %collective-permute-done.1.refs_4_), channel_id=1, source_target_pairs={{0,112},{16,0},{32,16},{48,32},{64,48},{80,64},{96,80},{112,96},{1... | collective-permute-start | bytes 2064392 | tf_op jit(solution)/shard_map/ppermute | solution.py:34
  55.0 9.9 %collective-permute-done.2.refs_5_ = bf16[4,224,384]{2,1,0:T(8,128)(2,1)S(1)} collective-permute-done((bf16[4,224,384]{2,1,0:T(8,128)(2,1)S(1)}, bf16[4,224,384]{2,1,0:T(8,128)(2,1)S(1)}, u32[]{:S(2)}, u32[]{:S(2)}) %collective-permute-start.2) | collective-permute-done | bytes 688160 | tf_op jit(solution)/shard_map/ppermute | solution.py:34
  64.9 1.9 collective-permute-start.4
  66.8 4.4 %copy.11 = bf16[640,2048]{0,1:T(8,128)(2,1)} copy(bf16[640,2048]{1,0:T(8,128)(2,1)} %param.10) | data formatting | bytes 5242880 | tf_op args[3]
  71.3 2.4 %fusion = f32[640]{0:T(1024)S(1)} fusion(bf16[640,2048]{0,1:T(8,128)(2,1)} %copy.11), kind=kLoop, calls=%fused_computation.2 | loop fusion | flops 3931520 | bytes 2624000 | tf_op jit(solution)/shard_map/reduce_sum | solution.py:29
  73.7 0.0 copy-done.4
  73.7 0.0 collective-permute-done.3.refs_6_
  73.7 4.6 %collective-permute-start.5 = (bf16[4,224,384]{2,1,0:T(8,128)(2,1)}, bf16[4,224,384]{2,1,0:T(8,128)(2,1)}, u32[]{:S(2)}, u32[]{:S(2)}) collective-permute-start(bf16[4,224,384]{2,1,0:T(8,128)(2,1)} %collective-permute-done.3.refs_6_), channel_id=1, source_target_pairs={{0,112},{16,0},{32,16},{48,32},{64,48},{80,64},{96,80},{112,96},{1... | collective-permute-start | bytes 2064392 | tf_op jit(solution)/shard_map/ppermute | solution.py:34
  78.3 3.1 %collective-permute-done.4.refs_7_ = bf16[4,224,384]{2,1,0:T(8,128)(2,1)} collective-permute-done((bf16[4,224,384]{2,1,0:T(8,128)(2,1)S(1)}, bf16[4,224,384]{2,1,0:T(8,128)(2,1)}, u32[]{:S(2)}, u32[]{:S(2)}) %collective-permute-start.4) | collective-permute-done | bytes 688160 | tf_op jit(solution)/shard_map/ppermute | solution.py:34
  81.3 1.9 collective-permute-start.6
  83.3 2.4 %fusion.6.refs_10_ = bf16[2048,640]{1,0:T(8,128)(2,1)S(1)} fusion(f32[2048]{0:T(1024)S(1)} %convert_element_type.118, f32[640]{0:T(1024)S(1)} %add_rsqrt_fusion, bf16[640,2048]{0,1:T(8,128)(2,1)} %copy.11), kind=kLoop, calls=%fused_computation.12 | loop fusion | flops 5242880 | bytes 5253632 | tf_op jit(solution)/shard_map/transpose | solution.py:224
  85.7 3.6 %collective-permute-done.5.refs_8_ = bf16[4,224,384]{2,1,0:T(8,128)(2,1)} collective-permute-done((bf16[4,224,384]{2,1,0:T(8,128)(2,1)}, bf16[4,224,384]{2,1,0:T(8,128)(2,1)}, u32[]{:S(2)}, u32[]{:S(2)}) %collective-permute-start.5) | collective-permute-done | bytes 688160 | tf_op jit(solution)/shard_map/ppermute | solution.py:34
  89.3 7.7 %collective-permute-done.6.refs_9_ = bf16[4,224,384]{2,1,0:T(8,128)(2,1)} collective-permute-done((bf16[4,224,384]{2,1,0:T(8,128)(2,1)}, bf16[4,224,384]{2,1,0:T(8,128)(2,1)}, u32[]{:S(2)}, u32[]{:S(2)}) %collective-permute-start.6) | collective-permute-done | bytes 688160 | tf_op jit(solution)/shard_map/ppermute | solution.py:34
  97.0 1.1 copy-done.1
  98.1 1.1 copy-done.3
  99.2 1.1 copy-done.5
  100.3 9.9 %shard_map.86 = (f32[384,640]{1,0:T(8,128)S(1)}, f32[384,640]{1,0:T(8,128)S(1)}, f32[16,2,640]{2,1,0:T(2,128)}, bf16[4,8,64,384]{3,2,1,0:T(8,128)(2,1)S(1)}) custom-call(s32[1]{0:T(128)} %bitcast.1.refs_0_, bf16[16,336,640]{2,1,0:T(8,128)(2,1)} %bitcast.25, bf16[4,224,384]{2,1,0:T(8,128)(2,1)S(1)} %bitcast.23, bf16[4,224,384]{2,1,0:T(8,128)(2,1)S(1)} %copy-done.1, ...), custom_call_target="tpu_custom_call" | custom-call | flops 3523215360 | bytes 20971520 | tf_op jit(solution)/shard_map/pallas_call | solution.py:119
  110.2 0.0 copy-start.6
  110.3 1.1 copy-done.6
  111.4 1.0 copy-done.8
  112.4 1.0 copy-done.10
  113.3 13.0 %all-to-all-start = ((f32[16,2,640]{2,1,0:T(2,128)}), f32[16,2,640]{2,1,0:T(2,128)S(1)}, u32[]{:S(2)}, u32[]{:S(2)}) async-start(f32[16,2,640]{2,1,0:T(2,128)} %get-tuple-element.13), calls=%async_computation | async-start | bytes 163840 | tf_op jit(solution)/shard_map/all_to_all | solution.py:230
  126.3 0.0 reduce-scatter.2.cloned.1.call-start
  127.0 0.1 pad_add_fusion.which_ref
  127.1 6.5 %all-to-all-done.lse_ref = f32[16,2,640]{2,1,0:T(2,128)S(1)} async-done(((f32[16,2,640]{2,1,0:T(2,128)}), f32[16,2,640]{2,1,0:T(2,128)S(1)}, u32[]{:S(2)}, u32[]{:S(2)}) %all-to-all-start) | async-done | bytes 81952 | tf_op jit(solution)/shard_map/all_to_all | solution.py:230
  133.6 1.4 copy-done.7
  135.0 1.2 copy-done.9
  136.2 1.2 copy-done.11
  137.4 2.5 %shard_map.87 = (bf16[384,640]{1,0:T(8,128)(2,1)S(1)}, bf16[320,2048]{1,0:T(8,128)(2,1)S(1)}, f32[320,2048]{1,0:T(8,128)S(1)}) custom-call(s32[2]{0:T(128)S(1)} %pad_add_fusion.which_ref, f32[384,640]{1,0:T(8,128)S(1)} %copy-done.9, f32[384,640]{1,0:T(8,128)S(1)} %copy-done.11, f32[16,2,640]{2,1,0:T(2,128)S(1)} %all-to-all-done.lse_ref, ...), custom_call_target="tpu_custom_call" | custom-call | flops 1006632960 | bytes 10485760 | tf_op jit(solution)/shard_map/pallas_call | solution.py:175
  139.9 3.1 %collective-permute-start.7 = (bf16[320,2048]{1,0:T(8,128)(2,1)S(1)}, bf16[320,2048]{1,0:T(8,128)(2,1)S(1)}, u32[]{:S(2)}, u32[]{:S(2)}) collective-permute-start(bf16[320,2048]{1,0:T(8,128)(2,1)S(1)} %get-tuple-element.17), channel_id=1, source_target_pairs={{0,8},{8,0},{1,9},{9,1},{2,10},{10,2},{3,11},{11,3},{4,12},{12,4},... | collective-permute-start | bytes 3932168 | tf_op jit(solution)/shard_map/ppermute | solution.py:234
  143.0 2.5 %collective-permute-done.7 = bf16[320,2048]{1,0:T(8,128)(2,1)S(1)} collective-permute-done((bf16[320,2048]{1,0:T(8,128)(2,1)S(1)}, bf16[320,2048]{1,0:T(8,128)(2,1)S(1)}, u32[]{:S(2)}, u32[]{:S(2)}) %collective-permute-start.7) | collective-permute-done | bytes 1310752 | tf_op jit(solution)/shard_map/ppermute | solution.py:234
  145.5 1.5 add_convert_fusion
  146.9 0.0 reduce-scatter.2.cloned.1.call-update
  147.0 0.7 copy-done.12
  147.7 1.7 convolution_convert_fusion
  149.4 22.8 %all_to_all.21 = bf16[4,512,384]{2,1,0:T(8,128)(2,1)S(1)} all-to-all(bf16[4,512,384]{2,1,0:T(8,128)(2,1)S(1)} %bitcast.26), channel_id=1, replica_groups=mesh['x'=4,'z'=8,'core'=2,'y'=8] {'x'}, dimensions={0} | all-to-all | bytes 3145728 | tf_op jit(solution)/shard_map/all_to_all | solution.py:239
  172.2 0.4 reduce_sum.71
  172.6 15.3 %all_to_all.22 = bf16[8,64,384]{2,1,0:T(8,128)(2,1)S(1)} all-to-all(bf16[8,64,384]{2,1,0:T(8,128)(2,1)S(1)} %bitcast.27), channel_id=1, replica_groups=mesh['x'=4,'z'=8,'core'=2,'y'=8] {'z'}, dimensions={0} | all-to-all | bytes 786432 | tf_op jit(solution)/shard_map/all_to_all | solution.py:241
  187.9 0.1 convert_reduce_fusion
  188.0 0.6 multiply_reduce_fusion
  188.6 1.6 fusion.8
  190.2 1.4 pad_maximum_fusion.2
  191.6 0.1 broadcast_in_dim.17
  191.6 0.1 broadcast_in_dim.18
  191.7 0.1 broadcast_in_dim.19
  191.9 28.7 %all_to_all.23 = f32[512,1,128]{2,1,0:T(1,128)S(1)} all-to-all(f32[512,1,128]{2,1,0:T(1,128)S(1)} %broadcast_in_dim.19), channel_id=1, replica_groups=mesh['x'=4,'z'=8,'core'=2,'y'=8] {'x','z','core','y'}, dimensions={0} | all-to-all | bytes 524288 | tf_op jit(solution)/shard_map/all_to_all | solution.py:247
  220.5 0.1 reduce_sum.75
  220.6 0.6 fusion.17
  222.6 0.6 fusion.10
  223.2 1.6 fusion.9
  (21 shorter events, 0.1 us)
Async XLA Ops:
  7.2 89.9 %all-gather.4.cloned.1.call-start = ((), (), s32[]{:S(2)}) async-start(), calls=%async_computation.6 | async-start | bytes 7311360 | tf_op jit(solution)/shard_map/all_gather | solution.py:222
  22.2 25.5 %collective-permute-start = (bf16[4,224,384]{2,1,0:T(8,128)(2,1)S(1)}, bf16[4,224,384]{2,1,0:T(8,128)(2,1)S(1)}, u32[]{:S(2)}, u32[]{:S(2)}) collective-permute-start(bf16[4,224,384]{2,1,0:T(8,128)(2,1)S(1)} %bitcast.21), channel_id=1, source_target_pairs={{0,16},{16,32},{32,48},{48,64},{64,80},{80,96},{96,112},{112,0},{1... | collective-permute-start | bytes 2064392 | tf_op jit(solution)/shard_map/ppermute | solution.py:34
  27.6 22.9 %collective-permute-start.1 = (bf16[4,224,384]{2,1,0:T(8,128)(2,1)S(1)}, bf16[4,224,384]{2,1,0:T(8,128)(2,1)S(1)}, u32[]{:S(2)}, u32[]{:S(2)}) collective-permute-start(bf16[4,224,384]{2,1,0:T(8,128)(2,1)S(1)} %bitcast.22), channel_id=1, source_target_pairs={{0,112},{16,0},{32,16},{48,32},{64,48},{80,64},{96,80},{112,96},{1... | collective-permute-start | bytes 2064392 | tf_op jit(solution)/shard_map/ppermute | solution.py:34
  47.7 17.2 %collective-permute-start.2 = (bf16[4,224,384]{2,1,0:T(8,128)(2,1)S(1)}, bf16[4,224,384]{2,1,0:T(8,128)(2,1)S(1)}, u32[]{:S(2)}, u32[]{:S(2)}) collective-permute-start(bf16[4,224,384]{2,1,0:T(8,128)(2,1)S(1)} %collective-permute-done.refs_3_), channel_id=1, source_target_pairs={{0,16},{16,32},{32,48},{48,64},{64,80},{80,96},{96,112},{112,0},{1... | collective-permute-start | bytes 2064392 | tf_op jit(solution)/shard_map/ppermute | solution.py:34
  49.6 0.9 copy-start
  50.5 23.2 %copy-start.2 = (bf16[4,224,384]{2,1,0:T(8,128)(2,1)}, bf16[4,224,384]{2,1,0:T(8,128)(2,1)S(1)}, u32[]{:S(2)}) copy-start(bf16[4,224,384]{2,1,0:T(8,128)(2,1)S(1)} %collective-permute-done.1.refs_4_) | copy-start | bytes 2064388
  50.5 23.2 %collective-permute-start.3 = (bf16[4,224,384]{2,1,0:T(8,128)(2,1)S(1)}, bf16[4,224,384]{2,1,0:T(8,128)(2,1)}, u32[]{:S(2)}, u32[]{:S(2)}) collective-permute-start(bf16[4,224,384]{2,1,0:T(8,128)(2,1)S(1)} %collective-permute-done.1.refs_4_), channel_id=1, source_target_pairs={{0,112},{16,0},{32,16},{48,32},{64,48},{80,64},{96,80},{112,96},{1... | collective-permute-start | bytes 2064392 | tf_op jit(solution)/shard_map/ppermute | solution.py:34
  64.9 8.7 %copy-start.4 = (bf16[4,224,384]{2,1,0:T(8,128)(2,1)}, bf16[4,224,384]{2,1,0:T(8,128)(2,1)S(1)}, u32[]{:S(2)}) copy-start(bf16[4,224,384]{2,1,0:T(8,128)(2,1)S(1)} %collective-permute-done.2.refs_5_) | copy-start | bytes 2064388
  64.9 16.4 %collective-permute-start.4 = (bf16[4,224,384]{2,1,0:T(8,128)(2,1)S(1)}, bf16[4,224,384]{2,1,0:T(8,128)(2,1)}, u32[]{:S(2)}, u32[]{:S(2)}) collective-permute-start(bf16[4,224,384]{2,1,0:T(8,128)(2,1)S(1)} %collective-permute-done.2.refs_5_), channel_id=1, source_target_pairs={{0,16},{16,32},{32,48},{48,64},{64,80},{80,96},{96,112},{112,0},{1... | collective-permute-start | bytes 2064392 | tf_op jit(solution)/shard_map/ppermute | solution.py:34
  71.3 12.0 %copy-start.13 = (bf16[2048]{0:T(1024)(128)(2,1)S(1)}, bf16[2048]{0:T(1024)(128)(2,1)}, u32[]{:S(2)}) copy-start(bf16[2048]{0:T(1024)(128)(2,1)} %param.11) | copy-start | bytes 12292
  73.7 15.6 %collective-permute-start.5 = (bf16[4,224,384]{2,1,0:T(8,128)(2,1)}, bf16[4,224,384]{2,1,0:T(8,128)(2,1)}, u32[]{:S(2)}, u32[]{:S(2)}) collective-permute-start(bf16[4,224,384]{2,1,0:T(8,128)(2,1)} %collective-permute-done.3.refs_6_), channel_id=1, source_target_pairs={{0,112},{16,0},{32,16},{48,32},{64,48},{80,64},{96,80},{112,96},{1... | collective-permute-start | bytes 2064392 | tf_op jit(solution)/shard_map/ppermute | solution.py:34
  81.3 15.7 %collective-permute-start.6 = (bf16[4,224,384]{2,1,0:T(8,128)(2,1)}, bf16[4,224,384]{2,1,0:T(8,128)(2,1)}, u32[]{:S(2)}, u32[]{:S(2)}) collective-permute-start(bf16[4,224,384]{2,1,0:T(8,128)(2,1)} %collective-permute-done.4.refs_7_), channel_id=1, source_target_pairs={{0,16},{16,32},{32,48},{48,64},{64,80},{80,96},{96,112},{112,0},{1... | collective-permute-start | bytes 2064392 | tf_op jit(solution)/shard_map/ppermute | solution.py:34
  97.0 1.1 copy-start.1
  98.1 1.1 copy-start.3
  99.2 1.1 copy-start.5
  110.2 1.2 copy-start.6
  111.4 1.0 copy-start.8
  112.4 1.0 copy-start.10
  113.3 20.3 %all-to-all-start = ((f32[16,2,640]{2,1,0:T(2,128)}), f32[16,2,640]{2,1,0:T(2,128)S(1)}, u32[]{:S(2)}, u32[]{:S(2)}) async-start(f32[16,2,640]{2,1,0:T(2,128)} %get-tuple-element.13), calls=%async_computation | async-start | bytes 163840 | tf_op jit(solution)/shard_map/all_to_all | solution.py:230
  126.3 62.3 %reduce-scatter.2.cloned.1.call-start = ((), (), s32[]{:S(2)}) async-start(), calls=%async_computation.5 | async-start | bytes 1474560 | tf_op jit(solution)/shard_map/reduce_scatter | solution.py:236
  133.6 1.4 copy-start.7
  135.0 1.2 copy-start.9
  136.2 1.2 copy-start.11
  139.9 5.5 %collective-permute-start.7 = (bf16[320,2048]{1,0:T(8,128)(2,1)S(1)}, bf16[320,2048]{1,0:T(8,128)(2,1)S(1)}, u32[]{:S(2)}, u32[]{:S(2)}) collective-permute-start(bf16[320,2048]{1,0:T(8,128)(2,1)S(1)} %get-tuple-element.17), channel_id=1, source_target_pairs={{0,8},{8,0},{1,9},{9,1},{2,10},{10,2},{3,11},{11,3},{4,12},{12,4},... | collective-permute-start | bytes 3932168 | tf_op jit(solution)/shard_map/ppermute | solution.py:234
  145.5 2.2 copy-start.12
Sparse Core Ops, SparseCore 0:
  22.4 59.1 all-gather.3
  147.1 28.7 reduce-scatter.1

commit v4 on v3

v4 whole, which is shorter than its diff:
```python
import jax
import jax.numpy as jnp
from jax import lax
from jax.experimental import pallas as pl
from jax.experimental.pallas import tpu as pltpu
from jax.sharding import Mesh, PartitionSpec as P

F32 = jnp.float32
BF16 = jnp.bfloat16
DT = 5120
NX, NZ, NC, NY = 4, 8, 2, 8
epsilon = 1e-06
HEAD_ROWS = 16
HBM = pl.BlockSpec(memory_space=pltpu.HBM)
VMEM = pl.BlockSpec(memory_space=pltpu.VMEM)
SMEM = pl.BlockSpec(memory_space=pltpu.SMEM)


def split3(values):
    high = values.astype(BF16)
    rest = values - high.astype(F32)
    middle = rest.astype(BF16)
    low = (rest - middle.astype(F32)).astype(BF16)
    return high, middle, low


def normalize(rows, gain):
    values = rows.astype(F32)
    mean_square = jnp.mean(values * values, axis=-1, keepdims=True)
    return (values * lax.rsqrt(mean_square + epsilon) * gain.astype(F32)).astype(BF16)


def shifted(values, axis, size, by):
    return lax.ppermute(values, axis, [(i, (i + by) % size) for i in range(size)])


def against(left, right, dims):
    return lax.dot_general(left, right, (dims, ((), ())), preferred_element_type=F32)


def log_sum_exp(values):
    top = jnp.max(values, axis=0, keepdims=True)
    return top + jnp.log(jnp.sum(jnp.exp(values - top), axis=0, keepdims=True))


def begin(copies):
    for copy in copies:
        copy.start()
    return copies


def finish(copies):
    for copy in copies:
        copy.wait()


def most_kernel(offsets, missing, wide, fs, z_ref, rows_ref, normed_ref, *refs):
    blocks, refs = refs[: len(offsets)], refs[len(offsets) :]
    student_ref, teacher_ref, scale_ref, weights_ref, last_rows, last_normed = refs[:6]
    rows, squares, student_w, teacher_w, normed = refs[6:11]
    row_sems, square_sem, student_sems, teacher_sems, normed_sem, weights_sem, last_sems = refs[11:]
    z = z_ref[0]
    parts = rows_ref.shape[0]
    ft, vocab = teacher_w.shape[2:]
    places = [lax.rem(z + offset + NZ, NZ) for offset in offsets]
    student_copies = [
        pltpu.make_async_copy(
            block.at[:, pl.ds(0, fs)], student_w.at[:, at], student_sems.at[k]
        )
        for k, (block, at) in enumerate(zip(blocks, places))
    ]
    normed_copy = pltpu.make_async_copy(normed_ref, normed, normed_sem)
    teacher_copies = [
        pltpu.make_async_copy(
            block.at[:, pl.ds(fs, ft)], teacher_w.at[:, at], teacher_sems.at[k]
        )
        for k, (block, at) in enumerate(zip(blocks, places))
    ]
    square_copy = pltpu.make_async_copy(
        rows_ref.at[:, pl.ds(wide, HEAD_ROWS)], squares, square_sem
    )
    row_copies = [
        pltpu.make_async_copy(
            rows_ref.at[k, pl.ds(0, wide)], rows.at[pl.ds(k * wide, wide)], row_sems.at[k]
        )
        for k in range(parts)
    ]
    at = lax.rem(z + missing + NZ, NZ)
    per_block = parts // NX
    fold = NZ // per_block
    inner = pl.multiple_of(lax.rem(at, fold) * ft, 16)
    last_copies = []
    for k in range(NX):
        source = pl.multiple_of(k * NZ * fs + at * fs, 16)
        last_copies.append(
            pltpu.make_async_copy(
                normed_ref.at[pl.ds(source, fs)],
                last_normed.at[pl.ds(k * fs, fs)],
                last_sems.at[k],
            )
        )
        last_copies.append(
            pltpu.make_async_copy(
                rows_ref.at[k * per_block + lax.div(at, fold), pl.ds(inner, ft)],
                last_rows.at[pl.ds(k * ft, ft)],
                last_sems.at[NX + k],
            )
        )
    begin(student_copies + [normed_copy] + teacher_copies + [square_copy] + row_copies)
    begin(last_copies)
    student_w[:, at] = jnp.zeros((NX, fs, vocab), BF16)
    teacher_w[:, at] = jnp.zeros((NX, ft, vocab), BF16)

    finish(student_copies + [normed_copy])
    weights_copy = pltpu.make_async_copy(student_w, weights_ref, weights_sem)
    weights_copy.start()
    step = NZ * fs
    total = None
    for k in range(NX):
        part = against(
            student_w[k].reshape(step, vocab), normed[pl.ds(k * step, step), :], ((0,), (0,))
        )
        total = part if total is None else total + part
    student_ref[...] = total

    finish(teacher_copies)
    step = NZ * ft
    total = None
    for k in range(NX):
        finish(row_copies[k * parts // NX : (k + 1) * parts // NX])
        part = against(
            teacher_w[k].reshape(step, vocab), rows[pl.ds(k * step, step), :], ((0,), (0,))
        )
        total = part if total is None else total + part
    teacher_ref[...] = total
    square_copy.wait()
    square = jnp.sum(jnp.sum(squares[...].astype(F32), axis=0), axis=0, keepdims=True)
    scale_ref[...] = lax.rsqrt(square / DT + epsilon)
    finish(last_copies + [weights_copy])


def most(z, rows, normed, blocks, offsets, missing, wide, fs):
    vocab = blocks[0].shape[2]
    ft = blocks[0].shape[1] - fs
    parts, _, tokens = rows.shape
    dma = pltpu.SemaphoreType.DMA

    def kernel(*refs):
        most_kernel(offsets, missing, wide, fs, *refs)

    return pl.pallas_call(
        kernel,
        out_shape=(
            jax.ShapeDtypeStruct((vocab, tokens), F32),
            jax.ShapeDtypeStruct((vocab, tokens), F32),
            jax.ShapeDtypeStruct((1, tokens), F32),
            jax.ShapeDtypeStruct((NX, NZ, fs, vocab), BF16),
            jax.ShapeDtypeStruct((NX * ft, tokens), BF16),
            jax.ShapeDtypeStruct((NX * fs, tokens), BF16),
        ),
        in_specs=[SMEM, HBM, HBM] + [HBM] * len(blocks),
        out_specs=(VMEM, VMEM, VMEM, HBM, VMEM, VMEM),
        scratch_shapes=[
            pltpu.VMEM((parts * wide, tokens), BF16),
            pltpu.VMEM((parts, HEAD_ROWS, tokens), BF16),
            pltpu.VMEM((NX, NZ, fs, vocab), BF16),
            pltpu.VMEM((NX, NZ, ft, vocab), BF16),
            pltpu.VMEM(normed.shape, BF16),
            dma((parts,)),
            dma(()),
            dma((len(blocks),)),
            dma((len(blocks),)),
            dma(()),
            dma(()),
            dma((2 * NX,)),
        ],
        compiler_params=pltpu.CompilerParams(vmem_limit_bytes=32 << 20),
        cost_estimate=pl.CostEstimate(
            flops=2 * vocab * tokens * (parts * wide + normed.shape[0]),
            bytes_accessed=20 << 20,
            transcendentals=0,
        ),
    )(z, rows, normed, *blocks)


def last_kernel(missing, fs, z_ref, rows_ref, normed_ref, block_ref, *refs):
    student_part, teacher_part, scale_ref, _, student_ref, teacher_ref, lse_ref, weights_ref = refs[:8]
    student_w, teacher_w, sems = refs[8:]
    ft, vocab = teacher_w.shape[1:]
    at = lax.rem(z_ref[0] + missing + NZ, NZ)
    copies = begin(
        [
            pltpu.make_async_copy(block_ref.at[:, pl.ds(0, fs)], student_w, sems.at[0]),
            pltpu.make_async_copy(block_ref.at[:, pl.ds(fs, ft)], teacher_w, sems.at[1]),
        ]
    )
    copies[0].wait()
    weights_copy = pltpu.make_async_copy(student_w, weights_ref.at[:, at], sems.at[2])
    weights_copy.start()
    total = student_part[...] + against(
        student_w[...].reshape(NX * fs, vocab), normed_ref[...], ((0,), (0,))
    )
    student_ref[...] = total
    student_lse = log_sum_exp(total)
    copies[1].wait()
    total = scale_ref[...] * (
        teacher_part[...]
        + against(teacher_w[...].reshape(NX * ft, vocab), rows_ref[...], ((0,), (0,)))
    )
    teacher_ref[...] = total
    both = jnp.concatenate([log_sum_exp(total), student_lse], axis=0)
    lse_ref[...] = jnp.broadcast_to(both[None], lse_ref.shape)
    weights_copy.wait()


def last(z, rows, normed, block, student, teacher, scale, weights, missing, fs):
    vocab, tokens = student.shape
    ft = block.shape[1] - fs

    def kernel(*refs):
        last_kernel(missing, fs, *refs)

    return pl.pallas_call(
        kernel,
        out_shape=(
            jax.ShapeDtypeStruct((vocab, tokens), F32),
            jax.ShapeDtypeStruct((vocab, tokens), F32),
            jax.ShapeDtypeStruct((NC * NY, 2, tokens), F32),
            jax.ShapeDtypeStruct(weights.shape, BF16),
        ),
        in_specs=[SMEM, VMEM, VMEM, HBM, VMEM, VMEM, VMEM, HBM],
        out_specs=(VMEM, VMEM, VMEM, HBM),
        input_output_aliases={7: 3},
        scratch_shapes=[
            pltpu.VMEM((NX, fs, vocab), BF16),
            pltpu.VMEM((NX, ft, vocab), BF16),
            pltpu.SemaphoreType.DMA((3,)),
        ],
        compiler_params=pltpu.CompilerParams(vmem_limit_bytes=24 << 20),
        cost_estimate=pl.CostEstimate(
            flops=2 * vocab * tokens * NX * (ft + fs),
            bytes_accessed=8 << 20,
            transcendentals=2 * vocab * tokens,
        ),
    )(z, rows, normed, block, student, teacher, scale, weights)


def grad_kernel(which_ref, student, teacher, lse_ref, weights, *refs):
    grad_ref, other_ref, mine_ref, turned = refs
    tokens = student.shape[1]
    lses = lse_ref[...]
    top = jnp.max(lses, axis=0)
    lse = top + jnp.log(jnp.sum(jnp.exp(lses - top[None]), axis=0))
    position = lax.broadcasted_iota(jnp.int32, (1, tokens), 1)
    live = (position < which_ref[1]).astype(F32)
    grad = live * (jnp.exp(student[...] - lse[1:2]) - jnp.exp(teacher[...] - lse[0:1]))
    grad_ref[...] = grad.astype(BF16)
    turned[...] = grad.T.astype(BF16)
    half = tokens // NC
    core = which_ref[0]
    mine = turned[pl.ds(pl.multiple_of(core * half, half), half), :]
    other = turned[pl.ds(pl.multiple_of((1 - core) * half, half), half), :]
    width = weights.shape[0] // NX
    for k in range(NX):
        columns = pl.ds(k * width, width)
        block = weights[columns, :]
        other_ref[:, columns] = against(other, block, ((1,), (1,))).astype(BF16)
        mine_ref[:, columns] = against(mine, block, ((1,), (1,)))


def gradient(which, student, teacher, lse, weights):
    vocab, tokens = student.shape
    features = weights.shape[0]
    half = tokens // NC
    return pl.pallas_call(
        grad_kernel,
        out_shape=(
            jax.ShapeDtypeStruct((vocab, tokens), BF16),
            jax.ShapeDtypeStruct((half, features), BF16),
            jax.ShapeDtypeStruct((half, features), F32),
        ),
        in_specs=[SMEM, VMEM, VMEM, VMEM, VMEM],
        out_specs=(VMEM, VMEM, VMEM),
        scratch_shapes=[pltpu.VMEM((tokens, vocab), BF16)],
        compiler_params=pltpu.CompilerParams(vmem_limit_bytes=24 << 20),
        cost_estimate=pl.CostEstimate(
            flops=2 * vocab * tokens * features,
            bytes_accessed=10 << 20,
            transcendentals=2 * vocab * tokens,
        ),
    )(which, student, teacher, lse, weights)


def head_kernel(normed_hbm, grad_ref, out_ref, normed, sems):
    width = normed.shape[0] // NX
    rows = [pl.ds(k * width, width) for k in range(NX)]
    copies = begin(
        [
            pltpu.make_async_copy(normed_hbm.at[rows[k]], normed.at[rows[k]], sems.at[k])
            for k in range(NX)
        ]
    )
    for k in range(NX):
        copies[k].wait()
        out_ref[rows[k], :] = against(normed[rows[k], :], grad_ref[...], ((1,), (1,))).astype(BF16)


def head_product(normed, grad):
    features, tokens = normed.shape
    vocab = grad.shape[0]
    return pl.pallas_call(
        head_kernel,
        out_shape=jax.ShapeDtypeStruct((features, vocab), BF16),
        in_specs=[HBM, VMEM],
        out_specs=VMEM,
        scratch_shapes=[pltpu.VMEM(normed.shape, BF16), pltpu.SemaphoreType.DMA((NX,))],
        compiler_params=pltpu.CompilerParams(vmem_limit_bytes=16 << 20),
        cost_estimate=pl.CostEstimate(
            flops=2 * vocab * tokens * features, bytes_accessed=5 << 20, transcendentals=0
        ),
    )(normed, grad)


def squares_kernel(parts_ref, row_ref, head_ref, out_ref):
    head = jnp.sum(parts_ref[...].astype(F32), axis=0)
    head_ref[...] = head
    row = row_ref[...].astype(F32)
    lane = lax.broadcasted_iota(jnp.int32, out_ref.shape, 1)
    out_ref[...] = jnp.where(lane < 64, jnp.sum(head * head), jnp.sum(row * row))


def updates_kernel(devices, squares_ref, head_ref, row_ref, head_out, row_out):
    squares = jnp.sum(squares_ref[...], axis=0, keepdims=True)
    head = head_ref[...]
    row = row_ref[...].astype(F32)
    head_out[...] = (
        head * lax.rsqrt(squares[:, :1] / (head.size * devices) + epsilon)
    ).astype(BF16)
    row_out[...] = (
        row * lax.rsqrt(squares[:, 64:65] / (row.size * devices) + epsilon)
    ).astype(BF16)


def body(
    teacher_rows, teacher_gain, teacher_head, student_rows, student_gain, student_head, lengths
):
    fs = student_head.shape[1]
    vocab = teacher_head.shape[0]
    z = lax.axis_index("z")
    c = lax.axis_index("core")

    heads = jnp.concatenate([student_head.T, teacher_head.T], axis=0)
    own = lax.all_gather(heads, "x", axis=0, tiled=False)
    blocks, offsets = [own], [0]
    right = left = own
    for step in range(1, NZ // 2 + 1):
        right = shifted(right, "z", NZ, 1)
        blocks.append(right)
        offsets.append(-step)
        if step < NZ // 2:
            left = shifted(left, "z", NZ, -1)
            blocks.append(left)
            offsets.append(step)

    teacher_rows, _ = lax.optimization_barrier((teacher_rows, own))
    block = teacher_rows.T
    wide = block.shape[0]
    values = block.astype(F32)
    scaled = (values * teacher_gain.astype(F32)[:, None]).astype(BF16)
    squares = jnp.stack(split3(jnp.sum(values * values, axis=0)), axis=0)
    sent = jnp.concatenate([scaled, jnp.pad(squares, ((0, HEAD_ROWS - 3), (0, 0)))], axis=0)
    rows = lax.all_gather(sent, ("core", "y"), axis=0, tiled=False)

    normed = normalize(student_rows, student_gain).T
    missing = offsets[-1]
    student_logits, teacher_logits, scale, weights, last_rows, last_normed = most(
        z[None], rows, normed, blocks[:-1], offsets[:-1], missing, wide, fs
    )
    student_logits, teacher_logits, lse, weights = last(
        z[None],
        last_rows,
        last_normed,
        blocks[-1],
        student_logits,
        teacher_logits,
        scale,
        weights,
        missing,
        fs,
    )
    student_w = weights.reshape(NX * NZ * fs, vocab)

    lse = lax.all_to_all(lse, ("core", "y"), 0, 0, tiled=True)
    which = jnp.stack([c, lengths[0]])
    logit_grad, other, mine = gradient(which, student_logits, teacher_logits, lse, student_w)

    other = lax.ppermute(other, "core", [(0, 1), (1, 0)])
    head_part = head_product(normed, logit_grad)
    other, head_part = lax.optimization_barrier((other, head_part))
    mine = (mine + other.astype(F32)).astype(BF16)
    row_grad = lax.psum_scatter(mine, "y", scatter_dimension=0, tiled=True)

    head_part = lax.all_to_all(head_part.reshape(NX, NZ * fs, vocab), "x", 0, 0, tiled=True)
    head_part = jnp.sum(head_part.astype(F32), axis=0).astype(BF16)
    head_part = lax.all_to_all(head_part.reshape(NZ, fs, vocab), "z", 0, 0, tiled=True)

    devices = NX * NZ * NC * NY
    head_grad, squares = pl.pallas_call(
        squares_kernel,
        out_shape=(
            jax.ShapeDtypeStruct((fs, vocab), F32),
            jax.ShapeDtypeStruct((devices, 128), F32),
        ),
    )(head_part, row_grad)
    squares = lax.all_to_all(squares, ("x", "z", "core", "y"), 0, 0, tiled=True)
    head_update, row_update = pl.pallas_call(
        lambda *refs: updates_kernel(devices, *refs),
        out_shape=(
            jax.ShapeDtypeStruct((fs, vocab), BF16),
            jax.ShapeDtypeStruct(row_grad.shape, BF16),
        ),
    )(squares, head_grad, row_grad)
    return (head_update.T, row_update)


def solution(mesh):
    mesh = Mesh(mesh.devices.reshape(NX, NZ, NC, NY), ("x", "z", "core", "y"))
    dp, mp = ("x", "z"), ("core", "y")
    placed = (P(dp, mp), P(mp), P(mp, dp), P(dp, None), P(), P(mp, dp), P(dp))
    return jax.shard_map(
        body,
        mesh=mesh,
        in_specs=placed,
        out_specs=(P(mp, dp), P(dp + mp, None)),
        check_vma=False,
    )
```

time: 233 us -> 234 us (level)
  Pallas kernels: 12.4 us -> 26.8 us
  waiting for transfers between devices: 44.8 us -> 34.7 us
  other arithmetic: 16.3 us -> 10.4 us
  blocking collectives: 78.1 us -> 82.1 us
  local copies, waits for them, and re-layouts: 17.1 us -> 19.5 us
    pallas_call x1 -> x5, Pallas kernels: 9.91 us -> 24.3 us  [the longest x1 14.3 us: most(): pl.pallas_call(kernel, out_shape=(jax.ShapeDtypeStruct((vocab, tokens), F...]
    ppermute x7, waiting for transfers between devices: 35.8 us -> 28.1 us  [shifted(): lax.ppermute(values, axis, [(i, (i + by) % size) for i in range(size)])]
    unnamed x29 -> x33, local copies, waits for them, and re-layouts: 16.2 us -> 19.5 us
    ppermute x1, waiting for transfers between devices: 2.46 us -> 0.01 us  [body(): other = lax.ppermute(other, 'core', [(0, 1), (1, 0)])]
    all_to_all x1, blocking collectives: 15.3 us -> 17.7 us  [body(): lax.all_to_all(head_part.reshape(NZ, fs, vocab), 'z', 0, 0, tiled=True)]
    reduce_sum x4 -> x0, other arithmetic: 2.36 us -> none  [the longest x1 1.61 us: body(): jnp.sum(row_grad * row_grad)]
  transfers between devices with their start and end apart: 11 -> 11, of which waited for: 7 -> 5; matrix products, arithmetic and copies ran while one was open for 5% -> 4% of each run, Pallas kernels for 0% -> 8%
where the time goes in v4:
time: 234 us; the launch traced here: 233 us
  blocking collectives  82.1 us (35%)
  starting transfers between devices  44.2 us (19%)
  waiting for transfers between devices  34.7 us (15%)
  Pallas kernels  26.8 us (11%)
  local copies, waits for them, and re-layouts  19.5 us (8%)
  between operations  14.9 us (6%)
  other arithmetic  10.4 us (4%)
    all_to_all x1, blocking collectives, body(): squares = lax.all_to_all(squares, ('x', 'z', 'core', 'y'), 0, 0, tiled=True)  30.1 us
    ppermute x7, starting transfers between devices, shifted(): lax.ppermute(values, axis, [(i, (i + by) % size) for i in range(size)])  28.8 us
    ppermute x7, waiting for transfers between devices, shifted(): lax.ppermute(values, axis, [(i, (i + by) % size) for i in range(size)])  28.1 us
    all_to_all x1, blocking collectives, body(): lax.all_to_all(head_part.reshape(NX, NZ * fs, vocab), 'x', 0, 0, tiled=True)  22.9 us
    unnamed x33, local copies, waits for them, and re-layouts  19.5 us
    all_to_all x1, blocking collectives, body(): lax.all_to_all(head_part.reshape(NZ, fs, vocab), 'z', 0, 0, tiled=True)  17.7 us
    pallas_call x1, Pallas kernels, most(): pl.pallas_call(kernel, out_shape=(jax.ShapeDtypeStruct((vocab, tokens), F...  14.3 us
    all_to_all x1, starting transfers between devices, body(): lse = lax.all_to_all(lse, ('core', 'y'), 0, 0, tiled=True)  12.3 us
  transfers between devices with their start and end apart: 11, of which 5 were waited for; matrix products, arithmetic and copies ran while one was open for 4% of the time, Pallas kernels for 8%

profile of v4, /device:TPU:1, one launch (start us, length us, event | category | flops | bytes accessed | tf_op | source)
XLA Modules:
  0.0 232.6 jit_solution(2427236601248533008)
XLA Ops:
  7.2 0.0 all-gather.4.cloned.1.call-start
  7.2 0.9 pad_maximum_fusion.1
  8.1 11.4 %all-gather = bf16[896,384]{1,0:T(8,128)(2,1)S(1)} all-gather(bf16[224,384]{1,0:T(8,128)(2,1)S(1)} %pad_maximum_fusion.1), channel_id=2, replica_groups=mesh['x'=4,'z'=8,'core'=2,'y'=8] {'x'}, dimensions={0}, use_global_device_ids=true | all-gather | bytes 860160 | tf_op jit(solution)/shard_map/all_gather | solution.py:353
  19.5 0.7 convert_element_type.99
  20.2 1.1 fusion.6
  21.4 0.8 pad_maximum_fusion
  22.2 0.0 all-gather.4.cloned.1.call-update
  22.3 5.3 %collective-permute-start = (bf16[4,224,384]{2,1,0:T(8,128)(2,1)S(1)}, bf16[4,224,384]{2,1,0:T(8,128)(2,1)S(1)}, u32[]{:S(2)}, u32[]{:S(2)}) collective-permute-start(bf16[4,224,384]{2,1,0:T(8,128)(2,1)S(1)} %bitcast.20), channel_id=1, source_target_pairs={{0,16},{16,32},{32,48},{48,64},{64,80},{80,96},{96,112},{112,0},{1... | collective-permute-start | bytes 2064392 | tf_op jit(solution)/shard_map/ppermute | solution.py:34
  27.6 8.6 %collective-permute-start.1 = (bf16[4,224,384]{2,1,0:T(8,128)(2,1)S(1)}, bf16[4,224,384]{2,1,0:T(8,128)(2,1)S(1)}, u32[]{:S(2)}, u32[]{:S(2)}) collective-permute-start(bf16[4,224,384]{2,1,0:T(8,128)(2,1)S(1)} %bitcast.21), channel_id=1, source_target_pairs={{0,112},{16,0},{32,16},{48,32},{64,48},{80,64},{96,80},{112,96},{1... | collective-permute-start | bytes 2064392 | tf_op jit(solution)/shard_map/ppermute | solution.py:34
  36.2 11.5 %collective-permute-done.refs_4_ = bf16[4,224,384]{2,1,0:T(8,128)(2,1)S(1)} collective-permute-done((bf16[4,224,384]{2,1,0:T(8,128)(2,1)S(1)}, bf16[4,224,384]{2,1,0:T(8,128)(2,1)S(1)}, u32[]{:S(2)}, u32[]{:S(2)}) %collective-permute-start) | collective-permute-done | bytes 688160 | tf_op jit(solution)/shard_map/ppermute | solution.py:34
  47.7 1.9 collective-permute-start.2
  49.6 0.0 copy-start.5
  49.6 0.8 copy-done.5
  50.5 0.0 collective-permute-done.1.refs_5_
  50.5 4.6 %collective-permute-start.3 = (bf16[4,224,384]{2,1,0:T(8,128)(2,1)S(1)}, bf16[4,224,384]{2,1,0:T(8,128)(2,1)}, u32[]{:S(2)}, u32[]{:S(2)}) collective-permute-start(bf16[4,224,384]{2,1,0:T(8,128)(2,1)S(1)} %collective-permute-done.1.refs_5_), channel_id=1, source_target_pairs={{0,112},{16,0},{32,16},{48,32},{64,48},{80,64},{96,80},{112,96},{1... | collective-permute-start | bytes 2064392 | tf_op jit(solution)/shard_map/ppermute | solution.py:34
  55.0 9.9 %collective-permute-done.2.refs_6_ = bf16[4,224,384]{2,1,0:T(8,128)(2,1)S(1)} collective-permute-done((bf16[4,224,384]{2,1,0:T(8,128)(2,1)S(1)}, bf16[4,224,384]{2,1,0:T(8,128)(2,1)S(1)}, u32[]{:S(2)}, u32[]{:S(2)}) %collective-permute-start.2) | collective-permute-done | bytes 688160 | tf_op jit(solution)/shard_map/ppermute | solution.py:34
  64.9 0.0 copy-start.9
  64.9 1.9 collective-permute-start.4
  66.9 4.4 %copy.11 = bf16[640,2048]{0,1:T(8,128)(2,1)} copy(bf16[640,2048]{1,0:T(8,128)(2,1)} %param.10) | data formatting | bytes 5242880 | tf_op args[3]
  71.2 0.0 copy-done.7
  71.2 0.0 copy-done.9
  71.2 0.0 copy-start.15
  71.2 2.4 %fusion = f32[640]{0:T(1024)S(1)} fusion(bf16[640,2048]{0,1:T(8,128)(2,1)} %copy.11), kind=kLoop, calls=%fused_computation.2 | loop fusion | flops 3931520 | bytes 2624000 | tf_op jit(solution)/shard_map/reduce_sum | solution.py:29
  73.6 0.0 collective-permute-done.3.refs_7_
  73.6 4.6 %collective-permute-start.5 = (bf16[4,224,384]{2,1,0:T(8,128)(2,1)}, bf16[4,224,384]{2,1,0:T(8,128)(2,1)}, u32[]{:S(2)}, u32[]{:S(2)}) collective-permute-start(bf16[4,224,384]{2,1,0:T(8,128)(2,1)} %collective-permute-done.3.refs_7_), channel_id=1, source_target_pairs={{0,112},{16,0},{32,16},{48,32},{64,48},{80,64},{96,80},{112,96},{1... | collective-permute-start | bytes 2064392 | tf_op jit(solution)/shard_map/ppermute | solution.py:34
  78.2 0.0 copy-done.15
  78.2 3.1 %collective-permute-done.4.refs_8_ = bf16[4,224,384]{2,1,0:T(8,128)(2,1)} collective-permute-done((bf16[4,224,384]{2,1,0:T(8,128)(2,1)S(1)}, bf16[4,224,384]{2,1,0:T(8,128)(2,1)}, u32[]{:S(2)}, u32[]{:S(2)}) %collective-permute-start.4) | collective-permute-done | bytes 688160 | tf_op jit(solution)/shard_map/ppermute | solution.py:34
  81.3 1.9 collective-permute-start.6
  83.3 2.4 %fusion.3.refs_2_.normed_hbm = bf16[2048,640]{1,0:T(8,128)(2,1)S(1)} fusion(bf16[640,2048]{0,1:T(8,128)(2,1)} %copy.11, f32[2048]{0:T(1024)S(1)} %convert_element_type.108, f32[640]{0:T(1024)S(1)} %add_rsqrt_fusion), kind=kLoop, calls=%fused_computation.5 | loop fusion | flops 5242880 | bytes 5253632 | tf_op jit(solution)/shard_map/transpose | solution.py:374
  85.7 3.6 %collective-permute-done.5.refs_9_ = bf16[4,224,384]{2,1,0:T(8,128)(2,1)} collective-permute-done((bf16[4,224,384]{2,1,0:T(8,128)(2,1)}, bf16[4,224,384]{2,1,0:T(8,128)(2,1)}, u32[]{:S(2)}, u32[]{:S(2)}) %collective-permute-start.5) | collective-permute-done | bytes 688160 | tf_op jit(solution)/shard_map/ppermute | solution.py:34
  89.2 0.0 all-gather.4.cloned.1.call-done
  89.2 3.0 %copy-done = bf16[5376,640]{1,0:T(8,128)(2,1)S(1)} copy-done((bf16[5376,640]{1,0:T(8,128)(2,1)S(1)}, bf16[5376,640]{1,0:T(8,128)(2,1)}, u32[]{:S(2)}) %copy-start) | copy-done | bytes 6881304
  92.2 1.1 copy-done.6
  93.3 1.1 copy-done.8
  94.4 1.1 copy-done.10
  95.5 14.3 %shard_map.86 = (f32[384,640]{1,0:T(8,128)S(1)}, f32[384,640]{1,0:T(8,128)S(1)}, f32[1,640]{1,0:T(1,128)S(1)}, bf16[4,8,64,384]{3,2,1,0:T(8,128)(2,1)S(1)}, bf16...) custom-call(s32[1]{0:T(128)} %bitcast.1.refs_0_, bf16[16,336,640]{2,1,0:T(8,128)(2,1)S(1)} %bitcast.18, ...), custom_call_target="tpu_custom_call" | custom-call | flops 3523215360 | bytes 20971520 | tf_op jit(solution)/shard_map/pallas_call | solution.py:151
  109.8 0.0 collective-permute-done.6.refs_3_
  109.8 2.9 %shard_map.87 = (f32[384,640]{1,0:T(8,128)S(1)}, f32[384,640]{1,0:T(8,128)S(1)}, f32[16,2,640]{2,1,0:T(2,128)}, bf16[4,8,64,384]{3,2,1,0:T(8,128)(2,1)S(1)}) custom-call(s32[1]{0:T(128)} %bitcast.1.refs_0_, bf16[640,640]{1,0:T(8,128)(2,1)S(1)} %get-tuple-element.23.refs_1_, ...), custom_call_target="tpu_custom_call", output_to_operand_aliasing={{3}: (7, {})} | custom-call | flops 440401920 | bytes 8388608 | tf_op jit(solution)/shard_map/pallas_call | solution.py:223
  112.7 0.0 copy-start.3
  112.7 1.2 copy-done.3
  113.9 0.9 copy-done.11
  114.8 0.9 copy-done.13
  115.8 12.3 %all-to-all-start = ((f32[16,2,640]{2,1,0:T(2,128)}), f32[16,2,640]{2,1,0:T(2,128)S(1)}, u32[]{:S(2)}, u32[]{:S(2)}) async-start(f32[16,2,640]{2,1,0:T(2,128)} %get-tuple-element.31), calls=%async_computation | async-start | bytes 163840 | tf_op jit(solution)/shard_map/all_to_all | solution.py:393
  128.0 0.0 reduce-scatter.2.cloned.1.call-start
  128.7 0.1 pad_add_fusion.which_ref
  128.8 6.5 %all-to-all-done.lse_ref = f32[16,2,640]{2,1,0:T(2,128)S(1)} async-done(((f32[16,2,640]{2,1,0:T(2,128)}), f32[16,2,640]{2,1,0:T(2,128)S(1)}, u32[]{:S(2)}, u32[]{:S(2)}) %all-to-all-start) | async-done | bytes 81952 | tf_op jit(solution)/shard_map/all_to_all | solution.py:393
  135.3 1.4 copy-done.4
  136.7 1.2 copy-done.12
  137.9 1.2 copy-done.14
  139.1 2.5 %shard_map.88 = (bf16[384,640]{1,0:T(8,128)(2,1)S(1)}, bf16[320,2048]{1,0:T(8,128)(2,1)S(1)}, f32[320,2048]{1,0:T(8,128)S(1)}) custom-call(s32[2]{0:T(128)S(1)} %pad_add_fusion.which_ref, f32[384,640]{1,0:T(8,128)S(1)} %copy-done.12, f32[384,640]{1,0:T(8,128)S(1)} %copy-done.14, f32[16,2,640]{2,1,0:T(2,128)S(1)} %all-to-all-done.lse_ref, ...), custom_call_target="tpu_custom_call" | custom-call | flops 1006632960 | bytes 10485760 | tf_op jit(solution)/shard_map/pallas_call | solution.py:275
  141.6 3.1 %collective-permute-start.7 = (bf16[320,2048]{1,0:T(8,128)(2,1)S(1)}, bf16[320,2048]{1,0:T(8,128)(2,1)S(1)}, u32[]{:S(2)}, u32[]{:S(2)}) collective-permute-start(bf16[320,2048]{1,0:T(8,128)(2,1)S(1)} %get-tuple-element.33), channel_id=1, source_target_pairs={{0,8},{8,0},{1,9},{9,1},{2,10},{10,2},{3,11},{11,3},{4,12},{12,4},... | collective-permute-start | bytes 3932168 | tf_op jit(solution)/shard_map/ppermute | solution.py:397
  144.7 3.2 %shard_map.89 = bf16[2048,384]{1,0:T(8,128)(2,1)S(1)} custom-call(bf16[2048,640]{1,0:T(8,128)(2,1)S(1)} %fusion.3.refs_2_.normed_hbm, bf16[384,640]{1,0:T(8,128)(2,1)S(1)} %get-tuple-element.34.grad_ref), custom_call_target="tpu_custom_call" | custom-call | flops 1006632960 | bytes 5242880 | tf_op jit(solution)/shard_map/pallas_call | solution.py:311
  148.0 0.0 copy-start.1
  148.0 1.2 copy-done.1
  149.1 0.0 collective-permute-done.7
  149.2 1.5 add_convert_fusion
  150.7 0.0 reduce-scatter.2.cloned.1.call-update
  150.7 0.0 copy-done.2
  150.7 22.9 %all_to_all.26 = bf16[4,512,384]{2,1,0:T(8,128)(2,1)S(1)} all-to-all(bf16[4,512,384]{2,1,0:T(8,128)(2,1)S(1)} %bitcast.19), channel_id=1, replica_groups=mesh['x'=4,'z'=8,'core'=2,'y'=8] {'x'}, dimensions={0} | all-to-all | bytes 3145728 | tf_op jit(solution)/shard_map/all_to_all | solution.py:403
  173.6 0.4 reduce_sum.35
  174.0 17.7 %all_to_all.27.parts_ref = bf16[8,64,384]{2,1,0:T(8,128)(2,1)} all-to-all(bf16[8,64,384]{2,1,0:T(8,128)(2,1)S(1)} %bitcast.24), channel_id=1, replica_groups=mesh['x'=4,'z'=8,'core'=2,'y'=8] {'z'}, dimensions={0} | all-to-all | bytes 786432 | tf_op jit(solution)/shard_map/all_to_all | solution.py:405
  191.7 2.0 shard_map.90
  193.7 30.1 %all_to_all.28 = f32[512,1,128]{2,1,0:T(1,128)} all-to-all(f32[512,1,128]{2,1,0:T(1,128)} %bitcast.26), channel_id=1, replica_groups=mesh['x'=4,'z'=8,'core'=2,'y'=8] {'x','z','core','y'}, dimensions={0} | all-to-all | bytes 524288 | tf_op jit(solution)/shard_map/all_to_all | solution.py:415
  223.8 1.9 shard_map.91
  (17 shorter events, 0.1 us)
Async XLA Ops:
  7.2 82.1 %all-gather.4.cloned.1.call-start = ((), (), s32[]{:S(2)}) async-start(), calls=%async_computation.6 | async-start | bytes 7311360 | tf_op jit(solution)/shard_map/all_gather | solution.py:372
  22.3 25.5 %collective-permute-start = (bf16[4,224,384]{2,1,0:T(8,128)(2,1)S(1)}, bf16[4,224,384]{2,1,0:T(8,128)(2,1)S(1)}, u32[]{:S(2)}, u32[]{:S(2)}) collective-permute-start(bf16[4,224,384]{2,1,0:T(8,128)(2,1)S(1)} %bitcast.20), channel_id=1, source_target_pairs={{0,16},{16,32},{32,48},{48,64},{64,80},{80,96},{96,112},{112,0},{1... | collective-permute-start | bytes 2064392 | tf_op jit(solution)/shard_map/ppermute | solution.py:34
  27.6 22.9 %collective-permute-start.1 = (bf16[4,224,384]{2,1,0:T(8,128)(2,1)S(1)}, bf16[4,224,384]{2,1,0:T(8,128)(2,1)S(1)}, u32[]{:S(2)}, u32[]{:S(2)}) collective-permute-start(bf16[4,224,384]{2,1,0:T(8,128)(2,1)S(1)} %bitcast.21), channel_id=1, source_target_pairs={{0,112},{16,0},{32,16},{48,32},{64,48},{80,64},{96,80},{112,96},{1... | collective-permute-start | bytes 2064392 | tf_op jit(solution)/shard_map/ppermute | solution.py:34
  47.7 17.2 %collective-permute-start.2 = (bf16[4,224,384]{2,1,0:T(8,128)(2,1)S(1)}, bf16[4,224,384]{2,1,0:T(8,128)(2,1)S(1)}, u32[]{:S(2)}, u32[]{:S(2)}) collective-permute-start(bf16[4,224,384]{2,1,0:T(8,128)(2,1)S(1)} %collective-permute-done.refs_4_), channel_id=1, source_target_pairs={{0,16},{16,32},{32,48},{48,64},{64,80},{80,96},{96,112},{112,0},{1... | collective-permute-start | bytes 2064392 | tf_op jit(solution)/shard_map/ppermute | solution.py:34
  49.6 0.8 copy-start.5
  50.5 20.8 %copy-start.7 = (bf16[4,224,384]{2,1,0:T(8,128)(2,1)}, bf16[4,224,384]{2,1,0:T(8,128)(2,1)S(1)}, u32[]{:S(2)}) copy-start(bf16[4,224,384]{2,1,0:T(8,128)(2,1)S(1)} %collective-permute-done.1.refs_5_) | copy-start | bytes 2064388
  50.5 23.2 %collective-permute-start.3 = (bf16[4,224,384]{2,1,0:T(8,128)(2,1)S(1)}, bf16[4,224,384]{2,1,0:T(8,128)(2,1)}, u32[]{:S(2)}, u32[]{:S(2)}) collective-permute-start(bf16[4,224,384]{2,1,0:T(8,128)(2,1)S(1)} %collective-permute-done.1.refs_5_), channel_id=1, source_target_pairs={{0,112},{16,0},{32,16},{48,32},{64,48},{80,64},{96,80},{112,96},{1... | collective-permute-start | bytes 2064392 | tf_op jit(solution)/shard_map/ppermute | solution.py:34
  64.9 6.3 %copy-start.9 = (bf16[4,224,384]{2,1,0:T(8,128)(2,1)}, bf16[4,224,384]{2,1,0:T(8,128)(2,1)S(1)}, u32[]{:S(2)}) copy-start(bf16[4,224,384]{2,1,0:T(8,128)(2,1)S(1)} %collective-permute-done.2.refs_6_) | copy-start | bytes 2064388
  64.9 16.4 %collective-permute-start.4 = (bf16[4,224,384]{2,1,0:T(8,128)(2,1)S(1)}, bf16[4,224,384]{2,1,0:T(8,128)(2,1)}, u32[]{:S(2)}, u32[]{:S(2)}) collective-permute-start(bf16[4,224,384]{2,1,0:T(8,128)(2,1)S(1)} %collective-permute-done.2.refs_6_), channel_id=1, source_target_pairs={{0,16},{16,32},{32,48},{48,64},{64,80},{80,96},{96,112},{112,0},{1... | collective-permute-start | bytes 2064392 | tf_op jit(solution)/shard_map/ppermute | solution.py:34
  71.2 7.0 %copy-start.15 = (bf16[2048]{0:T(1024)(128)(2,1)S(1)}, bf16[2048]{0:T(1024)(128)(2,1)}, u32[]{:S(2)}) copy-start(bf16[2048]{0:T(1024)(128)(2,1)} %param.11) | copy-start | bytes 12292
  73.6 15.6 %collective-permute-start.5 = (bf16[4,224,384]{2,1,0:T(8,128)(2,1)}, bf16[4,224,384]{2,1,0:T(8,128)(2,1)}, u32[]{:S(2)}, u32[]{:S(2)}) collective-permute-start(bf16[4,224,384]{2,1,0:T(8,128)(2,1)} %collective-permute-done.3.refs_7_), channel_id=1, source_target_pairs={{0,112},{16,0},{32,16},{48,32},{64,48},{80,64},{96,80},{112,96},{1... | collective-permute-start | bytes 2064392 | tf_op jit(solution)/shard_map/ppermute | solution.py:34
  81.3 28.4 %collective-permute-start.6 = (bf16[4,224,384]{2,1,0:T(8,128)(2,1)}, bf16[4,224,384]{2,1,0:T(8,128)(2,1)}, u32[]{:S(2)}, u32[]{:S(2)}) collective-permute-start(bf16[4,224,384]{2,1,0:T(8,128)(2,1)} %collective-permute-done.4.refs_8_), channel_id=1, source_target_pairs={{0,16},{16,32},{32,48},{48,64},{64,80},{80,96},{96,112},{112,0},{1... | collective-permute-start | bytes 2064392 | tf_op jit(solution)/shard_map/ppermute | solution.py:34
  89.2 3.0 %copy-start = (bf16[5376,640]{1,0:T(8,128)(2,1)S(1)}, bf16[5376,640]{1,0:T(8,128)(2,1)}, u32[]{:S(2)}) copy-start(bf16[5376,640]{1,0:T(8,128)(2,1)} %all-gather.4.cloned.1.call-done) | copy-start | bytes 20643844
  92.2 1.1 copy-start.6
  93.3 1.1 copy-start.8
  94.4 1.1 copy-start.10
  112.7 1.2 copy-start.3
  113.9 0.9 copy-start.11
  114.8 0.9 copy-start.13
  115.8 19.6 %all-to-all-start = ((f32[16,2,640]{2,1,0:T(2,128)}), f32[16,2,640]{2,1,0:T(2,128)S(1)}, u32[]{:S(2)}, u32[]{:S(2)}) async-start(f32[16,2,640]{2,1,0:T(2,128)} %get-tuple-element.31), calls=%async_computation | async-start | bytes 163840 | tf_op jit(solution)/shard_map/all_to_all | solution.py:393
  128.0 63.7 %reduce-scatter.2.cloned.1.call-start = ((), (), s32[]{:S(2)}) async-start(), calls=%async_computation.5 | async-start | bytes 1474560 | tf_op jit(solution)/shard_map/reduce_scatter | solution.py:401
  135.3 1.4 copy-start.4
  136.7 1.2 copy-start.12
  137.9 1.2 copy-start.14
  141.6 7.5 %collective-permute-start.7 = (bf16[320,2048]{1,0:T(8,128)(2,1)S(1)}, bf16[320,2048]{1,0:T(8,128)(2,1)S(1)}, u32[]{:S(2)}, u32[]{:S(2)}) collective-permute-start(bf16[320,2048]{1,0:T(8,128)(2,1)S(1)} %get-tuple-element.33), channel_id=1, source_target_pairs={{0,8},{8,0},{1,9},{9,1},{2,10},{10,2},{3,11},{11,3},{4,12},{12,4},... | collective-permute-start | bytes 3932168 | tf_op jit(solution)/shard_map/ppermute | solution.py:397
  148.0 1.2 copy-start.1
  149.1 1.5 copy-start.2
Sparse Core Ops, SparseCore 0:
  22.4 59.1 all-gather.3
  150.8 30.3 reduce-scatter.1

commit v5 on v4

v5 whole, which is shorter than its diff:
```python
import jax
import jax.numpy as jnp
from jax import lax
from jax.experimental import pallas as pl
from jax.experimental.pallas import tpu as pltpu
from jax.sharding import Mesh, PartitionSpec as P

F32 = jnp.float32
BF16 = jnp.bfloat16
DT = 5120
NX, NZ, NC, NY = 4, 8, 2, 8
epsilon = 1e-06
HEAD_ROWS = 16
LSE_ROWS = 8
GRANT = 60 << 20
HBM = pl.BlockSpec(memory_space=pltpu.HBM)
VMEM = pl.BlockSpec(memory_space=pltpu.VMEM)
SMEM = pl.BlockSpec(memory_space=pltpu.SMEM)


def split3(values):
    high = values.astype(BF16)
    rest = values - high.astype(F32)
    middle = rest.astype(BF16)
    low = (rest - middle.astype(F32)).astype(BF16)
    return high, middle, low


def normalize(rows, gain):
    values = rows.astype(F32)
    mean_square = jnp.mean(values * values, axis=-1, keepdims=True)
    return (values * lax.rsqrt(mean_square + epsilon) * gain.astype(F32)).astype(BF16)


def along(values):
    pairs = [(i * NC + c, (i + 1 - 2 * c) % NZ * NC + c) for i in range(NZ) for c in range(NC)]
    return lax.ppermute(values, ("z", "core"), pairs)


def swapped(values):
    return lax.ppermute(values, "core", [(0, 1), (1, 0)])


def against(left, right, dims):
    return lax.dot_general(left, right, (dims, ((), ())), preferred_element_type=F32)


def log_sum_exp(values):
    top = jnp.max(values, axis=0, keepdims=True)
    return top + jnp.log(jnp.sum(jnp.exp(values - top), axis=0, keepdims=True))


def place_of(where_ref, offset):
    return lax.rem(where_ref[0] + where_ref[1] * offset + NZ, NZ)


def begin(copies):
    for copy in copies:
        copy.start()
    return copies


def finish(copies):
    for copy in copies:
        copy.wait()


def most_kernel(offsets, missing, wide, fs, where_ref, rows_ref, normed_ref, *refs):
    blocks, refs = refs[: len(offsets)], refs[len(offsets) :]
    student_ref, teacher_ref, scale_ref, weights_ref = refs[:4]
    rows, squares, student_w, teacher_w, normed, student, teacher = refs[4:11]
    row_sems, square_sem, student_sems, teacher_sems, normed_sem, out_sems = refs[11:]
    parts = rows_ref.shape[0]
    ft, vocab = teacher_w.shape[2:]
    places = [place_of(where_ref, offset) for offset in offsets]
    student_copies = [
        pltpu.make_async_copy(
            block.at[:, pl.ds(0, fs)], student_w.at[:, at], student_sems.at[k]
        )
        for k, (block, at) in enumerate(zip(blocks, places))
    ]
    normed_copy = pltpu.make_async_copy(normed_ref, normed, normed_sem)
    teacher_copies = [
        pltpu.make_async_copy(
            block.at[:, pl.ds(fs, ft)], teacher_w.at[:, at], teacher_sems.at[k]
        )
        for k, (block, at) in enumerate(zip(blocks, places))
    ]
    square_copy = pltpu.make_async_copy(
        rows_ref.at[:, pl.ds(wide, HEAD_ROWS)], squares, square_sem
    )
    row_copies = [
        pltpu.make_async_copy(
            rows_ref.at[k, pl.ds(0, wide)], rows.at[pl.ds(k * wide, wide)], row_sems.at[k]
        )
        for k in range(parts)
    ]
    absent = [place_of(where_ref, offset) for offset in missing]
    begin(student_copies + [normed_copy] + teacher_copies + [square_copy] + row_copies)
    for at in absent:
        student_w[:, at] = jnp.zeros((NX, fs, vocab), BF16)
        teacher_w[:, at] = jnp.zeros((NX, ft, vocab), BF16)

    finish(student_copies + [normed_copy])
    out_copies = [
        pltpu.make_async_copy(source, out, out_sems.at[k])
        for k, (source, out) in enumerate(
            [(student_w, weights_ref), (student, student_ref), (teacher, teacher_ref)]
        )
    ]
    out_copies[0].start()
    step = NZ * fs
    total = None
    for k in range(NX):
        part = against(
            student_w[k].reshape(step, vocab), normed[pl.ds(k * step, step), :], ((0,), (0,))
        )
        total = part if total is None else total + part
    student[...] = total
    out_copies[1].start()

    finish(teacher_copies)
    step = NZ * ft
    total = None
    for k in range(NX):
        finish(row_copies[k * parts // NX : (k + 1) * parts // NX])
        part = against(
            teacher_w[k].reshape(step, vocab), rows[pl.ds(k * step, step), :], ((0,), (0,))
        )
        total = part if total is None else total + part
    teacher[...] = total
    out_copies[2].start()
    square_copy.wait()
    square = jnp.sum(jnp.sum(squares[...].astype(F32), axis=0), axis=0, keepdims=True)
    scale_ref[...] = lax.rsqrt(square / DT + epsilon)
    finish(out_copies)


def most(where, rows, normed, blocks, offsets, missing, wide, fs):
    vocab = blocks[0].shape[2]
    ft = blocks[0].shape[1] - fs
    parts, _, tokens = rows.shape
    dma = pltpu.SemaphoreType.DMA

    def kernel(*refs):
        most_kernel(offsets, missing, wide, fs, *refs)

    return pl.pallas_call(
        kernel,
        out_shape=(
            jax.ShapeDtypeStruct((vocab, tokens), F32),
            jax.ShapeDtypeStruct((vocab, tokens), F32),
            jax.ShapeDtypeStruct((1, tokens), F32),
            jax.ShapeDtypeStruct((NX, NZ, fs, vocab), BF16),
        ),
        in_specs=[SMEM, HBM, HBM] + [HBM] * len(blocks),
        out_specs=(HBM, HBM, VMEM, HBM),
        scratch_shapes=[
            pltpu.VMEM((parts * wide, tokens), BF16),
            pltpu.VMEM((parts, HEAD_ROWS, tokens), BF16),
            pltpu.VMEM((NX, NZ, fs, vocab), BF16),
            pltpu.VMEM((NX, NZ, ft, vocab), BF16),
            pltpu.VMEM(normed.shape, BF16),
            pltpu.VMEM((vocab, tokens), F32),
            pltpu.VMEM((vocab, tokens), F32),
            dma((parts,)),
            dma(()),
            dma((len(blocks),)),
            dma((len(blocks),)),
            dma(()),
            dma((3,)),
        ],
        compiler_params=pltpu.CompilerParams(vmem_limit_bytes=GRANT),
        cost_estimate=pl.CostEstimate(
            flops=2 * vocab * tokens * (parts * wide + normed.shape[0]),
            bytes_accessed=20 << 20,
            transcendentals=0,
        ),
    )(where, rows, normed, *blocks)


def last_kernel(missing, fs, where_ref, rows_ref, normed_ref, student_part, teacher_part, *refs):
    scale_ref, _, *blocks = refs[: 2 + len(missing)]
    student_ref, teacher_ref, lse_ref, weights_ref = refs[2 + len(missing) : 6 + len(missing)]
    rows, normed, student_w, teacher_w, student, teacher, sems, out_sems = refs[6 + len(missing) :]
    ft, vocab = teacher_w.shape[2:]
    per_block = rows_ref.shape[0] // NX
    fold = NZ // per_block
    places = [place_of(where_ref, offset) for offset in missing]
    first = [pltpu.make_async_copy(student_part, student, sems.at[0, 0])]
    second = [pltpu.make_async_copy(teacher_part, teacher, sems.at[0, 1])]
    for i, (block, at) in enumerate(zip(blocks, places)):
        copy_sems = sems.at[1 + i]
        inner = pl.multiple_of(lax.rem(at, fold) * ft, 16)
        first.append(
            pltpu.make_async_copy(block.at[:, pl.ds(0, fs)], student_w.at[i], copy_sems.at[0])
        )
        second.append(
            pltpu.make_async_copy(block.at[:, pl.ds(fs, ft)], teacher_w.at[i], copy_sems.at[1])
        )
        for k in range(NX):
            source = pl.multiple_of(k * NZ * fs + at * fs, 16)
            first.append(
                pltpu.make_async_copy(
                    normed_ref.at[pl.ds(source, fs)],
                    normed.at[i, pl.ds(k * fs, fs)],
                    copy_sems.at[2 + k],
                )
            )
            second.append(
                pltpu.make_async_copy(
                    rows_ref.at[k * per_block + lax.div(at, fold), pl.ds(inner, ft)],
                    rows.at[i, pl.ds(k * ft, ft)],
                    copy_sems.at[2 + NX + k],
                )
            )
    begin(first + second)
    finish(first)
    out_copies = [
        pltpu.make_async_copy(student_w.at[i], weights_ref.at[:, at], out_sems.at[2 + i])
        for i, at in enumerate(places)
    ]
    begin(out_copies)
    total = student[...]
    for i in range(len(missing)):
        total += against(student_w[i].reshape(NX * fs, vocab), normed[i], ((0,), (0,)))
    student[...] = total
    out_copies.append(pltpu.make_async_copy(student, student_ref, out_sems.at[0]))
    out_copies[-1].start()
    student_lse = log_sum_exp(total)
    finish(second)
    total = teacher[...]
    for i in range(len(missing)):
        total += against(teacher_w[i].reshape(NX * ft, vocab), rows[i], ((0,), (0,)))
    total = scale_ref[...] * total
    teacher[...] = total
    out_copies.append(pltpu.make_async_copy(teacher, teacher_ref, out_sems.at[1]))
    out_copies[-1].start()
    both = jnp.concatenate([log_sum_exp(total), student_lse], axis=0)
    both = jnp.concatenate([both] * (lse_ref.shape[1] // 2), axis=0)
    lse_ref[...] = jnp.broadcast_to(both[None], lse_ref.shape)
    finish(out_copies)


def last(where, rows, normed, blocks, student, teacher, scale, weights, missing, fs):
    vocab, tokens = student.shape
    ft = blocks[0].shape[1] - fs
    count = len(blocks)

    def kernel(*refs):
        last_kernel(missing, fs, *refs)

    return pl.pallas_call(
        kernel,
        out_shape=(
            jax.ShapeDtypeStruct((vocab, tokens), F32),
            jax.ShapeDtypeStruct((vocab, tokens), F32),
            jax.ShapeDtypeStruct((NC * NY, LSE_ROWS, tokens), F32),
            jax.ShapeDtypeStruct(weights.shape, BF16),
        ),
        in_specs=[SMEM, HBM, HBM, HBM, HBM, VMEM] + [HBM] * (1 + count),
        out_specs=(HBM, HBM, VMEM, HBM),
        input_output_aliases={6: 3},
        scratch_shapes=[
            pltpu.VMEM((count, NX * ft, tokens), BF16),
            pltpu.VMEM((count, NX * fs, tokens), BF16),
            pltpu.VMEM((count, NX, fs, vocab), BF16),
            pltpu.VMEM((count, NX, ft, vocab), BF16),
            pltpu.VMEM((vocab, tokens), F32),
            pltpu.VMEM((vocab, tokens), F32),
            pltpu.SemaphoreType.DMA((1 + count, 2 + 2 * NX)),
            pltpu.SemaphoreType.DMA((2 + count,)),
        ],
        compiler_params=pltpu.CompilerParams(vmem_limit_bytes=GRANT),
        cost_estimate=pl.CostEstimate(
            flops=2 * vocab * tokens * NX * (ft + fs) * count,
            bytes_accessed=8 << 20,
            transcendentals=2 * vocab * tokens,
        ),
    )(where, rows, normed, student, teacher, scale, weights, *blocks)


def grad_kernel(which_ref, student_hbm, teacher_hbm, lse_ref, weights_hbm, normed_hbm, *refs):
    other_hbm, mine_hbm, head_hbm = refs[:3]
    student, teacher, weights, normed, grad_t, turned, other, mine, head, sems, out_sems = refs[3:]
    copies = begin(
        [
            pltpu.make_async_copy(source, held, sems.at[k])
            for k, (source, held) in enumerate(
                [
                    (student_hbm, student),
                    (teacher_hbm, teacher),
                    (weights_hbm, weights),
                    (normed_hbm, normed),
                ]
            )
        ]
    )
    tokens = student.shape[1]
    lses = lse_ref[:, 0:2]
    top = jnp.max(lses, axis=0)
    lse = top + jnp.log(jnp.sum(jnp.exp(lses - top[None]), axis=0))
    position = lax.broadcasted_iota(jnp.int32, (1, tokens), 1)
    live = (position < which_ref[1]).astype(F32)
    finish(copies[:2])
    grad = live * (jnp.exp(student[...] - lse[1:2]) - jnp.exp(teacher[...] - lse[0:1]))
    grad_t[...] = grad.astype(BF16)
    turned[...] = grad.T.astype(BF16)
    half = tokens // NC
    core = which_ref[0]
    parts = [
        (other, other_hbm, turned[pl.ds(pl.multiple_of((1 - core) * half, half), half), :]),
        (mine, mine_hbm, turned[pl.ds(pl.multiple_of(core * half, half), half), :]),
    ]
    width = weights.shape[0] // NX
    slices = [pl.ds(k * width, width) for k in range(NX)]
    copies[2].wait()
    out_copies = []
    for i, (out, hbm, block) in enumerate(parts):
        for columns in slices:
            out[:, columns] = against(block, weights[columns, :], ((1,), (1,))).astype(BF16)
        out_copies.append(pltpu.make_async_copy(out, hbm, out_sems.at[i]))
        out_copies[-1].start()
    copies[3].wait()
    for k, rows in enumerate(slices):
        head[rows, :] = against(normed[rows, :], grad_t[...], ((1,), (1,))).astype(BF16)
        out_copies.append(pltpu.make_async_copy(head.at[rows], head_hbm.at[rows], out_sems.at[2 + k]))
        out_copies[-1].start()
    finish(out_copies)


def gradient(which, student, teacher, lse, weights, normed):
    vocab, tokens = student.shape
    features = weights.shape[0]
    half = tokens // NC
    return pl.pallas_call(
        grad_kernel,
        out_shape=(
            jax.ShapeDtypeStruct((half, features), BF16),
            jax.ShapeDtypeStruct((half, features), BF16),
            jax.ShapeDtypeStruct((features, vocab), BF16),
        ),
        in_specs=[SMEM, HBM, HBM, VMEM, HBM, HBM],
        out_specs=(HBM, HBM, HBM),
        scratch_shapes=[
            pltpu.VMEM((vocab, tokens), F32),
            pltpu.VMEM((vocab, tokens), F32),
            pltpu.VMEM((features, vocab), BF16),
            pltpu.VMEM((features, tokens), BF16),
            pltpu.VMEM((vocab, tokens), BF16),
            pltpu.VMEM((tokens, vocab), BF16),
            pltpu.VMEM((half, features), BF16),
            pltpu.VMEM((half, features), BF16),
            pltpu.VMEM((features, vocab), BF16),
            pltpu.SemaphoreType.DMA((4,)),
            pltpu.SemaphoreType.DMA((2 + NX,)),
        ],
        compiler_params=pltpu.CompilerParams(vmem_limit_bytes=GRANT),
        cost_estimate=pl.CostEstimate(
            flops=4 * vocab * tokens * features,
            bytes_accessed=10 << 20,
            transcendentals=2 * vocab * tokens,
        ),
    )(which, student, teacher, lse, weights, normed)


def squares_kernel(parts_ref, row_ref, head_ref, out_ref):
    head = jnp.sum(parts_ref[...].astype(F32), axis=0)
    head_ref[...] = head
    row = row_ref[...].astype(F32)
    lane = lax.broadcasted_iota(jnp.int32, out_ref.shape, 1)
    out_ref[...] = jnp.where(lane < 64, jnp.sum(head * head), jnp.sum(row * row))


def updates_kernel(devices, squares_ref, head_ref, row_ref, head_out, row_out):
    squares = jnp.sum(squares_ref[...], axis=0, keepdims=True)
    head = head_ref[...]
    row = row_ref[...].astype(F32)
    head_out[...] = (
        head * lax.rsqrt(squares[:, :1] / (head.size * devices) + epsilon)
    ).astype(BF16)
    row_out[...] = (
        row * lax.rsqrt(squares[:, 64:65] / (row.size * devices) + epsilon)
    ).astype(BF16)


def body(
    teacher_rows, teacher_gain, teacher_head, student_rows, student_gain, student_head, lengths
):
    fs = student_head.shape[1]
    vocab = teacher_head.shape[0]
    z = lax.axis_index("z")
    c = lax.axis_index("core")

    block = teacher_rows.T
    wide = block.shape[0]
    values = block.astype(F32)
    scaled = (values * teacher_gain.astype(F32)[:, None]).astype(BF16)
    squares = jnp.stack(split3(jnp.sum(values * values, axis=0)), axis=0)
    sent = jnp.concatenate([scaled, jnp.pad(squares, ((0, HEAD_ROWS - 3), (0, 0)))], axis=0)
    rows = lax.all_gather(sent, ("core", "y"), axis=0, tiled=False)

    heads = jnp.concatenate([student_head.T, teacher_head.T], axis=0)
    own = lax.all_gather(heads, "x", axis=0, tiled=False)
    blocks, offsets = [own], [0]
    mine, theirs = own, swapped(own)
    for step in range(1, NZ // 2):
        mine, theirs = along(mine), along(theirs)
        blocks += [mine, swapped(theirs)]
        offsets += [-step, step]
    blocks.append(along(mine))
    offsets.append(-NZ // 2)

    normed = normalize(student_rows, student_gain).T
    where = jnp.stack([z, 1 - 2 * c])
    missing = offsets[-2:]
    student_logits, teacher_logits, scale, weights = most(
        where, rows, normed, blocks[:-2], offsets[:-2], missing, wide, fs
    )
    student_logits, teacher_logits, lse, weights = last(
        where,
        rows,
        normed,
        blocks[-2:],
        student_logits,
        teacher_logits,
        scale,
        weights,
        missing,
        fs,
    )
    student_w = weights.reshape(NX * NZ * fs, vocab)

    which = jnp.stack([c, lengths[0]])
    lse, which, normed = lax.optimization_barrier((lse, which, normed))
    lse = lax.all_to_all(lse, ("core", "y"), 0, 0, tiled=True)
    other, mine, head_part = gradient(
        which, student_logits, teacher_logits, lse, student_w, normed
    )

    mine = (mine.astype(F32) + swapped(other).astype(F32)).astype(BF16)
    row_grad = lax.psum_scatter(mine, "y", scatter_dimension=0, tiled=True)

    head_part = lax.all_to_all(head_part.reshape(NX, NZ * fs, vocab), "x", 0, 0, tiled=True)
    head_part = jnp.sum(head_part.astype(F32), axis=0).astype(BF16)
    head_part = lax.all_to_all(head_part.reshape(NZ, fs, vocab), "z", 0, 0, tiled=True)

    devices = NX * NZ * NC * NY
    head_grad, squares = pl.pallas_call(
        squares_kernel,
        out_shape=(
            jax.ShapeDtypeStruct((fs, vocab), F32),
            jax.ShapeDtypeStruct((devices, 128), F32),
        ),
    )(head_part, row_grad)
    squares = lax.all_to_all(squares, ("x", "z", "core", "y"), 0, 0, tiled=True)
    head_update, row_update = pl.pallas_call(
        lambda *refs: updates_kernel(devices, *refs),
        out_shape=(
            jax.ShapeDtypeStruct((fs, vocab), BF16),
            jax.ShapeDtypeStruct(row_grad.shape, BF16),
        ),
    )(squares, head_grad, row_grad)
    return (head_update.T, row_update)


def solution(mesh):
    mesh = Mesh(mesh.devices.reshape(NX, NZ, NC, NY), ("x", "z", "core", "y"))
    dp, mp = ("x", "z"), ("core", "y")
    placed = (P(dp, mp), P(mp), P(mp, dp), P(dp, None), P(), P(mp, dp), P(dp))
    return jax.shard_map(
        body,
        mesh=mesh,
        in_specs=placed,
        out_specs=(P(mp, dp), P(dp + mp, None)),
        check_vma=False,
    )
```

time: 234 us -> 228 us (0.974)
  waiting for transfers between devices: 34.7 us -> 13.5 us
  blocking collectives: 82.1 us -> 100 us
  local copies, waits for them, and re-layouts: 19.5 us -> 4.07 us
  starting transfers between devices: 44.2 us -> 51 us
  Pallas kernels: 26.8 us -> 32 us
    ppermute x8 -> x12, starting transfers between devices: 31.8 us -> 50.9 us  [the longest x7 29.7 us: along(): return lax.ppermute(values, ('z', 'core'), pairs)]
    all_to_all x0 -> x1, blocking collectives: none -> 18 us  [body(): lse = lax.all_to_all(lse, ('core', 'y'), 0, 0, tiled=True)]
    unnamed x33 -> x11, local copies, waits for them, and re-layouts: 19.5 us -> 4.06 us
    ppermute x8 -> x12, waiting for transfers between devices: 28.1 us -> 13.5 us  [the longest x7 10.6 us: along(): return lax.ppermute(values, ('z', 'core'), pairs)]
    all_to_all x1 -> x0, starting transfers between devices: 12.3 us -> none  [body(): lse = lax.all_to_all(lse, ('core', 'y'), 0, 0, tiled=True)]
    all_to_all x1 -> x0, waiting for transfers between devices: 6.53 us -> none  [body(): lse = lax.all_to_all(lse, ('core', 'y'), 0, 0, tiled=True)]
    pallas_call x1, Pallas kernels: 2.92 us -> 6.62 us  [last(): pl.pallas_call(kernel, out_shape=(jax.ShapeDtypeStruct((vocab, tokens), F...]
    pallas_call x2 -> x1, Pallas kernels: 5.72 us -> 7.06 us  [gradient(): pl.pallas_call(grad_kernel, out_shape=(jax.ShapeDtypeStruct((half, featur...]
  transfers between devices with their start and end apart: 11 -> 14, of which waited for: 5 -> 5; matrix products, arithmetic and copies ran while one was open for 4% -> 4% of each run, Pallas kernels for 8% -> 6%
where the time goes in v5:
time: 228 us; the launch traced here: 227 us
  blocking collectives  100 us (44%)
  starting transfers between devices  51 us (22%)
  Pallas kernels  32 us (14%)
  between operations  14.9 us (7%)
  waiting for transfers between devices  13.5 us (6%)
  other arithmetic  11.1 us (5%)
  local copies, waits for them, and re-layouts  4.07 us (2%)
    all_to_all x1, blocking collectives, body(): squares = lax.all_to_all(squares, ('x', 'z', 'core', 'y'), 0, 0, tiled=True)  31.5 us
    ppermute x7, starting transfers between devices, along(): return lax.ppermute(values, ('z', 'core'), pairs)  29.7 us
    all_to_all x1, blocking collectives, body(): lax.all_to_all(head_part.reshape(NX, NZ * fs, vocab), 'x', 0, 0, tiled=True)  23.8 us
    ppermute x5, starting transfers between devices, swapped(): return lax.ppermute(values, 'core', [(0, 1), (1, 0)])  21.2 us
    all_to_all x1, blocking collectives, body(): lse = lax.all_to_all(lse, ('core', 'y'), 0, 0, tiled=True)  18 us
    all_to_all x1, blocking collectives, body(): lax.all_to_all(head_part.reshape(NZ, fs, vocab), 'z', 0, 0, tiled=True)  15.7 us
    pallas_call x1, Pallas kernels, most(): pl.pallas_call(kernel, out_shape=(jax.ShapeDtypeStruct((vocab, tokens), F...  14.3 us
    all_gather x1, blocking collectives, body(): own = lax.all_gather(heads, 'x', axis=0, tiled=False)  11.4 us
  transfers between devices with their start and end apart: 14, of which 5 were waited for; matrix products, arithmetic and copies ran while one was open for 4% of the time, Pallas kernels for 6%

profile of v5, /device:TPU:1, one launch (start us, length us, event | category | flops | bytes accessed | tf_op | source)
XLA Modules:
  0.0 227.0 jit_solution(6145907225830283811)
XLA Ops:
  7.2 0.0 all-gather.4.cloned.1.call-start
  7.2 0.7 convert_element_type.102
  7.9 1.1 fusion.6
  9.1 0.8 pad_maximum_fusion
  9.9 0.0 all-gather.4.cloned.1.call-update
  9.9 0.0 reduce-scatter.2.cloned.1.call-start
  10.0 0.9 pad_maximum_fusion.1
  10.9 11.4 %all-gather.1 = bf16[896,384]{1,0:T(8,128)(2,1)S(1)} all-gather(bf16[224,384]{1,0:T(8,128)(2,1)S(1)} %pad_maximum_fusion.1), channel_id=3, replica_groups=mesh['x'=4,'z'=8,'core'=2,'y'=8] {'x'}, dimensions={0}, use_global_device_ids=true | all-gather | bytes 860160 | tf_op jit(solution)/shard_map/all_gather | solution.py:404
  22.3 0.0 copy-start
  22.3 10.5 %collective-permute-start.1 = (bf16[4,224,384]{2,1,0:T(8,128)(2,1)S(1)}, bf16[4,224,384]{2,1,0:T(8,128)(2,1)S(1)}, u32[]{:S(2)}, u32[]{:S(2)}) collective-permute-start(bf16[4,224,384]{2,1,0:T(8,128)(2,1)S(1)} %bitcast.21), channel_id=1, source_target_pairs={{0,8},{8,0},{1,9},{9,1},{2,10},{10,2},{3,11},{11,3},{4,12},{12,4},... | collective-permute-start | bytes 2064392 | tf_op jit(solution)/shard_map/ppermute | solution.py:41
  32.8 5.6 %collective-permute-start = (bf16[4,224,384]{2,1,0:T(8,128)(2,1)S(1)}, bf16[4,224,384]{2,1,0:T(8,128)(2,1)}, u32[]{:S(2)}, u32[]{:S(2)}) collective-permute-start(bf16[4,224,384]{2,1,0:T(8,128)(2,1)S(1)} %bitcast.22), channel_id=1, source_target_pairs={{0,16},{8,120},{16,32},{24,8},{32,48},{40,24},{48,64},{56,40},{64,... | collective-permute-start | bytes 2064392 | tf_op jit(solution)/shard_map/ppermute | solution.py:37
  38.4 0.0 collective-permute-done.1
  38.5 2.2 collective-permute-start.2
  40.6 5.7 %collective-permute-done.refs_4_ = bf16[4,224,384]{2,1,0:T(8,128)(2,1)} collective-permute-done((bf16[4,224,384]{2,1,0:T(8,128)(2,1)S(1)}, bf16[4,224,384]{2,1,0:T(8,128)(2,1)}, u32[]{:S(2)}, u32[]{:S(2)}) %collective-permute-start) | collective-permute-done | bytes 688160 | tf_op jit(solution)/shard_map/ppermute | solution.py:37
  46.3 5.4 %collective-permute-start.4 = (bf16[4,224,384]{2,1,0:T(8,128)(2,1)}, bf16[4,224,384]{2,1,0:T(8,128)(2,1)}, u32[]{:S(2)}, u32[]{:S(2)}) collective-permute-start(bf16[4,224,384]{2,1,0:T(8,128)(2,1)} %collective-permute-done.refs_4_), channel_id=1, source_target_pairs={{0,16},{8,120},{16,32},{24,8},{32,48},{40,24},{48,64},{56,40},{64,... | collective-permute-start | bytes 2064392 | tf_op jit(solution)/shard_map/ppermute | solution.py:37
  51.7 2.0 collective-permute-done.2
  53.7 5.4 %collective-permute-start.5 = (bf16[4,224,384]{2,1,0:T(8,128)(2,1)}, bf16[4,224,384]{2,1,0:T(8,128)(2,1)}, u32[]{:S(2)}, u32[]{:S(2)}) collective-permute-start(bf16[4,224,384]{2,1,0:T(8,128)(2,1)} %collective-permute-done.2), channel_id=1, source_target_pairs={{0,16},{8,120},{16,32},{24,8},{32,48},{40,24},{48,64},{56,40},{64,... | collective-permute-start | bytes 2064392 | tf_op jit(solution)/shard_map/ppermute | solution.py:37
  59.1 0.0 copy-start.4
  59.1 3.2 %copy.11 = bf16[640,2048]{0,1:T(8,128)(2,1)S(1)} copy(bf16[640,2048]{1,0:T(8,128)(2,1)} %param.10) | data formatting | bytes 5242880 | tf_op args[3]
  62.3 0.0 copy-done
  62.3 0.0 copy-done.4
  63.0 0.0 collective-permute-done.4.refs_6_
  63.0 3.5 %collective-permute-start.7 = (bf16[4,224,384]{2,1,0:T(8,128)(2,1)}, bf16[4,224,384]{2,1,0:T(8,128)(2,1)S(1)}, u32[]{:S(2)}, u32[]{:S(2)}) collective-permute-start(bf16[4,224,384]{2,1,0:T(8,128)(2,1)} %collective-permute-done.4.refs_6_), channel_id=1, source_target_pairs={{0,16},{8,120},{16,32},{24,8},{32,48},{40,24},{48,64},{56,40},{64,... | collective-permute-start | bytes 2064392 | tf_op jit(solution)/shard_map/ppermute | solution.py:37
  66.5 2.1 collective-permute-done.5
  68.5 5.0 %collective-permute-start.8 = (bf16[4,224,384]{2,1,0:T(8,128)(2,1)}, bf16[4,224,384]{2,1,0:T(8,128)(2,1)}, u32[]{:S(2)}, u32[]{:S(2)}) collective-permute-start(bf16[4,224,384]{2,1,0:T(8,128)(2,1)} %collective-permute-done.5), channel_id=1, source_target_pairs={{0,16},{8,120},{16,32},{24,8},{32,48},{40,24},{48,64},{56,40},{64,... | collective-permute-start | bytes 2064392 | tf_op jit(solution)/shard_map/ppermute | solution.py:37
  73.6 0.6 pad_add_fusion.refs_0_
  74.2 0.6 fusion
  74.8 1.9 collective-permute-start.3
  76.7 2.4 %collective-permute-start.6 = (bf16[4,224,384]{2,1,0:T(8,128)(2,1)}, bf16[4,224,384]{2,1,0:T(8,128)(2,1)}, u32[]{:S(2)}, u32[]{:S(2)}) collective-permute-start(bf16[4,224,384]{2,1,0:T(8,128)(2,1)} %collective-permute-done.5), channel_id=1, source_target_pairs={{0,8},{8,0},{1,9},{9,1},{2,10},{10,2},{3,11},{11,3},{4,12},{12,4},... | collective-permute-start | bytes 2064392 | tf_op jit(solution)/shard_map/ppermute | solution.py:41
  79.1 0.6 pad_add_fusion.1.which_ref
  79.7 0.0 collective-permute-done.7.refs_8_
  79.7 0.0 copy-start.2
  79.7 2.6 %collective-permute-start.10 = (bf16[4,224,384]{2,1,0:T(8,128)(2,1)S(1)}, bf16[4,224,384]{2,1,0:T(8,128)(2,1)}, u32[]{:S(2)}, u32[]{:S(2)}) collective-permute-start(bf16[4,224,384]{2,1,0:T(8,128)(2,1)S(1)} %collective-permute-done.7.refs_8_), channel_id=1, source_target_pairs={{0,16},{8,120},{16,32},{24,8},{32,48},{40,24},{48,64},{56,40},{64,... | collective-permute-start | bytes 2064392 | tf_op jit(solution)/shard_map/ppermute | solution.py:37
  82.3 1.0 collective-permute-done.8
  83.3 3.2 %collective-permute-start.9 = (bf16[4,224,384]{2,1,0:T(8,128)(2,1)}, bf16[4,224,384]{2,1,0:T(8,128)(2,1)}, u32[]{:S(2)}, u32[]{:S(2)}) collective-permute-start(bf16[4,224,384]{2,1,0:T(8,128)(2,1)} %collective-permute-done.8), channel_id=1, source_target_pairs={{0,8},{8,0},{1,9},{9,1},{2,10},{10,2},{3,11},{11,3},{4,12},{12,4},... | collective-permute-start | bytes 2064392 | tf_op jit(solution)/shard_map/ppermute | solution.py:41
  86.5 2.2 fusion.3.refs_2_.normed_hbm
  88.7 0.0 copy-done.2
  88.7 0.0 collective-permute-done.3.refs_5_
  88.8 0.0 copy-start.3
  88.8 0.9 copy-done.3
  89.6 0.0 collective-permute-done.6.refs_7_
  89.6 0.0 all-gather.4.cloned.1.call-done
  89.6 14.3 %shard_map.86 = (f32[384,640]{1,0:T(8,128)}, f32[384,640]{1,0:T(8,128)}, f32[1,640]{1,0:T(1,128)}, bf16[4,8,64,384]{3,2,1,0:T(8,128)(2,1)}) custom-call(s32[2]{0:T(128)} %pad_add_fusion.refs_0_, bf16[16,336,640]{2,1,0:T(8,128)(2,1)} %bitcast.19, bf16[2048,640]{1,0:T(8,128)(2,1)} %fusion.3.refs_2_.normed_hbm, bf16[4,224,384]{2,1,0:T(8,128)(2,1)} %bitcast.23, ...), custom_call_target="tpu_custom_call" | custom-call | flops 3523215360 | bytes 20971520 | tf_op jit(solution)/shard_map/pallas_call | solution.py:148
  104.0 0.0 collective-permute-done.10.refs_8_
  104.0 0.0 collective-permute-done.9.refs_7_
  104.0 6.6 %shard_map.87 = (f32[384,640]{1,0:T(8,128)}, f32[384,640]{1,0:T(8,128)}, f32[16,8,640]{2,1,0:T(8,128)}, bf16[4,8,64,384]{3,2,1,0:T(8,128)(2,1)}) custom-call(s32[2]{0:T(128)} %pad_add_fusion.refs_0_, bf16[16,336,640]{2,1,0:T(8,128)(2,1)} %bitcast.20, bf16[2048,640]{1,0:T(8,128)(2,1)} %fusion.3.refs_2_.normed_hbm, ...), custom_call_target="tpu_custom_call", output_to_operand_aliasing={{3}: (6, {})} | custom-call | flops 880803840 | bytes 8388608 | tf_op jit(solution)/shard_map/pallas_call | solution.py:253
  110.6 18.0 %all_to_all.26.lse_ref = f32[16,8,640]{2,1,0:T(8,128)} all-to-all(f32[16,8,640]{2,1,0:T(8,128)} %get-tuple-element.28), channel_id=1, replica_groups=mesh['x'=4,'z'=8,'core'=2,'y'=8] {'core','y'}, dimensions={0} | all-to-all | bytes 655360 | tf_op jit(solution)/shard_map/all_to_all | solution.py:436
  128.7 7.1 %shard_map.88 = (bf16[320,2048]{1,0:T(8,128)(2,1)}, bf16[320,2048]{1,0:T(8,128)(2,1)}, bf16[2048,384]{1,0:T(8,128)(2,1)}) custom-call(s32[2]{0:T(128)} %pad_add_fusion.1.which_ref, f32[384,640]{1,0:T(8,128)} %get-tuple-element.26.student_hbm, f32[384,640]{1,0:T(8,128)} %get-tuple-element.27.teacher_hbm, f32[16,8,640]{2,1,0:T(8,128)} %all_to_all.26.lse_ref, ...), custom_call_target="tpu_custom_call" | custom-call | flops 2013265920 | bytes 10485760 | tf_op jit(solution)/shard_map/pallas_call | solution.py:336
  135.7 3.1 %collective-permute-start.11 = (bf16[320,2048]{1,0:T(8,128)(2,1)}, bf16[320,2048]{1,0:T(8,128)(2,1)S(1)}, u32[]{:S(2)}, u32[]{:S(2)}) collective-permute-start(bf16[320,2048]{1,0:T(8,128)(2,1)} %get-tuple-element.33), channel_id=1, source_target_pairs={{0,8},{8,0},{1,9},{9,1},{2,10},{10,2},{3,11},{11,3},{4,12},{12,4},... | collective-permute-start | bytes 3932168 | tf_op jit(solution)/shard_map/ppermute | solution.py:41
  138.9 2.9 %collective-permute-done.11 = bf16[320,2048]{1,0:T(8,128)(2,1)S(1)} collective-permute-done((bf16[320,2048]{1,0:T(8,128)(2,1)}, bf16[320,2048]{1,0:T(8,128)(2,1)S(1)}, u32[]{:S(2)}, u32[]{:S(2)}) %collective-permute-start.11) | collective-permute-done | bytes 1310752 | tf_op jit(solution)/shard_map/ppermute | solution.py:41
  141.7 0.0 copy-start.1
  141.7 3.0 %add_convert_fusion = bf16[320,2048]{1,0:T(8,128)(2,1)} fusion(bf16[320,2048]{1,0:T(8,128)(2,1)S(1)} %collective-permute-done.11, bf16[320,2048]{1,0:T(8,128)(2,1)} %get-tuple-element.32), kind=kLoop, calls=%fused_computation.6 | loop fusion | flops 2621440 | bytes 3932160 | tf_op jit(solution)/shard_map/convert_element_type | solution.py:441
  144.7 0.0 reduce-scatter.2.cloned.1.call-update
  144.8 0.0 copy-done.1
  144.8 23.8 %all_to_all.27 = bf16[4,512,384]{2,1,0:T(8,128)(2,1)S(1)} all-to-all(bf16[4,512,384]{2,1,0:T(8,128)(2,1)S(1)} %bitcast.24), channel_id=1, replica_groups=mesh['x'=4,'z'=8,'core'=2,'y'=8] {'x'}, dimensions={0} | all-to-all | bytes 3145728 | tf_op jit(solution)/shard_map/all_to_all | solution.py:444
  168.6 0.4 reduce_sum.35
  169.0 15.7 %all_to_all.28.parts_ref = bf16[8,64,384]{2,1,0:T(8,128)(2,1)} all-to-all(bf16[8,64,384]{2,1,0:T(8,128)(2,1)S(1)} %bitcast.25), channel_id=1, replica_groups=mesh['x'=4,'z'=8,'core'=2,'y'=8] {'z'}, dimensions={0} | all-to-all | bytes 786432 | tf_op jit(solution)/shard_map/all_to_all | solution.py:446
  184.7 0.0 reduce-scatter.2.cloned.1.call-done.row_ref.refs_2_
  184.7 2.0 shard_map.89
  186.8 31.5 %all_to_all.29 = f32[512,1,128]{2,1,0:T(1,128)} all-to-all(f32[512,1,128]{2,1,0:T(1,128)} %bitcast.28), channel_id=1, replica_groups=mesh['x'=4,'z'=8,'core'=2,'y'=8] {'x','z','core','y'}, dimensions={0} | all-to-all | bytes 524288 | tf_op jit(solution)/shard_map/all_to_all | solution.py:456
  218.2 1.9 shard_map.90
  (5 shorter events, 0.0 us)
Async XLA Ops:
  7.2 82.5 %all-gather.4.cloned.1.call-start = ((), (), s32[]{:S(2)}) async-start(), calls=%async_computation.6 | async-start | bytes 7311360 | tf_op jit(solution)/shard_map/all_gather | solution.py:401
  9.9 174.8 %reduce-scatter.2.cloned.1.call-start = ((), (), s32[]{:S(2)}) async-start(), calls=%async_computation.5 | async-start | bytes 1474560 | tf_op jit(solution)/shard_map/reduce_scatter | solution.py:442
  22.3 40.0 %copy-start = (bf16[896,384]{1,0:T(8,128)(2,1)}, bf16[896,384]{1,0:T(8,128)(2,1)S(1)}, u32[]{:S(2)}) copy-start(bf16[896,384]{1,0:T(8,128)(2,1)S(1)} %all-gather.1) | copy-start | bytes 2064388
  22.3 16.1 %collective-permute-start.1 = (bf16[4,224,384]{2,1,0:T(8,128)(2,1)S(1)}, bf16[4,224,384]{2,1,0:T(8,128)(2,1)S(1)}, u32[]{:S(2)}, u32[]{:S(2)}) collective-permute-start(bf16[4,224,384]{2,1,0:T(8,128)(2,1)S(1)} %bitcast.21), channel_id=1, source_target_pairs={{0,8},{8,0},{1,9},{9,1},{2,10},{10,2},{3,11},{11,3},{4,12},{12,4},... | collective-permute-start | bytes 2064392 | tf_op jit(solution)/shard_map/ppermute | solution.py:41
  32.8 13.5 %collective-permute-start = (bf16[4,224,384]{2,1,0:T(8,128)(2,1)S(1)}, bf16[4,224,384]{2,1,0:T(8,128)(2,1)}, u32[]{:S(2)}, u32[]{:S(2)}) collective-permute-start(bf16[4,224,384]{2,1,0:T(8,128)(2,1)S(1)} %bitcast.22), channel_id=1, source_target_pairs={{0,16},{8,120},{16,32},{24,8},{32,48},{40,24},{48,64},{56,40},{64,... | collective-permute-start | bytes 2064392 | tf_op jit(solution)/shard_map/ppermute | solution.py:37
  38.5 15.2 %collective-permute-start.2 = (bf16[4,224,384]{2,1,0:T(8,128)(2,1)S(1)}, bf16[4,224,384]{2,1,0:T(8,128)(2,1)}, u32[]{:S(2)}, u32[]{:S(2)}) collective-permute-start(bf16[4,224,384]{2,1,0:T(8,128)(2,1)S(1)} %collective-permute-done.1), channel_id=1, source_target_pairs={{0,16},{8,120},{16,32},{24,8},{32,48},{40,24},{48,64},{56,40},{64,... | collective-permute-start | bytes 2064392 | tf_op jit(solution)/shard_map/ppermute | solution.py:37
  46.3 16.7 %collective-permute-start.4 = (bf16[4,224,384]{2,1,0:T(8,128)(2,1)}, bf16[4,224,384]{2,1,0:T(8,128)(2,1)}, u32[]{:S(2)}, u32[]{:S(2)}) collective-permute-start(bf16[4,224,384]{2,1,0:T(8,128)(2,1)} %collective-permute-done.refs_4_), channel_id=1, source_target_pairs={{0,16},{8,120},{16,32},{24,8},{32,48},{40,24},{48,64},{56,40},{64,... | collective-permute-start | bytes 2064392 | tf_op jit(solution)/shard_map/ppermute | solution.py:37
  53.7 14.9 %collective-permute-start.5 = (bf16[4,224,384]{2,1,0:T(8,128)(2,1)}, bf16[4,224,384]{2,1,0:T(8,128)(2,1)}, u32[]{:S(2)}, u32[]{:S(2)}) collective-permute-start(bf16[4,224,384]{2,1,0:T(8,128)(2,1)} %collective-permute-done.2), channel_id=1, source_target_pairs={{0,16},{8,120},{16,32},{24,8},{32,48},{40,24},{48,64},{56,40},{64,... | collective-permute-start | bytes 2064392 | tf_op jit(solution)/shard_map/ppermute | solution.py:37
  59.1 3.2 %copy-start.4 = (bf16[2048]{0:T(1024)(128)(2,1)S(1)}, bf16[2048]{0:T(1024)(128)(2,1)}, u32[]{:S(2)}) copy-start(bf16[2048]{0:T(1024)(128)(2,1)} %param.11) | copy-start | bytes 12292
  63.0 16.7 %collective-permute-start.7 = (bf16[4,224,384]{2,1,0:T(8,128)(2,1)}, bf16[4,224,384]{2,1,0:T(8,128)(2,1)S(1)}, u32[]{:S(2)}, u32[]{:S(2)}) collective-permute-start(bf16[4,224,384]{2,1,0:T(8,128)(2,1)} %collective-permute-done.4.refs_6_), channel_id=1, source_target_pairs={{0,16},{8,120},{16,32},{24,8},{32,48},{40,24},{48,64},{56,40},{64,... | collective-permute-start | bytes 2064392 | tf_op jit(solution)/shard_map/ppermute | solution.py:37
  68.5 14.7 %collective-permute-start.8 = (bf16[4,224,384]{2,1,0:T(8,128)(2,1)}, bf16[4,224,384]{2,1,0:T(8,128)(2,1)}, u32[]{:S(2)}, u32[]{:S(2)}) collective-permute-start(bf16[4,224,384]{2,1,0:T(8,128)(2,1)} %collective-permute-done.5), channel_id=1, source_target_pairs={{0,16},{8,120},{16,32},{24,8},{32,48},{40,24},{48,64},{56,40},{64,... | collective-permute-start | bytes 2064392 | tf_op jit(solution)/shard_map/ppermute | solution.py:37
  74.8 14.0 %collective-permute-start.3 = (bf16[4,224,384]{2,1,0:T(8,128)(2,1)}, bf16[4,224,384]{2,1,0:T(8,128)(2,1)S(1)}, u32[]{:S(2)}, u32[]{:S(2)}) collective-permute-start(bf16[4,224,384]{2,1,0:T(8,128)(2,1)} %collective-permute-done.2), channel_id=1, source_target_pairs={{0,8},{8,0},{1,9},{9,1},{2,10},{10,2},{3,11},{11,3},{4,12},{12,4},... | collective-permute-start | bytes 2064392 | tf_op jit(solution)/shard_map/ppermute | solution.py:41
  76.7 12.9 %collective-permute-start.6 = (bf16[4,224,384]{2,1,0:T(8,128)(2,1)}, bf16[4,224,384]{2,1,0:T(8,128)(2,1)}, u32[]{:S(2)}, u32[]{:S(2)}) collective-permute-start(bf16[4,224,384]{2,1,0:T(8,128)(2,1)} %collective-permute-done.5), channel_id=1, source_target_pairs={{0,8},{8,0},{1,9},{9,1},{2,10},{10,2},{3,11},{11,3},{4,12},{12,4},... | collective-permute-start | bytes 2064392 | tf_op jit(solution)/shard_map/ppermute | solution.py:41
  79.7 9.0 %copy-start.2 = (bf16[4,224,384]{2,1,0:T(8,128)(2,1)}, bf16[4,224,384]{2,1,0:T(8,128)(2,1)S(1)}, u32[]{:S(2)}) copy-start(bf16[4,224,384]{2,1,0:T(8,128)(2,1)S(1)} %collective-permute-done.7.refs_8_) | copy-start | bytes 2064388
  79.7 24.2 %collective-permute-start.10 = (bf16[4,224,384]{2,1,0:T(8,128)(2,1)S(1)}, bf16[4,224,384]{2,1,0:T(8,128)(2,1)}, u32[]{:S(2)}, u32[]{:S(2)}) collective-permute-start(bf16[4,224,384]{2,1,0:T(8,128)(2,1)S(1)} %collective-permute-done.7.refs_8_), channel_id=1, source_target_pairs={{0,16},{8,120},{16,32},{24,8},{32,48},{40,24},{48,64},{56,40},{64,... | collective-permute-start | bytes 2064392 | tf_op jit(solution)/shard_map/ppermute | solution.py:37
  83.3 20.7 %collective-permute-start.9 = (bf16[4,224,384]{2,1,0:T(8,128)(2,1)}, bf16[4,224,384]{2,1,0:T(8,128)(2,1)}, u32[]{:S(2)}, u32[]{:S(2)}) collective-permute-start(bf16[4,224,384]{2,1,0:T(8,128)(2,1)} %collective-permute-done.8), channel_id=1, source_target_pairs={{0,8},{8,0},{1,9},{9,1},{2,10},{10,2},{3,11},{11,3},{4,12},{12,4},... | collective-permute-start | bytes 2064392 | tf_op jit(solution)/shard_map/ppermute | solution.py:41
  88.8 0.9 copy-start.3
  135.7 6.0 %collective-permute-start.11 = (bf16[320,2048]{1,0:T(8,128)(2,1)}, bf16[320,2048]{1,0:T(8,128)(2,1)S(1)}, u32[]{:S(2)}, u32[]{:S(2)}) collective-permute-start(bf16[320,2048]{1,0:T(8,128)(2,1)} %get-tuple-element.33), channel_id=1, source_target_pairs={{0,8},{8,0},{1,9},{9,1},{2,10},{10,2},{3,11},{11,3},{4,12},{12,4},... | collective-permute-start | bytes 3932168 | tf_op jit(solution)/shard_map/ppermute | solution.py:41
  141.7 3.0 %copy-start.1 = (bf16[2048,384]{1,0:T(8,128)(2,1)S(1)}, bf16[2048,384]{1,0:T(8,128)(2,1)}, u32[]{:S(2)}) copy-start(bf16[2048,384]{1,0:T(8,128)(2,1)} %get-tuple-element.31) | copy-start | bytes 4718596
Sparse Core Ops, SparseCore 0:
  10.1 57.0 all-gather.3
  144.9 33.3 reduce-scatter.1

commit v6 on v5

v6 whole, which is shorter than its diff:
```python
import jax
import jax.numpy as jnp
from jax import lax
from jax.experimental import pallas as pl
from jax.experimental.pallas import tpu as pltpu
from jax.sharding import Mesh, PartitionSpec as P

F32 = jnp.float32
BF16 = jnp.bfloat16
DT = 5120
NX, NZ, NC, NY = 4, 8, 2, 8
epsilon = 1e-06
HEAD_ROWS = 16
LSE_ROWS = 8
GRANT = 60 << 20
HBM = pl.BlockSpec(memory_space=pltpu.HBM)
VMEM = pl.BlockSpec(memory_space=pltpu.VMEM)
SMEM = pl.BlockSpec(memory_space=pltpu.SMEM)


def split3(values):
    high = values.astype(BF16)
    rest = values - high.astype(F32)
    middle = rest.astype(BF16)
    low = (rest - middle.astype(F32)).astype(BF16)
    return high, middle, low


def normalize(rows, gain):
    values = rows.astype(F32)
    mean_square = jnp.mean(values * values, axis=-1, keepdims=True)
    return (values * lax.rsqrt(mean_square + epsilon) * gain.astype(F32)).astype(BF16)


def along(values):
    pairs = [(i * NC + c, (i + 1 - 2 * c) % NZ * NC + c) for i in range(NZ) for c in range(NC)]
    return lax.ppermute(values, ("z", "core"), pairs)


def swapped(values):
    return lax.ppermute(values, "core", [(0, 1), (1, 0)])


def against(left, right, dims):
    return lax.dot_general(left, right, (dims, ((), ())), preferred_element_type=F32)


def log_sum_exp(values):
    top = jnp.max(values, axis=0, keepdims=True)
    return top + jnp.log(jnp.sum(jnp.exp(values - top), axis=0, keepdims=True))


def place_of(where_ref, offset):
    return lax.rem(where_ref[0] + where_ref[1] * offset + NZ, NZ)


def begin(copies):
    for copy in copies:
        copy.start()
    return copies


def finish(copies):
    for copy in copies:
        copy.wait()


def block_copies(where_ref, offsets, fs, rows_ref, normed_ref, blocks, held, sems):
    rows, normed, student_w, teacher_w = held
    ft = teacher_w.shape[2]
    per_block = rows_ref.shape[0] // NX
    fold = NZ // per_block
    student, teacher = [], []
    for i, (block, offset) in enumerate(zip(blocks, offsets)):
        at = place_of(where_ref, offset)
        inner = pl.multiple_of(lax.rem(at, fold) * ft, 16)
        copy_sems = sems.at[i]
        student.append(
            pltpu.make_async_copy(block.at[:, pl.ds(0, fs)], student_w.at[:, i], copy_sems.at[0])
        )
        teacher.append(
            pltpu.make_async_copy(block.at[:, pl.ds(fs, ft)], teacher_w.at[:, i], copy_sems.at[1])
        )
        for k in range(NX):
            source = pl.multiple_of(k * NZ * fs + at * fs, 16)
            student.append(
                pltpu.make_async_copy(
                    normed_ref.at[pl.ds(source, fs)], normed.at[k, i], copy_sems.at[2 + k]
                )
            )
            teacher.append(
                pltpu.make_async_copy(
                    rows_ref.at[k * per_block + lax.div(at, fold), pl.ds(inner, ft)],
                    rows.at[k, i],
                    copy_sems.at[2 + NX + k],
                )
            )
    return student, teacher


def weights_copies(where_ref, offsets, student_w, weights_ref, sems):
    return [
        pltpu.make_async_copy(
            student_w.at[:, i], weights_ref.at[:, place_of(where_ref, offset)], sems.at[i]
        )
        for i, offset in enumerate(offsets)
    ]


def product(weights, rows):
    features = weights.shape[1] * weights.shape[2]
    total = None
    for k in range(NX):
        part = against(
            weights[k].reshape(features, weights.shape[3]),
            rows[k].reshape(features, rows.shape[3]),
            ((0,), (0,)),
        )
        total = part if total is None else total + part
    return total


def held_blocks(count, fs, ft, vocab, tokens):
    return [
        pltpu.VMEM((NX, count, ft, tokens), BF16),
        pltpu.VMEM((NX, count, fs, tokens), BF16),
        pltpu.VMEM((NX, count, fs, vocab), BF16),
        pltpu.VMEM((NX, count, ft, vocab), BF16),
        pltpu.VMEM((vocab, tokens), F32),
        pltpu.VMEM((vocab, tokens), F32),
        pltpu.SemaphoreType.DMA((count, 2 + 2 * NX)),
        pltpu.SemaphoreType.DMA((count,)),
        pltpu.SemaphoreType.DMA((4,)),
    ]


def most_kernel(offsets, wide, fs, where_ref, rows_ref, normed_ref, *refs):
    count = len(offsets)
    blocks, refs = refs[:count], refs[count:]
    student_ref, teacher_ref, scale_ref, weights_ref, squares = refs[:5]
    *held, student, teacher, sems, weights_sems, out_sems = refs[5:]
    first, second = block_copies(
        where_ref, offsets, fs, rows_ref, normed_ref, blocks, held, sems
    )
    square_copy = pltpu.make_async_copy(
        rows_ref.at[:, pl.ds(wide, HEAD_ROWS)], squares, out_sems.at[0]
    )
    begin(first + second + [square_copy])
    finish(first)
    out_copies = begin(weights_copies(where_ref, offsets, held[2], weights_ref, weights_sems))
    student[...] = product(held[2], held[1])
    out_copies.append(pltpu.make_async_copy(student, student_ref, out_sems.at[1]))
    out_copies[-1].start()
    finish(second)
    teacher[...] = product(held[3], held[0])
    out_copies.append(pltpu.make_async_copy(teacher, teacher_ref, out_sems.at[2]))
    out_copies[-1].start()
    square_copy.wait()
    square = jnp.sum(jnp.sum(squares[...].astype(F32), axis=0), axis=0, keepdims=True)
    scale_ref[...] = lax.rsqrt(square / DT + epsilon)
    finish(out_copies)


def most(where, rows, normed, blocks, offsets, wide, fs):
    vocab = blocks[0].shape[2]
    ft = blocks[0].shape[1] - fs
    parts, _, tokens = rows.shape

    def kernel(*refs):
        most_kernel(offsets, wide, fs, *refs)

    return pl.pallas_call(
        kernel,
        out_shape=(
            jax.ShapeDtypeStruct((vocab, tokens), F32),
            jax.ShapeDtypeStruct((vocab, tokens), F32),
            jax.ShapeDtypeStruct((1, tokens), F32),
            jax.ShapeDtypeStruct((NX, NZ, fs, vocab), BF16),
        ),
        in_specs=[SMEM, HBM, HBM] + [HBM] * len(blocks),
        out_specs=(HBM, HBM, VMEM, HBM),
        scratch_shapes=[pltpu.VMEM((parts, HEAD_ROWS, tokens), BF16)]
        + held_blocks(len(blocks), fs, ft, vocab, tokens),
        compiler_params=pltpu.CompilerParams(vmem_limit_bytes=GRANT),
        cost_estimate=pl.CostEstimate(
            flops=2 * vocab * tokens * NX * (ft + fs) * len(blocks),
            bytes_accessed=12 << 20,
            transcendentals=0,
        ),
    )(where, rows, normed, *blocks)


def last_kernel(offsets, fs, where_ref, rows_ref, normed_ref, student_part, teacher_part, *refs):
    count = len(offsets)
    scale_ref, _, *blocks = refs[: 2 + count]
    student_ref, teacher_ref, lse_ref, weights_ref = refs[2 + count : 6 + count]
    *held, student, teacher, sems, weights_sems, out_sems = refs[6 + count :]
    first, second = block_copies(
        where_ref, offsets, fs, rows_ref, normed_ref, blocks, held, sems
    )
    first.append(pltpu.make_async_copy(student_part, student, out_sems.at[0]))
    second.append(pltpu.make_async_copy(teacher_part, teacher, out_sems.at[1]))
    begin(first + second)
    finish(first)
    out_copies = begin(weights_copies(where_ref, offsets, held[2], weights_ref, weights_sems))
    total = student[...] + product(held[2], held[1])
    student[...] = total
    out_copies.append(pltpu.make_async_copy(student, student_ref, out_sems.at[2]))
    out_copies[-1].start()
    student_lse = log_sum_exp(total)
    finish(second)
    total = scale_ref[...] * (teacher[...] + product(held[3], held[0]))
    teacher[...] = total
    out_copies.append(pltpu.make_async_copy(teacher, teacher_ref, out_sems.at[3]))
    out_copies[-1].start()
    both = jnp.concatenate([log_sum_exp(total), student_lse], axis=0)
    both = jnp.concatenate([both] * (lse_ref.shape[1] // 2), axis=0)
    lse_ref[...] = jnp.broadcast_to(both[None], lse_ref.shape)
    finish(out_copies)


def last(where, rows, normed, blocks, student, teacher, scale, weights, offsets, fs):
    vocab, tokens = student.shape
    ft = blocks[0].shape[1] - fs

    def kernel(*refs):
        last_kernel(offsets, fs, *refs)

    return pl.pallas_call(
        kernel,
        out_shape=(
            jax.ShapeDtypeStruct((vocab, tokens), F32),
            jax.ShapeDtypeStruct((vocab, tokens), F32),
            jax.ShapeDtypeStruct((NC * NY, LSE_ROWS, tokens), F32),
            jax.ShapeDtypeStruct(weights.shape, BF16),
        ),
        in_specs=[SMEM, HBM, HBM, HBM, HBM, VMEM] + [HBM] * (1 + len(blocks)),
        out_specs=(HBM, HBM, VMEM, HBM),
        input_output_aliases={6: 3},
        scratch_shapes=held_blocks(len(blocks), fs, ft, vocab, tokens),
        compiler_params=pltpu.CompilerParams(vmem_limit_bytes=GRANT),
        cost_estimate=pl.CostEstimate(
            flops=2 * vocab * tokens * NX * (ft + fs) * len(blocks),
            bytes_accessed=8 << 20,
            transcendentals=2 * vocab * tokens,
        ),
    )(where, rows, normed, student, teacher, scale, weights, *blocks)


def grad_kernel(which_ref, student_hbm, teacher_hbm, lse_ref, weights_hbm, *refs):
    other_hbm, mine_hbm, grad_hbm = refs[:3]
    student, teacher, weights, grad_t, turned, other, mine, sems, out_sems = refs[3:]
    copies = begin(
        [
            pltpu.make_async_copy(source, held, sems.at[k])
            for k, (source, held) in enumerate(
                [
                    (student_hbm, student),
                    (teacher_hbm, teacher),
                    (weights_hbm, weights),
                ]
            )
        ]
    )
    tokens = student.shape[1]
    lses = lse_ref[:, 0:2]
    top = jnp.max(lses, axis=0)
    lse = top + jnp.log(jnp.sum(jnp.exp(lses - top[None]), axis=0))
    position = lax.broadcasted_iota(jnp.int32, (1, tokens), 1)
    live = (position < which_ref[1]).astype(F32)
    finish(copies[:2])
    grad = live * (jnp.exp(student[...] - lse[1:2]) - jnp.exp(teacher[...] - lse[0:1]))
    grad_t[...] = grad.astype(BF16)
    turned[...] = grad_t[...].T
    out_copies = begin([pltpu.make_async_copy(grad_t, grad_hbm, out_sems.at[2])])
    half = tokens // NC
    core = which_ref[0]
    parts = [
        (other, other_hbm, turned[pl.ds(pl.multiple_of((1 - core) * half, half), half), :]),
        (mine, mine_hbm, turned[pl.ds(pl.multiple_of(core * half, half), half), :]),
    ]
    width = weights.shape[0] // NX
    slices = [pl.ds(k * width, width) for k in range(NX)]
    copies[2].wait()
    for i, (out, hbm, block) in enumerate(parts):
        for columns in slices:
            out[:, columns] = against(block, weights[columns, :], ((1,), (1,))).astype(BF16)
        out_copies.append(pltpu.make_async_copy(out, hbm, out_sems.at[i]))
        out_copies[-1].start()
    finish(out_copies)


def gradient(which, student, teacher, lse, weights):
    vocab, tokens = student.shape
    features = weights.shape[0]
    half = tokens // NC
    return pl.pallas_call(
        grad_kernel,
        out_shape=(
            jax.ShapeDtypeStruct((half, features), BF16),
            jax.ShapeDtypeStruct((half, features), BF16),
            jax.ShapeDtypeStruct((vocab, tokens), BF16),
        ),
        in_specs=[SMEM, HBM, HBM, VMEM, HBM],
        out_specs=(HBM, HBM, HBM),
        scratch_shapes=[
            pltpu.VMEM((vocab, tokens), F32),
            pltpu.VMEM((vocab, tokens), F32),
            pltpu.VMEM((features, vocab), BF16),
            pltpu.VMEM((vocab, tokens), BF16),
            pltpu.VMEM((tokens, vocab), BF16),
            pltpu.VMEM((half, features), BF16),
            pltpu.VMEM((half, features), BF16),
            pltpu.SemaphoreType.DMA((3,)),
            pltpu.SemaphoreType.DMA((3,)),
        ],
        compiler_params=pltpu.CompilerParams(vmem_limit_bytes=GRANT),
        cost_estimate=pl.CostEstimate(
            flops=2 * vocab * tokens * features,
            bytes_accessed=10 << 20,
            transcendentals=2 * vocab * tokens,
        ),
    )(which, student, teacher, lse, weights)


def head_kernel(normed_hbm, grad_hbm, out_hbm, normed, grad, out, sems, out_sems):
    width = normed.shape[0] // NX
    slices = [pl.ds(k * width, width) for k in range(NX)]
    copies = [pltpu.make_async_copy(grad_hbm, grad, sems.at[NX])]
    copies += [
        pltpu.make_async_copy(normed_hbm.at[rows], normed.at[rows], sems.at[k])
        for k, rows in enumerate(slices)
    ]
    begin(copies)
    copies[0].wait()
    out_copies = []
    for k, rows in enumerate(slices):
        copies[1 + k].wait()
        out[rows, :] = against(normed[rows, :], grad[...], ((1,), (1,))).astype(BF16)
        out_copies.append(pltpu.make_async_copy(out.at[rows], out_hbm.at[rows], out_sems.at[k]))
        out_copies[-1].start()
    finish(out_copies)


def head_product(normed, grad):
    features, vocab = normed.shape[0], grad.shape[0]
    return pl.pallas_call(
        head_kernel,
        out_shape=jax.ShapeDtypeStruct((features, vocab), BF16),
        in_specs=[HBM, HBM],
        out_specs=HBM,
        scratch_shapes=[
            pltpu.VMEM(normed.shape, BF16),
            pltpu.VMEM(grad.shape, BF16),
            pltpu.VMEM((features, vocab), BF16),
            pltpu.SemaphoreType.DMA((1 + NX,)),
            pltpu.SemaphoreType.DMA((NX,)),
        ],
        compiler_params=pltpu.CompilerParams(vmem_limit_bytes=GRANT),
        cost_estimate=pl.CostEstimate(
            flops=2 * vocab * normed.size, bytes_accessed=5 << 20, transcendentals=0
        ),
    )(normed, grad)


def squares_kernel(parts_ref, row_ref, head_ref, out_ref):
    head = jnp.sum(parts_ref[...].astype(F32), axis=0)
    head_ref[...] = head
    row = row_ref[...].astype(F32)
    lane = lax.broadcasted_iota(jnp.int32, out_ref.shape, 1)
    out_ref[...] = jnp.where(lane < 64, jnp.sum(head * head), jnp.sum(row * row))


def updates_kernel(devices, squares_ref, head_ref, row_ref, head_out, row_out):
    squares = jnp.sum(squares_ref[...], axis=0, keepdims=True)
    head = head_ref[...]
    row = row_ref[...].astype(F32)
    head_out[...] = (
        head * lax.rsqrt(squares[:, :1] / (head.size * devices) + epsilon)
    ).astype(BF16)
    row_out[...] = (
        row * lax.rsqrt(squares[:, 64:65] / (row.size * devices) + epsilon)
    ).astype(BF16)


def body(
    teacher_rows, teacher_gain, teacher_head, student_rows, student_gain, student_head, lengths
):
    fs = student_head.shape[1]
    vocab = teacher_head.shape[0]
    z = lax.axis_index("z")
    c = lax.axis_index("core")

    block = teacher_rows.T
    wide = block.shape[0]
    values = block.astype(F32)
    scaled = (values * teacher_gain.astype(F32)[:, None]).astype(BF16)
    squares = jnp.stack(split3(jnp.sum(values * values, axis=0)), axis=0)
    sent = jnp.concatenate([scaled, jnp.pad(squares, ((0, HEAD_ROWS - 3), (0, 0)))], axis=0)
    rows = lax.all_gather(sent, ("core", "y"), axis=0, tiled=False)

    normed = normalize(student_rows, student_gain).T
    heads = jnp.concatenate([student_head.T, teacher_head.T], axis=0)
    own = lax.all_gather(heads, "x", axis=0, tiled=False)
    blocks, offsets = [own], [0]
    mine, theirs = own, swapped(own)
    for step in range(1, NZ // 2):
        mine, theirs = along(mine), along(theirs)
        if step == 1:
            theirs, normed = lax.optimization_barrier((theirs, normed))
        if step < NZ // 2 - 1:
            blocks += [mine, swapped(theirs)]
            offsets += [-step, step]

    early = len(blocks)
    where = jnp.stack([z, 1 - 2 * c])
    student_logits, teacher_logits, scale, weights = most(
        where, rows, normed, blocks[:early], offsets[:early], wide, fs
    )
    mine, theirs, student_logits, teacher_logits, scale, weights = lax.optimization_barrier(
        (mine, theirs, student_logits, teacher_logits, scale, weights)
    )
    blocks += [mine, swapped(theirs), along(mine)]
    offsets += [1 - NZ // 2, NZ // 2 - 1, -NZ // 2]
    student_logits, teacher_logits, lse, weights = last(
        where,
        rows,
        normed,
        blocks[early:],
        student_logits,
        teacher_logits,
        scale,
        weights,
        offsets[early:],
        fs,
    )
    student_w = weights.reshape(NX * NZ * fs, vocab)

    which = jnp.stack([c, lengths[0]])
    lse, which, normed = lax.optimization_barrier((lse, which, normed))
    lse = lax.all_to_all(lse, ("core", "y"), 0, 0, tiled=True)
    other, mine, logit_grad = gradient(which, student_logits, teacher_logits, lse, student_w)
    other = swapped(other)
    head_part = head_product(normed, logit_grad)

    mine = (mine.astype(F32) + other.astype(F32)).astype(BF16)
    row_grad = lax.psum_scatter(mine, "y", scatter_dimension=0, tiled=True)

    head_part = lax.all_to_all(head_part.reshape(NX, NZ * fs, vocab), "x", 0, 0, tiled=True)
    head_part = jnp.sum(head_part.astype(F32), axis=0).astype(BF16)
    head_part = lax.all_to_all(head_part.reshape(NZ, fs, vocab), "z", 0, 0, tiled=True)

    devices = NX * NZ * NC * NY
    head_grad, squares = pl.pallas_call(
        squares_kernel,
        out_shape=(
            jax.ShapeDtypeStruct((fs, vocab), F32),
            jax.ShapeDtypeStruct((devices, 128), F32),
        ),
    )(head_part, row_grad)
    squares = lax.all_to_all(squares, ("x", "z", "core", "y"), 0, 0, tiled=True)
    head_update, row_update = pl.pallas_call(
        lambda *refs: updates_kernel(devices, *refs),
        out_shape=(
            jax.ShapeDtypeStruct((fs, vocab), BF16),
            jax.ShapeDtypeStruct(row_grad.shape, BF16),
        ),
    )(squares, head_grad, row_grad)
    return (head_update.T, row_update)


def solution(mesh):
    mesh = Mesh(mesh.devices.reshape(NX, NZ, NC, NY), ("x", "z", "core", "y"))
    dp, mp = ("x", "z"), ("core", "y")
    placed = (P(dp, mp), P(mp), P(mp, dp), P(dp, None), P(), P(mp, dp), P(dp))
    return jax.shard_map(
        body,
        mesh=mesh,
        in_specs=placed,
        out_specs=(P(mp, dp), P(dp + mp, None)),
        check_vma=False,
    )
```

time: 228 us -> 244 us (1.070)
  waiting for transfers between devices: 13.5 us -> 29.2 us
  blocking collectives: 100 us -> 103 us
  starting transfers between devices: 51 us -> 48.2 us
    ppermute x7, waiting for transfers between devices: 10.6 us -> 26.4 us  [along(): return lax.ppermute(values, ('z', 'core'), pairs)]
    ppermute x7, starting transfers between devices: 29.7 us -> 23 us  [along(): return lax.ppermute(values, ('z', 'core'), pairs)]
    pallas_call x1, Pallas kernels: 14.3 us -> 9.47 us  [most(): pl.pallas_call(kernel, out_shape=(jax.ShapeDtypeStruct((vocab, tokens), F...]
    pallas_call x0 -> x1, Pallas kernels: none -> 4.44 us  [head_product(): pl.pallas_call(head_kernel, out_shape=jax.ShapeDtypeStruct((features, voc...]
    ppermute x5, starting transfers between devices: 21.2 us -> 25.1 us  [swapped(): return lax.ppermute(values, 'core', [(0, 1), (1, 0)])]
    unnamed x11 -> x17, local copies, waits for them, and re-layouts: 4.06 us -> 5.08 us
  transfers between devices with their start and end apart: 14 -> 14, of which waited for: 5 -> 6; matrix products, arithmetic and copies ran while one was open for 4% -> 4% of each run, Pallas kernels for 6% -> 6%
where the time goes in v6:
time: 244 us; the launch traced here: 243 us
  blocking collectives  103 us (42%)
  starting transfers between devices  48.2 us (20%)
  Pallas kernels  31.5 us (13%)
  waiting for transfers between devices  29.2 us (12%)
  between operations  15 us (6%)
  other arithmetic  11 us (5%)
  local copies, waits for them, and re-layouts  5.09 us (2%)
    all_to_all x1, blocking collectives, body(): squares = lax.all_to_all(squares, ('x', 'z', 'core', 'y'), 0, 0, tiled=True)  31.6 us
    ppermute x7, waiting for transfers between devices, along(): return lax.ppermute(values, ('z', 'core'), pairs)  26.4 us
    ppermute x5, starting transfers between devices, swapped(): return lax.ppermute(values, 'core', [(0, 1), (1, 0)])  25.1 us
    all_to_all x1, blocking collectives, body(): lax.all_to_all(head_part.reshape(NX, NZ * fs, vocab), 'x', 0, 0, tiled=True)  24 us
    ppermute x7, starting transfers between devices, along(): return lax.ppermute(values, ('z', 'core'), pairs)  23 us
    all_to_all x1, blocking collectives, body(): lse = lax.all_to_all(lse, ('core', 'y'), 0, 0, tiled=True)  20 us
    all_to_all x1, blocking collectives, body(): lax.all_to_all(head_part.reshape(NZ, fs, vocab), 'z', 0, 0, tiled=True)  15.7 us
    all_gather x1, blocking collectives, body(): own = lax.all_gather(heads, 'x', axis=0, tiled=False)  11.4 us
  transfers between devices with their start and end apart: 14, of which 6 were waited for; matrix products, arithmetic and copies ran while one was open for 4% of the time, Pallas kernels for 6%

profile of v6, /device:TPU:1, one launch (start us, length us, event | category | flops | bytes accessed | tf_op | source)
XLA Modules:
  0.0 242.6 jit_solution(12051508585996489873)
XLA Ops:
  7.2 0.0 all-gather.4.cloned.1.call-start
  7.2 0.7 convert_element_type.102
  7.9 1.1 fusion.6
  9.1 0.8 pad_maximum_fusion
  9.9 0.0 all-gather.4.cloned.1.call-update
  9.9 0.0 reduce-scatter.2.cloned.1.call-start
  10.0 0.9 pad_maximum_fusion.1
  10.9 11.4 %all-gather.1 = bf16[896,384]{1,0:T(8,128)(2,1)S(1)} all-gather(bf16[224,384]{1,0:T(8,128)(2,1)S(1)} %pad_maximum_fusion.1), channel_id=3, replica_groups=mesh['x'=4,'z'=8,'core'=2,'y'=8] {'x'}, dimensions={0}, use_global_device_ids=true | all-gather | bytes 860160 | tf_op jit(solution)/shard_map/all_gather | solution.py:404
  22.3 0.0 copy-start
  22.3 10.5 %collective-permute-start = (bf16[4,224,384]{2,1,0:T(8,128)(2,1)S(1)}, bf16[4,224,384]{2,1,0:T(8,128)(2,1)}, u32[]{:S(2)}, u32[]{:S(2)}) collective-permute-start(bf16[4,224,384]{2,1,0:T(8,128)(2,1)S(1)} %bitcast.23), channel_id=1, source_target_pairs={{0,8},{8,0},{1,9},{9,1},{2,10},{10,2},{3,11},{11,3},{4,12},{12,4},... | collective-permute-start | bytes 2064392 | tf_op jit(solution)/shard_map/ppermute | solution.py:41
  32.8 5.6 %collective-permute-start.2 = (bf16[4,224,384]{2,1,0:T(8,128)(2,1)S(1)}, bf16[4,224,384]{2,1,0:T(8,128)(2,1)}, u32[]{:S(2)}, u32[]{:S(2)}) collective-permute-start(bf16[4,224,384]{2,1,0:T(8,128)(2,1)S(1)} %bitcast.24), channel_id=1, source_target_pairs={{0,16},{8,120},{16,32},{24,8},{32,48},{40,24},{48,64},{56,40},{64,... | collective-permute-start | bytes 2064392 | tf_op jit(solution)/shard_map/ppermute | solution.py:37
  38.5 3.2 %copy.11 = bf16[640,2048]{0,1:T(8,128)(2,1)S(1)} copy(bf16[640,2048]{1,0:T(8,128)(2,1)} %param.10) | data formatting | bytes 5242880 | tf_op args[3]
  41.7 0.0 copy-done
  41.7 0.0 copy-start.7
  41.7 0.6 fusion
  42.3 0.0 collective-permute-done
  42.3 2.2 collective-permute-start.1
  44.5 0.0 copy-done.7
  44.5 2.3 fusion.3.refs_2_.normed_hbm
  46.7 7.8 %collective-permute-done.1 = bf16[4,224,384]{2,1,0:T(8,128)(2,1)} collective-permute-done((bf16[4,224,384]{2,1,0:T(8,128)(2,1)}, bf16[4,224,384]{2,1,0:T(8,128)(2,1)}, u32[]{:S(2)}, u32[]{:S(2)}) %collective-permute-start.1) | collective-permute-done | bytes 688160 | tf_op jit(solution)/shard_map/ppermute | solution.py:37
  54.6 4.5 %collective-permute-start.5 = (bf16[4,224,384]{2,1,0:T(8,128)(2,1)}, bf16[4,224,384]{2,1,0:T(8,128)(2,1)S(1)}, u32[]{:S(2)}, u32[]{:S(2)}) collective-permute-start(bf16[4,224,384]{2,1,0:T(8,128)(2,1)} %collective-permute-done.1), channel_id=1, source_target_pairs={{0,16},{8,120},{16,32},{24,8},{32,48},{40,24},{48,64},{56,40},{64,... | collective-permute-start | bytes 2064392 | tf_op jit(solution)/shard_map/ppermute | solution.py:37
  59.1 0.0 collective-permute-done.2.refs_4_
  59.1 1.9 collective-permute-start.3
  61.1 1.9 collective-permute-start.7
  63.0 4.3 %collective-permute-done.5 = bf16[4,224,384]{2,1,0:T(8,128)(2,1)S(1)} collective-permute-done((bf16[4,224,384]{2,1,0:T(8,128)(2,1)}, bf16[4,224,384]{2,1,0:T(8,128)(2,1)S(1)}, u32[]{:S(2)}, u32[]{:S(2)}) %collective-permute-start.5) | collective-permute-done | bytes 688160 | tf_op jit(solution)/shard_map/ppermute | solution.py:37
  67.3 4.0 %collective-permute-start.8 = (bf16[4,224,384]{2,1,0:T(8,128)(2,1)S(1)}, bf16[4,224,384]{2,1,0:T(8,128)(2,1)S(1)}, u32[]{:S(2)}, u32[]{:S(2)}) collective-permute-start(bf16[4,224,384]{2,1,0:T(8,128)(2,1)S(1)} %collective-permute-done.5), channel_id=1, source_target_pairs={{0,8},{8,0},{1,9},{9,1},{2,10},{10,2},{3,11},{11,3},{4,12},{12,4},... | collective-permute-start | bytes 2064392 | tf_op jit(solution)/shard_map/ppermute | solution.py:41
  71.3 3.4 %collective-permute-done.3.refs_6_ = bf16[4,224,384]{2,1,0:T(8,128)(2,1)S(1)} collective-permute-done((bf16[4,224,384]{2,1,0:T(8,128)(2,1)}, bf16[4,224,384]{2,1,0:T(8,128)(2,1)S(1)}, u32[]{:S(2)}, u32[]{:S(2)}) %collective-permute-start.3) | collective-permute-done | bytes 688160 | tf_op jit(solution)/shard_map/ppermute | solution.py:37
  74.7 0.0 copy-start.4
  74.7 4.9 %collective-permute-start.4 = (bf16[4,224,384]{2,1,0:T(8,128)(2,1)S(1)}, bf16[4,224,384]{2,1,0:T(8,128)(2,1)S(1)}, u32[]{:S(2)}, u32[]{:S(2)}) collective-permute-start(bf16[4,224,384]{2,1,0:T(8,128)(2,1)S(1)} %collective-permute-done.3.refs_6_), channel_id=1, source_target_pairs={{0,16},{8,120},{16,32},{24,8},{32,48},{40,24},{48,64},{56,40},{64,... | collective-permute-start | bytes 2064392 | tf_op jit(solution)/shard_map/ppermute | solution.py:37
  79.6 1.9 collective-permute-start.6
  81.5 0.6 pad_add_fusion.refs_0_
  82.1 0.0 collective-permute-done.7.refs_5_
  82.1 0.0 collective-permute-done.8.refs_7_
  82.1 0.0 copy-start.6
  82.1 0.0 all-gather.4.cloned.1.call-done
  82.1 0.0 copy-done.4
  82.1 0.8 copy-done.5
  82.9 0.2 copy-done.6
  83.2 9.5 %shard_map.86 = (f32[384,640]{1,0:T(8,128)}, f32[384,640]{1,0:T(8,128)}, f32[1,640]{1,0:T(1,128)}, bf16[4,8,64,384]{3,2,1,0:T(8,128)(2,1)}) custom-call(s32[2]{0:T(128)} %pad_add_fusion.refs_0_, bf16[16,336,640]{2,1,0:T(8,128)(2,1)} %bitcast.19, bf16[2048,640]{1,0:T(8,128)(2,1)} %fusion.3.refs_2_.normed_hbm, bf16[4,224,384]{2,1,0:T(8,128)(2,1)} %bitcast.25, ...), custom_call_target="tpu_custom_call" | custom-call | flops 2202009600 | bytes 12582912 | tf_op jit(solution)/shard_map/pallas_call | solution.py:172
  92.6 0.0 collective-permute-done.4.refs_7_
  92.6 0.0 copy-start.1
  92.6 2.2 collective-permute-done.6
  94.8 5.3 %collective-permute-start.9 = (bf16[4,224,384]{2,1,0:T(8,128)(2,1)}, bf16[4,224,384]{2,1,0:T(8,128)(2,1)S(1)}, u32[]{:S(2)}, u32[]{:S(2)}) collective-permute-start(bf16[4,224,384]{2,1,0:T(8,128)(2,1)} %collective-permute-done.6), channel_id=1, source_target_pairs={{0,8},{8,0},{1,9},{9,1},{2,10},{10,2},{3,11},{11,3},{4,12},{12,4},... | collective-permute-start | bytes 2064392 | tf_op jit(solution)/shard_map/ppermute | solution.py:41
  100.2 1.9 collective-permute-start.10
  102.7 0.7 pad_add_fusion.1.which_ref
  103.4 0.0 collective-permute-done.9.refs_8_
  103.4 8.7 %collective-permute-done.10.refs_9_ = bf16[4,224,384]{2,1,0:T(8,128)(2,1)S(1)} collective-permute-done((bf16[4,224,384]{2,1,0:T(8,128)(2,1)S(1)}, bf16[4,224,384]{2,1,0:T(8,128)(2,1)S(1)}, u32[]{:S(2)}, u32[]{:S(2)}) %collective-permute-start.10) | collective-permute-done | bytes 688160 | tf_op jit(solution)/shard_map/ppermute | solution.py:37
  112.1 0.0 copy-done.1
  112.1 0.0 copy-done.2
  112.2 0.9 copy-done.3
  113.0 8.0 %shard_map.87 = (f32[384,640]{1,0:T(8,128)}, f32[384,640]{1,0:T(8,128)}, f32[16,8,640]{2,1,0:T(8,128)}, bf16[4,8,64,384]{3,2,1,0:T(8,128)(2,1)}) custom-call(s32[2]{0:T(128)} %pad_add_fusion.refs_0_, bf16[16,336,640]{2,1,0:T(8,128)(2,1)} %bitcast.20, bf16[2048,640]{1,0:T(8,128)(2,1)} %fusion.3.refs_2_.normed_hbm, ...), custom_call_target="tpu_custom_call", output_to_operand_aliasing={{3}: (6, {})} | custom-call | flops 1321205760 | bytes 8388608 | tf_op jit(solution)/shard_map/pallas_call | solution.py:229
  121.1 20.0 %all_to_all.26.lse_ref = f32[16,8,640]{2,1,0:T(8,128)} all-to-all(f32[16,8,640]{2,1,0:T(8,128)} %get-tuple-element.45), channel_id=1, replica_groups=mesh['x'=4,'z'=8,'core'=2,'y'=8] {'core','y'}, dimensions={0} | all-to-all | bytes 655360 | tf_op jit(solution)/shard_map/all_to_all | solution.py:441
  141.1 5.7 %shard_map.88 = (bf16[320,2048]{1,0:T(8,128)(2,1)}, bf16[320,2048]{1,0:T(8,128)(2,1)}, bf16[384,640]{1,0:T(8,128)(2,1)}) custom-call(s32[2]{0:T(128)} %pad_add_fusion.1.which_ref, f32[384,640]{1,0:T(8,128)} %get-tuple-element.43.student_hbm, f32[384,640]{1,0:T(8,128)} %get-tuple-element.44.teacher_hbm, f32[16,8,640]{2,1,0:T(8,128)} %all_to_all.26.lse_ref, ...), custom_call_target="tpu_custom_call" | custom-call | flops 1006632960 | bytes 10485760 | tf_op jit(solution)/shard_map/pallas_call | solution.py:297
  146.7 3.3 %collective-permute-start.11 = (bf16[320,2048]{1,0:T(8,128)(2,1)}, bf16[320,2048]{1,0:T(8,128)(2,1)S(1)}, u32[]{:S(2)}, u32[]{:S(2)}) collective-permute-start(bf16[320,2048]{1,0:T(8,128)(2,1)} %get-tuple-element.49), channel_id=1, source_target_pairs={{0,8},{8,0},{1,9},{9,1},{2,10},{10,2},{3,11},{11,3},{4,12},{12,4},... | collective-permute-start | bytes 3932168 | tf_op jit(solution)/shard_map/ppermute | solution.py:41
  150.1 2.7 %collective-permute-done.11 = bf16[320,2048]{1,0:T(8,128)(2,1)S(1)} collective-permute-done((bf16[320,2048]{1,0:T(8,128)(2,1)}, bf16[320,2048]{1,0:T(8,128)(2,1)S(1)}, u32[]{:S(2)}, u32[]{:S(2)}) %collective-permute-start.11) | collective-permute-done | bytes 1310752 | tf_op jit(solution)/shard_map/ppermute | solution.py:41
  152.7 2.9 %add_convert_fusion = bf16[320,2048]{1,0:T(8,128)(2,1)} fusion(bf16[320,2048]{1,0:T(8,128)(2,1)S(1)} %collective-permute-done.11, bf16[320,2048]{1,0:T(8,128)(2,1)} %get-tuple-element.48), kind=kLoop, calls=%fused_computation.6 | loop fusion | flops 2621440 | bytes 3932160 | tf_op jit(solution)/shard_map/convert_element_type | solution.py:446
  155.6 0.0 reduce-scatter.2.cloned.1.call-update
  155.6 4.4 %shard_map.89 = bf16[2048,384]{1,0:T(8,128)(2,1)} custom-call(bf16[2048,640]{1,0:T(8,128)(2,1)} %fusion.3.refs_2_.normed_hbm, bf16[384,640]{1,0:T(8,128)(2,1)} %get-tuple-element.47.grad_hbm), custom_call_target="tpu_custom_call" | custom-call | flops 1006632960 | bytes 5242880 | tf_op jit(solution)/shard_map/pallas_call | solution.py:347
  160.1 24.0 %all_to_all.27 = bf16[4,512,384]{2,1,0:T(8,128)(2,1)S(1)} all-to-all(bf16[4,512,384]{2,1,0:T(8,128)(2,1)} %bitcast.21), channel_id=1, replica_groups=mesh['x'=4,'z'=8,'core'=2,'y'=8] {'x'}, dimensions={0} | all-to-all | bytes 3145728 | tf_op jit(solution)/shard_map/all_to_all | solution.py:449
  184.1 0.4 reduce_sum.35
  184.5 15.7 %all_to_all.28.parts_ref = bf16[8,64,384]{2,1,0:T(8,128)(2,1)} all-to-all(bf16[8,64,384]{2,1,0:T(8,128)(2,1)S(1)} %bitcast.26), channel_id=1, replica_groups=mesh['x'=4,'z'=8,'core'=2,'y'=8] {'z'}, dimensions={0} | all-to-all | bytes 786432 | tf_op jit(solution)/shard_map/all_to_all | solution.py:451
  200.3 2.0 shard_map.90
  202.3 31.6 %all_to_all.29 = f32[512,1,128]{2,1,0:T(1,128)} all-to-all(f32[512,1,128]{2,1,0:T(1,128)} %bitcast.28), channel_id=1, replica_groups=mesh['x'=4,'z'=8,'core'=2,'y'=8] {'x','z','core','y'}, dimensions={0} | all-to-all | bytes 524288 | tf_op jit(solution)/shard_map/all_to_all | solution.py:461
  233.9 1.9 shard_map.91
  (9 shorter events, 0.0 us)
Async XLA Ops:
  7.2 75.0 %all-gather.4.cloned.1.call-start = ((), (), s32[]{:S(2)}) async-start(), calls=%async_computation.6 | async-start | bytes 7311360 | tf_op jit(solution)/shard_map/all_gather | solution.py:400
  9.9 190.3 %reduce-scatter.2.cloned.1.call-start = ((), (), s32[]{:S(2)}) async-start(), calls=%async_computation.5 | async-start | bytes 1474560 | tf_op jit(solution)/shard_map/reduce_scatter | solution.py:447
  22.3 19.3 %copy-start = (bf16[896,384]{1,0:T(8,128)(2,1)}, bf16[896,384]{1,0:T(8,128)(2,1)S(1)}, u32[]{:S(2)}) copy-start(bf16[896,384]{1,0:T(8,128)(2,1)S(1)} %all-gather.1) | copy-start | bytes 2064388
  22.3 20.0 %collective-permute-start = (bf16[4,224,384]{2,1,0:T(8,128)(2,1)S(1)}, bf16[4,224,384]{2,1,0:T(8,128)(2,1)}, u32[]{:S(2)}, u32[]{:S(2)}) collective-permute-start(bf16[4,224,384]{2,1,0:T(8,128)(2,1)S(1)} %bitcast.23), channel_id=1, source_target_pairs={{0,8},{8,0},{1,9},{9,1},{2,10},{10,2},{3,11},{11,3},{4,12},{12,4},... | collective-permute-start | bytes 2064392 | tf_op jit(solution)/shard_map/ppermute | solution.py:41
  32.8 26.3 %collective-permute-start.2 = (bf16[4,224,384]{2,1,0:T(8,128)(2,1)S(1)}, bf16[4,224,384]{2,1,0:T(8,128)(2,1)}, u32[]{:S(2)}, u32[]{:S(2)}) collective-permute-start(bf16[4,224,384]{2,1,0:T(8,128)(2,1)S(1)} %bitcast.24), channel_id=1, source_target_pairs={{0,16},{8,120},{16,32},{24,8},{32,48},{40,24},{48,64},{56,40},{64,... | collective-permute-start | bytes 2064392 | tf_op jit(solution)/shard_map/ppermute | solution.py:37
  41.7 2.8 %copy-start.7 = (bf16[2048]{0:T(1024)(128)(2,1)S(1)}, bf16[2048]{0:T(1024)(128)(2,1)}, u32[]{:S(2)}) copy-start(bf16[2048]{0:T(1024)(128)(2,1)} %param.11) | copy-start | bytes 12292
  42.3 12.3 %collective-permute-start.1 = (bf16[4,224,384]{2,1,0:T(8,128)(2,1)}, bf16[4,224,384]{2,1,0:T(8,128)(2,1)}, u32[]{:S(2)}, u32[]{:S(2)}) collective-permute-start(bf16[4,224,384]{2,1,0:T(8,128)(2,1)} %collective-permute-done), channel_id=1, source_target_pairs={{0,16},{8,120},{16,32},{24,8},{32,48},{40,24},{48,64},{56,40},{64,... | collective-permute-start | bytes 2064392 | tf_op jit(solution)/shard_map/ppermute | solution.py:37
  54.6 12.7 %collective-permute-start.5 = (bf16[4,224,384]{2,1,0:T(8,128)(2,1)}, bf16[4,224,384]{2,1,0:T(8,128)(2,1)S(1)}, u32[]{:S(2)}, u32[]{:S(2)}) collective-permute-start(bf16[4,224,384]{2,1,0:T(8,128)(2,1)} %collective-permute-done.1), channel_id=1, source_target_pairs={{0,16},{8,120},{16,32},{24,8},{32,48},{40,24},{48,64},{56,40},{64,... | collective-permute-start | bytes 2064392 | tf_op jit(solution)/shard_map/ppermute | solution.py:37
  59.1 15.5 %collective-permute-start.3 = (bf16[4,224,384]{2,1,0:T(8,128)(2,1)}, bf16[4,224,384]{2,1,0:T(8,128)(2,1)S(1)}, u32[]{:S(2)}, u32[]{:S(2)}) collective-permute-start(bf16[4,224,384]{2,1,0:T(8,128)(2,1)} %collective-permute-done.2.refs_4_), channel_id=1, source_target_pairs={{0,16},{8,120},{16,32},{24,8},{32,48},{40,24},{48,64},{56,40},{64,... | collective-permute-start | bytes 2064392 | tf_op jit(solution)/shard_map/ppermute | solution.py:37
  61.1 21.0 %collective-permute-start.7 = (bf16[4,224,384]{2,1,0:T(8,128)(2,1)}, bf16[4,224,384]{2,1,0:T(8,128)(2,1)S(1)}, u32[]{:S(2)}, u32[]{:S(2)}) collective-permute-start(bf16[4,224,384]{2,1,0:T(8,128)(2,1)} %collective-permute-done.1), channel_id=1, source_target_pairs={{0,8},{8,0},{1,9},{9,1},{2,10},{10,2},{3,11},{11,3},{4,12},{12,4},... | collective-permute-start | bytes 2064392 | tf_op jit(solution)/shard_map/ppermute | solution.py:41
  67.3 14.8 %collective-permute-start.8 = (bf16[4,224,384]{2,1,0:T(8,128)(2,1)S(1)}, bf16[4,224,384]{2,1,0:T(8,128)(2,1)S(1)}, u32[]{:S(2)}, u32[]{:S(2)}) collective-permute-start(bf16[4,224,384]{2,1,0:T(8,128)(2,1)S(1)} %collective-permute-done.5), channel_id=1, source_target_pairs={{0,8},{8,0},{1,9},{9,1},{2,10},{10,2},{3,11},{11,3},{4,12},{12,4},... | collective-permute-start | bytes 2064392 | tf_op jit(solution)/shard_map/ppermute | solution.py:41
  74.7 7.5 %copy-start.4 = (bf16[4,224,384]{2,1,0:T(8,128)(2,1)}, bf16[4,224,384]{2,1,0:T(8,128)(2,1)S(1)}, u32[]{:S(2)}) copy-start(bf16[4,224,384]{2,1,0:T(8,128)(2,1)S(1)} %collective-permute-done.3.refs_6_) | copy-start | bytes 2064388
  74.7 18.0 %collective-permute-start.4 = (bf16[4,224,384]{2,1,0:T(8,128)(2,1)S(1)}, bf16[4,224,384]{2,1,0:T(8,128)(2,1)S(1)}, u32[]{:S(2)}, u32[]{:S(2)}) collective-permute-start(bf16[4,224,384]{2,1,0:T(8,128)(2,1)S(1)} %collective-permute-done.3.refs_6_), channel_id=1, source_target_pairs={{0,16},{8,120},{16,32},{24,8},{32,48},{40,24},{48,64},{56,40},{64,... | collective-permute-start | bytes 2064392 | tf_op jit(solution)/shard_map/ppermute | solution.py:37
  79.6 15.2 %collective-permute-start.6 = (bf16[4,224,384]{2,1,0:T(8,128)(2,1)S(1)}, bf16[4,224,384]{2,1,0:T(8,128)(2,1)}, u32[]{:S(2)}, u32[]{:S(2)}) collective-permute-start(bf16[4,224,384]{2,1,0:T(8,128)(2,1)S(1)} %collective-permute-done.5), channel_id=1, source_target_pairs={{0,16},{8,120},{16,32},{24,8},{32,48},{40,24},{48,64},{56,40},{64,... | collective-permute-start | bytes 2064392 | tf_op jit(solution)/shard_map/ppermute | solution.py:37
  82.1 0.9 copy-start.5
  82.1 1.1 copy-start.6
  92.6 19.5 %copy-start.1 = (bf16[4,224,384]{2,1,0:T(8,128)(2,1)}, bf16[4,224,384]{2,1,0:T(8,128)(2,1)S(1)}, u32[]{:S(2)}) copy-start(bf16[4,224,384]{2,1,0:T(8,128)(2,1)S(1)} %collective-permute-done.4.refs_7_) | copy-start | bytes 2064388
  94.8 8.6 %collective-permute-start.9 = (bf16[4,224,384]{2,1,0:T(8,128)(2,1)}, bf16[4,224,384]{2,1,0:T(8,128)(2,1)S(1)}, u32[]{:S(2)}, u32[]{:S(2)}) collective-permute-start(bf16[4,224,384]{2,1,0:T(8,128)(2,1)} %collective-permute-done.6), channel_id=1, source_target_pairs={{0,8},{8,0},{1,9},{9,1},{2,10},{10,2},{3,11},{11,3},{4,12},{12,4},... | collective-permute-start | bytes 2064392 | tf_op jit(solution)/shard_map/ppermute | solution.py:41
  100.2 12.0 %collective-permute-start.10 = (bf16[4,224,384]{2,1,0:T(8,128)(2,1)S(1)}, bf16[4,224,384]{2,1,0:T(8,128)(2,1)S(1)}, u32[]{:S(2)}, u32[]{:S(2)}) collective-permute-start(bf16[4,224,384]{2,1,0:T(8,128)(2,1)S(1)} %collective-permute-done.4.refs_7_), channel_id=1, source_target_pairs={{0,16},{8,120},{16,32},{24,8},{32,48},{40,24},{48,64},{56,40},{64,... | collective-permute-start | bytes 2064392 | tf_op jit(solution)/shard_map/ppermute | solution.py:37
  103.4 8.7 %copy-start.2 = (bf16[4,224,384]{2,1,0:T(8,128)(2,1)}, bf16[4,224,384]{2,1,0:T(8,128)(2,1)S(1)}, u32[]{:S(2)}) copy-start(bf16[4,224,384]{2,1,0:T(8,128)(2,1)S(1)} %collective-permute-done.9.refs_8_) | copy-start | bytes 2064388
  112.1 0.9 copy-start.3
  146.7 6.0 %collective-permute-start.11 = (bf16[320,2048]{1,0:T(8,128)(2,1)}, bf16[320,2048]{1,0:T(8,128)(2,1)S(1)}, u32[]{:S(2)}, u32[]{:S(2)}) collective-permute-start(bf16[320,2048]{1,0:T(8,128)(2,1)} %get-tuple-element.49), channel_id=1, source_target_pairs={{0,8},{8,0},{1,9},{9,1},{2,10},{10,2},{3,11},{11,3},{4,12},{12,4},... | collective-permute-start | bytes 3932168 | tf_op jit(solution)/shard_map/ppermute | solution.py:41
Sparse Core Ops, SparseCore 0:
  10.1 57.0 all-gather.3
  155.8 33.2 reduce-scatter.1

commit v7 on v6

--- a/solution.py
+++ b/solution.py
@@ -247,9 +247,9 @@
     )(where, rows, normed, student, teacher, scale, weights, *blocks)
 
 
-def grad_kernel(which_ref, student_hbm, teacher_hbm, lse_ref, weights_hbm, *refs):
-    other_hbm, mine_hbm, grad_hbm = refs[:3]
-    student, teacher, weights, grad_t, turned, other, mine, sems, out_sems = refs[3:]
+def grad_kernel(which_ref, student_hbm, teacher_hbm, lse_ref, weights_hbm, normed_hbm, *refs):
+    other_hbm, mine_hbm, head_hbm = refs[:3]
+    student, teacher, weights, normed, grad_t, turned, other, mine, head, sems, out_sems = refs[3:]
     copies = begin(
         [
             pltpu.make_async_copy(source, held, sems.at[k])
@@ -258,6 +258,7 @@
                     (student_hbm, student),
                     (teacher_hbm, teacher),
                     (weights_hbm, weights),
+                    (normed_hbm, normed),
                 ]
             )
         ]
@@ -272,7 +273,6 @@
     grad = live * (jnp.exp(student[...] - lse[1:2]) - jnp.exp(teacher[...] - lse[0:1]))
     grad_t[...] = grad.astype(BF16)
     turned[...] = grad_t[...].T
-    out_copies = begin([pltpu.make_async_copy(grad_t, grad_hbm, out_sems.at[2])])
     half = tokens // NC
     core = which_ref[0]
     parts = [
@@ -282,15 +282,21 @@
     width = weights.shape[0] // NX
     slices = [pl.ds(k * width, width) for k in range(NX)]
     copies[2].wait()
+    out_copies = []
     for i, (out, hbm, block) in enumerate(parts):
         for columns in slices:
             out[:, columns] = against(block, weights[columns, :], ((1,), (1,))).astype(BF16)
         out_copies.append(pltpu.make_async_copy(out, hbm, out_sems.at[i]))
         out_copies[-1].start()
+    copies[3].wait()
+    for k, rows in enumerate(slices):
+        head[rows, :] = against(normed[rows, :], grad_t[...], ((1,), (1,))).astype(BF16)
+        out_copies.append(pltpu.make_async_copy(head.at[rows], head_hbm.at[rows], out_sems.at[2 + k]))
+        out_copies[-1].start()
     finish(out_copies)
 
 
-def gradient(which, student, teacher, lse, weights):
+def gradient(which, student, teacher, lse, weights, normed):
     vocab, tokens = student.shape
     features = weights.shape[0]
     half = tokens // NC
@@ -299,68 +305,30 @@
         out_shape=(
             jax.ShapeDtypeStruct((half, features), BF16),
             jax.ShapeDtypeStruct((half, features), BF16),
-            jax.ShapeDtypeStruct((vocab, tokens), BF16),
-        ),
-        in_specs=[SMEM, HBM, HBM, VMEM, HBM],
+            jax.ShapeDtypeStruct((features, vocab), BF16),
+        ),
+        in_specs=[SMEM, HBM, HBM, VMEM, HBM, HBM],
         out_specs=(HBM, HBM, HBM),
         scratch_shapes=[
             pltpu.VMEM((vocab, tokens), F32),
             pltpu.VMEM((vocab, tokens), F32),
             pltpu.VMEM((features, vocab), BF16),
+            pltpu.VMEM((features, tokens), BF16),
             pltpu.VMEM((vocab, tokens), BF16),
             pltpu.VMEM((tokens, vocab), BF16),
             pltpu.VMEM((half, features), BF16),
             pltpu.VMEM((half, features), BF16),
-            pltpu.SemaphoreType.DMA((3,)),
-            pltpu.SemaphoreType.DMA((3,)),
+            pltpu.VMEM((features, vocab), BF16),
+            pltpu.SemaphoreType.DMA((4,)),
+            pltpu.SemaphoreType.DMA((2 + NX,)),
         ],
         compiler_params=pltpu.CompilerParams(vmem_limit_bytes=GRANT),
         cost_estimate=pl.CostEstimate(
-            flops=2 * vocab * tokens * features,
+            flops=4 * vocab * tokens * features,
             bytes_accessed=10 << 20,
             transcendentals=2 * vocab * tokens,
         ),
-    )(which, student, teacher, lse, weights)
-
-
-def head_kernel(normed_hbm, grad_hbm, out_hbm, normed, grad, out, sems, out_sems):
-    width = normed.shape[0] // NX
-    slices = [pl.ds(k * width, width) for k in range(NX)]
-    copies = [pltpu.make_async_copy(grad_hbm, grad, sems.at[NX])]
-    copies += [
-        pltpu.make_async_copy(normed_hbm.at[rows], normed.at[rows], sems.at[k])
-        for k, rows in enumerate(slices)
-    ]
-    begin(copies)
-    copies[0].wait()
-    out_copies = []
-    for k, rows in enumerate(slices):
-        copies[1 + k].wait()
-        out[rows, :] = against(normed[rows, :], grad[...], ((1,), (1,))).astype(BF16)
-        out_copies.append(pltpu.make_async_copy(out.at[rows], out_hbm.at[rows], out_sems.at[k]))
-        out_copies[-1].start()
-    finish(out_copies)
-
-
-def head_product(normed, grad):
-    features, vocab = normed.shape[0], grad.shape[0]
-    return pl.pallas_call(
-        head_kernel,
-        out_shape=jax.ShapeDtypeStruct((features, vocab), BF16),
-        in_specs=[HBM, HBM],
-        out_specs=HBM,
-        scratch_shapes=[
-            pltpu.VMEM(normed.shape, BF16),
-            pltpu.VMEM(grad.shape, BF16),
-            pltpu.VMEM((features, vocab), BF16),
-            pltpu.SemaphoreType.DMA((1 + NX,)),
-            pltpu.SemaphoreType.DMA((NX,)),
-        ],
-        compiler_params=pltpu.CompilerParams(vmem_limit_bytes=GRANT),
-        cost_estimate=pl.CostEstimate(
-            flops=2 * vocab * normed.size, bytes_accessed=5 << 20, transcendentals=0
-        ),
-    )(normed, grad)
+    )(which, student, teacher, lse, weights, normed)
 
 
 def squares_kernel(parts_ref, row_ref, head_ref, out_ref):
@@ -399,29 +367,29 @@
     sent = jnp.concatenate([scaled, jnp.pad(squares, ((0, HEAD_ROWS - 3), (0, 0)))], axis=0)
     rows = lax.all_gather(sent, ("core", "y"), axis=0, tiled=False)
 
-    normed = normalize(student_rows, student_gain).T
     heads = jnp.concatenate([student_head.T, teacher_head.T], axis=0)
     own = lax.all_gather(heads, "x", axis=0, tiled=False)
     blocks, offsets = [own], [0]
     mine, theirs = own, swapped(own)
     for step in range(1, NZ // 2):
         mine, theirs = along(mine), along(theirs)
-        if step == 1:
-            theirs, normed = lax.optimization_barrier((theirs, normed))
         if step < NZ // 2 - 1:
             blocks += [mine, swapped(theirs)]
             offsets += [-step, step]
 
+    normed = normalize(student_rows, student_gain).T
     early = len(blocks)
+    blocks += [mine, along(mine)]
+    offsets += [1 - NZ // 2, -NZ // 2]
     where = jnp.stack([z, 1 - 2 * c])
     student_logits, teacher_logits, scale, weights = most(
         where, rows, normed, blocks[:early], offsets[:early], wide, fs
     )
-    mine, theirs, student_logits, teacher_logits, scale, weights = lax.optimization_barrier(
-        (mine, theirs, student_logits, teacher_logits, scale, weights)
-    )
-    blocks += [mine, swapped(theirs), along(mine)]
-    offsets += [1 - NZ // 2, NZ // 2 - 1, -NZ // 2]
+    theirs, student_logits, teacher_logits, scale, weights = lax.optimization_barrier(
+        (theirs, student_logits, teacher_logits, scale, weights)
+    )
+    blocks.append(swapped(theirs))
+    offsets.append(NZ // 2 - 1)
     student_logits, teacher_logits, lse, weights = last(
         where,
         rows,
@@ -439,10 +407,11 @@
     which = jnp.stack([c, lengths[0]])
     lse, which, normed = lax.optimization_barrier((lse, which, normed))
     lse = lax.all_to_all(lse, ("core", "y"), 0, 0, tiled=True)
-    other, mine, logit_grad = gradient(which, student_logits, teacher_logits, lse, student_w)
+    other, mine, head_part = gradient(
+        which, student_logits, teacher_logits, lse, student_w, normed
+    )
+
     other = swapped(other)
-    head_part = head_product(normed, logit_grad)
-
     mine = (mine.astype(F32) + other.astype(F32)).astype(BF16)
     row_grad = lax.psum_scatter(mine, "y", scatter_dimension=0, tiled=True)
 

time: 244 us -> 221 us (0.906)
  waiting for transfers between devices: 29.2 us -> 12.1 us
  Pallas kernels: 31.5 us -> 28.5 us
  blocking collectives: 103 us -> 100 us
    ppermute x7, waiting for transfers between devices: 26.4 us -> 8.53 us  [along(): return lax.ppermute(values, ('z', 'core'), pairs)]
    ppermute x7, starting transfers between devices: 23 us -> 27.6 us  [along(): return lax.ppermute(values, ('z', 'core'), pairs)]
    pallas_call x1 -> x0, Pallas kernels: 4.44 us -> none  [head_product(): pl.pallas_call(head_kernel, out_shape=jax.ShapeDtypeStruct((features, voc...]
    ppermute x5, starting transfers between devices: 25.1 us -> 21.4 us  [swapped(): return lax.ppermute(values, 'core', [(0, 1), (1, 0)])]
    unnamed x17 -> x13, local copies, waits for them, and re-layouts: 5.08 us -> 4.25 us
  transfers between devices with their start and end apart: 14 -> 14, of which waited for: 6 -> 5; matrix products, arithmetic and copies ran while one was open for 4% -> 4% of each run, Pallas kernels for 6% -> 4%
where the time goes in v7:
time: 221 us; the launch traced here: 220 us
  blocking collectives  100 us (45%)
  starting transfers between devices  49.1 us (22%)
  Pallas kernels  28.5 us (13%)
  between operations  15 us (7%)
  waiting for transfers between devices  12.1 us (5%)
  other arithmetic  11.1 us (5%)
  local copies, waits for them, and re-layouts  4.26 us (2%)
    all_to_all x1, blocking collectives, body(): squares = lax.all_to_all(squares, ('x', 'z', 'core', 'y'), 0, 0, tiled=True)  31.4 us
    ppermute x7, starting transfers between devices, along(): return lax.ppermute(values, ('z', 'core'), pairs)  27.6 us
    all_to_all x1, blocking collectives, body(): lax.all_to_all(head_part.reshape(NX, NZ * fs, vocab), 'x', 0, 0, tiled=True)  23.8 us
    ppermute x5, starting transfers between devices, swapped(): return lax.ppermute(values, 'core', [(0, 1), (1, 0)])  21.4 us
    all_to_all x1, blocking collectives, body(): lse = lax.all_to_all(lse, ('core', 'y'), 0, 0, tiled=True)  18.1 us
    all_to_all x1, blocking collectives, body(): lax.all_to_all(head_part.reshape(NZ, fs, vocab), 'z', 0, 0, tiled=True)  15.8 us
    all_gather x1, blocking collectives, body(): own = lax.all_gather(heads, 'x', axis=0, tiled=False)  11.4 us
    pallas_call x1, Pallas kernels, most(): pl.pallas_call(kernel, out_shape=(jax.ShapeDtypeStruct((vocab, tokens), F...  9.46 us
  transfers between devices with their start and end apart: 14, of which 5 were waited for; matrix products, arithmetic and copies ran while one was open for 4% of the time, Pallas kernels for 4%

profile of v7, /device:TPU:1, one launch (start us, length us, event | category | flops | bytes accessed | tf_op | source)
XLA Modules:
  0.0 220.4 jit_solution(4527397064100831056)
XLA Ops:
  7.2 0.0 copy-start.5
  7.2 0.0 all-gather.4.cloned.1.call-start
  7.2 0.7 convert_element_type.102
  7.9 1.1 fusion.6
  9.1 0.8 pad_maximum_fusion
  9.9 0.0 all-gather.4.cloned.1.call-update
  9.9 0.0 reduce-scatter.2.cloned.1.call-start
  10.0 0.9 pad_maximum_fusion.1
  10.9 11.4 %all-gather.1 = bf16[896,384]{1,0:T(8,128)(2,1)S(1)} all-gather(bf16[224,384]{1,0:T(8,128)(2,1)S(1)} %pad_maximum_fusion.1), channel_id=3, replica_groups=mesh['x'=4,'z'=8,'core'=2,'y'=8] {'x'}, dimensions={0}, use_global_device_ids=true | all-gather | bytes 860160 | tf_op jit(solution)/shard_map/all_gather | solution.py:371
  22.3 0.0 copy-start
  22.3 10.5 %collective-permute-start = (bf16[4,224,384]{2,1,0:T(8,128)(2,1)S(1)}, bf16[4,224,384]{2,1,0:T(8,128)(2,1)S(1)}, u32[]{:S(2)}, u32[]{:S(2)}) collective-permute-start(bf16[4,224,384]{2,1,0:T(8,128)(2,1)S(1)} %bitcast.21), channel_id=1, source_target_pairs={{0,8},{8,0},{1,9},{9,1},{2,10},{10,2},{3,11},{11,3},{4,12},{12,4},... | collective-permute-start | bytes 2064392 | tf_op jit(solution)/shard_map/ppermute | solution.py:41
  32.8 5.6 %collective-permute-start.4 = (bf16[4,224,384]{2,1,0:T(8,128)(2,1)S(1)}, bf16[4,224,384]{2,1,0:T(8,128)(2,1)}, u32[]{:S(2)}, u32[]{:S(2)}) collective-permute-start(bf16[4,224,384]{2,1,0:T(8,128)(2,1)S(1)} %bitcast.22), channel_id=1, source_target_pairs={{0,16},{8,120},{16,32},{24,8},{32,48},{40,24},{48,64},{56,40},{64,... | collective-permute-start | bytes 2064392 | tf_op jit(solution)/shard_map/ppermute | solution.py:37
  38.5 0.0 collective-permute-done
  38.5 2.2 collective-permute-start.1
  40.7 5.7 %collective-permute-done.4.refs_4_ = bf16[4,224,384]{2,1,0:T(8,128)(2,1)} collective-permute-done((bf16[4,224,384]{2,1,0:T(8,128)(2,1)S(1)}, bf16[4,224,384]{2,1,0:T(8,128)(2,1)}, u32[]{:S(2)}, u32[]{:S(2)}) %collective-permute-start.4) | collective-permute-done | bytes 688160 | tf_op jit(solution)/shard_map/ppermute | solution.py:37
  46.3 5.4 %collective-permute-start.6 = (bf16[4,224,384]{2,1,0:T(8,128)(2,1)}, bf16[4,224,384]{2,1,0:T(8,128)(2,1)}, u32[]{:S(2)}, u32[]{:S(2)}) collective-permute-start(bf16[4,224,384]{2,1,0:T(8,128)(2,1)} %collective-permute-done.4.refs_4_), channel_id=1, source_target_pairs={{0,16},{8,120},{16,32},{24,8},{32,48},{40,24},{48,64},{56,40},{64,... | collective-permute-start | bytes 2064392 | tf_op jit(solution)/shard_map/ppermute | solution.py:37
  51.8 2.0 collective-permute-done.1
  53.7 5.4 %collective-permute-start.2 = (bf16[4,224,384]{2,1,0:T(8,128)(2,1)}, bf16[4,224,384]{2,1,0:T(8,128)(2,1)}, u32[]{:S(2)}, u32[]{:S(2)}) collective-permute-start(bf16[4,224,384]{2,1,0:T(8,128)(2,1)} %collective-permute-done.1), channel_id=1, source_target_pairs={{0,16},{8,120},{16,32},{24,8},{32,48},{40,24},{48,64},{56,40},{64,... | collective-permute-start | bytes 2064392 | tf_op jit(solution)/shard_map/ppermute | solution.py:37
  59.1 0.0 copy-done.5
  59.1 3.2 %copy.11 = bf16[640,2048]{0,1:T(8,128)(2,1)S(1)} copy(bf16[640,2048]{1,0:T(8,128)(2,1)} %param.10) | data formatting | bytes 5242880 | tf_op args[3]
  62.3 0.0 copy-done
  62.4 0.6 fusion
  63.0 1.9 collective-permute-start.5
  64.9 0.0 collective-permute-done.6.refs_6_
  64.9 2.7 %collective-permute-start.8 = (bf16[4,224,384]{2,1,0:T(8,128)(2,1)}, bf16[4,224,384]{2,1,0:T(8,128)(2,1)S(1)}, u32[]{:S(2)}, u32[]{:S(2)}) collective-permute-start(bf16[4,224,384]{2,1,0:T(8,128)(2,1)} %collective-permute-done.6.refs_6_), channel_id=1, source_target_pairs={{0,16},{8,120},{16,32},{24,8},{32,48},{40,24},{48,64},{56,40},{64,... | collective-permute-start | bytes 2064392 | tf_op jit(solution)/shard_map/ppermute | solution.py:37
  67.6 0.9 collective-permute-done.2
  68.6 3.2 %collective-permute-start.7 = (bf16[4,224,384]{2,1,0:T(8,128)(2,1)}, bf16[4,224,384]{2,1,0:T(8,128)(2,1)}, u32[]{:S(2)}, u32[]{:S(2)}) collective-permute-start(bf16[4,224,384]{2,1,0:T(8,128)(2,1)} %collective-permute-done.2), channel_id=1, source_target_pairs={{0,8},{8,0},{1,9},{9,1},{2,10},{10,2},{3,11},{11,3},{4,12},{12,4},... | collective-permute-start | bytes 2064392 | tf_op jit(solution)/shard_map/ppermute | solution.py:41
  71.8 0.7 pad_add_fusion.refs_0_
  72.5 3.7 %collective-permute-start.3 = (bf16[4,224,384]{2,1,0:T(8,128)(2,1)}, bf16[4,224,384]{2,1,0:T(8,128)(2,1)}, u32[]{:S(2)}, u32[]{:S(2)}) collective-permute-start(bf16[4,224,384]{2,1,0:T(8,128)(2,1)} %collective-permute-done.2), channel_id=1, source_target_pairs={{0,16},{8,120},{16,32},{24,8},{32,48},{40,24},{48,64},{56,40},{64,... | collective-permute-start | bytes 2064392 | tf_op jit(solution)/shard_map/ppermute | solution.py:37
  76.2 2.2 fusion.3.refs_2_.normed_hbm
  78.3 0.0 collective-permute-done.8.refs_7_
  78.3 0.0 copy-start.2
  78.3 2.5 %collective-permute-start.9 = (bf16[4,224,384]{2,1,0:T(8,128)(2,1)S(1)}, bf16[4,224,384]{2,1,0:T(8,128)(2,1)S(1)}, u32[]{:S(2)}, u32[]{:S(2)}) collective-permute-start(bf16[4,224,384]{2,1,0:T(8,128)(2,1)S(1)} %collective-permute-done.8.refs_7_), channel_id=1, source_target_pairs={{0,16},{8,120},{16,32},{24,8},{32,48},{40,24},{48,64},{56,40},{64,... | collective-permute-start | bytes 2064392 | tf_op jit(solution)/shard_map/ppermute | solution.py:37
  80.8 0.0 collective-permute-done.5.refs_5_
  80.9 0.0 collective-permute-done.7.refs_7_
  80.9 0.0 all-gather.4.cloned.1.call-done
  80.9 9.5 %shard_map.86 = (f32[384,640]{1,0:T(8,128)}, f32[384,640]{1,0:T(8,128)}, f32[1,640]{1,0:T(1,128)}, bf16[4,8,64,384]{3,2,1,0:T(8,128)(2,1)}) custom-call(s32[2]{0:T(128)} %pad_add_fusion.refs_0_, bf16[16,336,640]{2,1,0:T(8,128)(2,1)} %bitcast.19, bf16[2048,640]{1,0:T(8,128)(2,1)} %fusion.3.refs_2_.normed_hbm, bf16[4,224,384]{2,1,0:T(8,128)(2,1)} %bitcast.23, ...), custom_call_target="tpu_custom_call" | custom-call | flops 2202009600 | bytes 12582912 | tf_op jit(solution)/shard_map/pallas_call | solution.py:172
  90.4 0.0 copy-done.2
  90.4 0.0 collective-permute-done.3
  90.4 2.6 %collective-permute-start.10 = (bf16[4,224,384]{2,1,0:T(8,128)(2,1)}, bf16[4,224,384]{2,1,0:T(8,128)(2,1)S(1)}, u32[]{:S(2)}, u32[]{:S(2)}) collective-permute-start(bf16[4,224,384]{2,1,0:T(8,128)(2,1)} %collective-permute-done.3), channel_id=1, source_target_pairs={{0,8},{8,0},{1,9},{9,1},{2,10},{10,2},{3,11},{11,3},{4,12},{12,4},... | collective-permute-start | bytes 2064392 | tf_op jit(solution)/shard_map/ppermute | solution.py:41
  93.7 0.6 pad_add_fusion.1.which_ref
  94.3 0.0 collective-permute-done.9.refs_8_
  94.3 0.0 copy-start.3
  94.3 0.7 collective-permute-done.10.refs_9_
  95.0 0.2 copy-done.3
  95.2 0.0 copy-start.4
  95.2 0.9 copy-done.4
  96.0 8.0 %shard_map.87 = (f32[384,640]{1,0:T(8,128)}, f32[384,640]{1,0:T(8,128)}, f32[16,8,640]{2,1,0:T(8,128)}, bf16[4,8,64,384]{3,2,1,0:T(8,128)(2,1)}) custom-call(s32[2]{0:T(128)} %pad_add_fusion.refs_0_, bf16[16,336,640]{2,1,0:T(8,128)(2,1)} %bitcast.20, bf16[2048,640]{1,0:T(8,128)(2,1)} %fusion.3.refs_2_.normed_hbm, ...), custom_call_target="tpu_custom_call", output_to_operand_aliasing={{3}: (6, {})} | custom-call | flops 1321205760 | bytes 8388608 | tf_op jit(solution)/shard_map/pallas_call | solution.py:229
  104.1 18.1 %all_to_all.26.lse_ref = f32[16,8,640]{2,1,0:T(8,128)} all-to-all(f32[16,8,640]{2,1,0:T(8,128)} %get-tuple-element.38), channel_id=1, replica_groups=mesh['x'=4,'z'=8,'core'=2,'y'=8] {'core','y'}, dimensions={0} | all-to-all | bytes 655360 | tf_op jit(solution)/shard_map/all_to_all | solution.py:409
  122.1 7.1 %shard_map.88 = (bf16[320,2048]{1,0:T(8,128)(2,1)}, bf16[320,2048]{1,0:T(8,128)(2,1)}, bf16[2048,384]{1,0:T(8,128)(2,1)}) custom-call(s32[2]{0:T(128)} %pad_add_fusion.1.which_ref, f32[384,640]{1,0:T(8,128)} %get-tuple-element.36.student_hbm, f32[384,640]{1,0:T(8,128)} %get-tuple-element.37.teacher_hbm, f32[16,8,640]{2,1,0:T(8,128)} %all_to_all.26.lse_ref, ...), custom_call_target="tpu_custom_call" | custom-call | flops 2013265920 | bytes 10485760 | tf_op jit(solution)/shard_map/pallas_call | solution.py:303
  129.2 3.1 %collective-permute-start.11 = (bf16[320,2048]{1,0:T(8,128)(2,1)}, bf16[320,2048]{1,0:T(8,128)(2,1)S(1)}, u32[]{:S(2)}, u32[]{:S(2)}) collective-permute-start(bf16[320,2048]{1,0:T(8,128)(2,1)} %get-tuple-element.43), channel_id=1, source_target_pairs={{0,8},{8,0},{1,9},{9,1},{2,10},{10,2},{3,11},{11,3},{4,12},{12,4},... | collective-permute-start | bytes 3932168 | tf_op jit(solution)/shard_map/ppermute | solution.py:41
  132.4 2.9 %collective-permute-done.11 = bf16[320,2048]{1,0:T(8,128)(2,1)S(1)} collective-permute-done((bf16[320,2048]{1,0:T(8,128)(2,1)}, bf16[320,2048]{1,0:T(8,128)(2,1)S(1)}, u32[]{:S(2)}, u32[]{:S(2)}) %collective-permute-start.11) | collective-permute-done | bytes 1310752 | tf_op jit(solution)/shard_map/ppermute | solution.py:41
  135.2 0.0 copy-start.1
  135.2 3.0 %add_convert_fusion = bf16[320,2048]{1,0:T(8,128)(2,1)} fusion(bf16[320,2048]{1,0:T(8,128)(2,1)S(1)} %collective-permute-done.11, bf16[320,2048]{1,0:T(8,128)(2,1)} %get-tuple-element.42), kind=kLoop, calls=%fused_computation.6 | loop fusion | flops 2621440 | bytes 3932160 | tf_op jit(solution)/shard_map/convert_element_type | solution.py:415
  138.2 0.0 reduce-scatter.2.cloned.1.call-update
  138.2 0.0 copy-done.1
  138.3 23.8 %all_to_all.27 = bf16[4,512,384]{2,1,0:T(8,128)(2,1)S(1)} all-to-all(bf16[4,512,384]{2,1,0:T(8,128)(2,1)S(1)} %bitcast.24), channel_id=1, replica_groups=mesh['x'=4,'z'=8,'core'=2,'y'=8] {'x'}, dimensions={0} | all-to-all | bytes 3145728 | tf_op jit(solution)/shard_map/all_to_all | solution.py:418
  162.0 0.4 reduce_sum.35
  162.5 15.8 %all_to_all.28.parts_ref = bf16[8,64,384]{2,1,0:T(8,128)(2,1)} all-to-all(bf16[8,64,384]{2,1,0:T(8,128)(2,1)S(1)} %bitcast.25), channel_id=1, replica_groups=mesh['x'=4,'z'=8,'core'=2,'y'=8] {'z'}, dimensions={0} | all-to-all | bytes 786432 | tf_op jit(solution)/shard_map/all_to_all | solution.py:420
  178.3 0.0 reduce-scatter.2.cloned.1.call-done.row_ref.refs_2_
  178.3 2.0 shard_map.89
  180.3 31.4 %all_to_all.29 = f32[512,1,128]{2,1,0:T(1,128)} all-to-all(f32[512,1,128]{2,1,0:T(1,128)} %bitcast.28), channel_id=1, replica_groups=mesh['x'=4,'z'=8,'core'=2,'y'=8] {'x','z','core','y'}, dimensions={0} | all-to-all | bytes 524288 | tf_op jit(solution)/shard_map/all_to_all | solution.py:430
  211.6 1.9 shard_map.90
  (5 shorter events, 0.0 us)
Async XLA Ops:
  7.2 52.0 %copy-start.5 = (bf16[2048]{0:T(1024)(128)(2,1)S(1)}, bf16[2048]{0:T(1024)(128)(2,1)}, u32[]{:S(2)}) copy-start(bf16[2048]{0:T(1024)(128)(2,1)} %param.11) | copy-start | bytes 12292
  7.2 73.7 %all-gather.4.cloned.1.call-start = ((), (), s32[]{:S(2)}) async-start(), calls=%async_computation.6 | async-start | bytes 7311360 | tf_op jit(solution)/shard_map/all_gather | solution.py:368
  9.9 168.3 %reduce-scatter.2.cloned.1.call-start = ((), (), s32[]{:S(2)}) async-start(), calls=%async_computation.5 | async-start | bytes 1474560 | tf_op jit(solution)/shard_map/reduce_scatter | solution.py:416
  22.3 40.0 %copy-start = (bf16[896,384]{1,0:T(8,128)(2,1)}, bf16[896,384]{1,0:T(8,128)(2,1)S(1)}, u32[]{:S(2)}) copy-start(bf16[896,384]{1,0:T(8,128)(2,1)S(1)} %all-gather.1) | copy-start | bytes 2064388
  22.3 16.1 %collective-permute-start = (bf16[4,224,384]{2,1,0:T(8,128)(2,1)S(1)}, bf16[4,224,384]{2,1,0:T(8,128)(2,1)S(1)}, u32[]{:S(2)}, u32[]{:S(2)}) collective-permute-start(bf16[4,224,384]{2,1,0:T(8,128)(2,1)S(1)} %bitcast.21), channel_id=1, source_target_pairs={{0,8},{8,0},{1,9},{9,1},{2,10},{10,2},{3,11},{11,3},{4,12},{12,4},... | collective-permute-start | bytes 2064392 | tf_op jit(solution)/shard_map/ppermute | solution.py:41
  32.8 13.5 %collective-permute-start.4 = (bf16[4,224,384]{2,1,0:T(8,128)(2,1)S(1)}, bf16[4,224,384]{2,1,0:T(8,128)(2,1)}, u32[]{:S(2)}, u32[]{:S(2)}) collective-permute-start(bf16[4,224,384]{2,1,0:T(8,128)(2,1)S(1)} %bitcast.22), channel_id=1, source_target_pairs={{0,16},{8,120},{16,32},{24,8},{32,48},{40,24},{48,64},{56,40},{64,... | collective-permute-start | bytes 2064392 | tf_op jit(solution)/shard_map/ppermute | solution.py:37
  38.5 15.2 %collective-permute-start.1 = (bf16[4,224,384]{2,1,0:T(8,128)(2,1)S(1)}, bf16[4,224,384]{2,1,0:T(8,128)(2,1)}, u32[]{:S(2)}, u32[]{:S(2)}) collective-permute-start(bf16[4,224,384]{2,1,0:T(8,128)(2,1)S(1)} %collective-permute-done), channel_id=1, source_target_pairs={{0,16},{8,120},{16,32},{24,8},{32,48},{40,24},{48,64},{56,40},{64,... | collective-permute-start | bytes 2064392 | tf_op jit(solution)/shard_map/ppermute | solution.py:37
  46.3 18.6 %collective-permute-start.6 = (bf16[4,224,384]{2,1,0:T(8,128)(2,1)}, bf16[4,224,384]{2,1,0:T(8,128)(2,1)}, u32[]{:S(2)}, u32[]{:S(2)}) collective-permute-start(bf16[4,224,384]{2,1,0:T(8,128)(2,1)} %collective-permute-done.4.refs_4_), channel_id=1, source_target_pairs={{0,16},{8,120},{16,32},{24,8},{32,48},{40,24},{48,64},{56,40},{64,... | collective-permute-start | bytes 2064392 | tf_op jit(solution)/shard_map/ppermute | solution.py:37
  53.7 14.9 %collective-permute-start.2 = (bf16[4,224,384]{2,1,0:T(8,128)(2,1)}, bf16[4,224,384]{2,1,0:T(8,128)(2,1)}, u32[]{:S(2)}, u32[]{:S(2)}) collective-permute-start(bf16[4,224,384]{2,1,0:T(8,128)(2,1)} %collective-permute-done.1), channel_id=1, source_target_pairs={{0,16},{8,120},{16,32},{24,8},{32,48},{40,24},{48,64},{56,40},{64,... | collective-permute-start | bytes 2064392 | tf_op jit(solution)/shard_map/ppermute | solution.py:37
  63.0 17.9 %collective-permute-start.5 = (bf16[4,224,384]{2,1,0:T(8,128)(2,1)}, bf16[4,224,384]{2,1,0:T(8,128)(2,1)}, u32[]{:S(2)}, u32[]{:S(2)}) collective-permute-start(bf16[4,224,384]{2,1,0:T(8,128)(2,1)} %collective-permute-done.1), channel_id=1, source_target_pairs={{0,8},{8,0},{1,9},{9,1},{2,10},{10,2},{3,11},{11,3},{4,12},{12,4},... | collective-permute-start | bytes 2064392 | tf_op jit(solution)/shard_map/ppermute | solution.py:41
  64.9 13.4 %collective-permute-start.8 = (bf16[4,224,384]{2,1,0:T(8,128)(2,1)}, bf16[4,224,384]{2,1,0:T(8,128)(2,1)S(1)}, u32[]{:S(2)}, u32[]{:S(2)}) collective-permute-start(bf16[4,224,384]{2,1,0:T(8,128)(2,1)} %collective-permute-done.6.refs_6_), channel_id=1, source_target_pairs={{0,16},{8,120},{16,32},{24,8},{32,48},{40,24},{48,64},{56,40},{64,... | collective-permute-start | bytes 2064392 | tf_op jit(solution)/shard_map/ppermute | solution.py:37
  68.6 12.3 %collective-permute-start.7 = (bf16[4,224,384]{2,1,0:T(8,128)(2,1)}, bf16[4,224,384]{2,1,0:T(8,128)(2,1)}, u32[]{:S(2)}, u32[]{:S(2)}) collective-permute-start(bf16[4,224,384]{2,1,0:T(8,128)(2,1)} %collective-permute-done.2), channel_id=1, source_target_pairs={{0,8},{8,0},{1,9},{9,1},{2,10},{10,2},{3,11},{11,3},{4,12},{12,4},... | collective-permute-start | bytes 2064392 | tf_op jit(solution)/shard_map/ppermute | solution.py:41
  72.5 17.9 %collective-permute-start.3 = (bf16[4,224,384]{2,1,0:T(8,128)(2,1)}, bf16[4,224,384]{2,1,0:T(8,128)(2,1)}, u32[]{:S(2)}, u32[]{:S(2)}) collective-permute-start(bf16[4,224,384]{2,1,0:T(8,128)(2,1)} %collective-permute-done.2), channel_id=1, source_target_pairs={{0,16},{8,120},{16,32},{24,8},{32,48},{40,24},{48,64},{56,40},{64,... | collective-permute-start | bytes 2064392 | tf_op jit(solution)/shard_map/ppermute | solution.py:37
  78.3 12.0 %copy-start.2 = (bf16[4,224,384]{2,1,0:T(8,128)(2,1)}, bf16[4,224,384]{2,1,0:T(8,128)(2,1)S(1)}, u32[]{:S(2)}) copy-start(bf16[4,224,384]{2,1,0:T(8,128)(2,1)S(1)} %collective-permute-done.8.refs_7_) | copy-start | bytes 2064388
  78.3 16.0 %collective-permute-start.9 = (bf16[4,224,384]{2,1,0:T(8,128)(2,1)S(1)}, bf16[4,224,384]{2,1,0:T(8,128)(2,1)S(1)}, u32[]{:S(2)}, u32[]{:S(2)}) collective-permute-start(bf16[4,224,384]{2,1,0:T(8,128)(2,1)S(1)} %collective-permute-done.8.refs_7_), channel_id=1, source_target_pairs={{0,16},{8,120},{16,32},{24,8},{32,48},{40,24},{48,64},{56,40},{64,... | collective-permute-start | bytes 2064392 | tf_op jit(solution)/shard_map/ppermute | solution.py:37
  90.4 4.6 %collective-permute-start.10 = (bf16[4,224,384]{2,1,0:T(8,128)(2,1)}, bf16[4,224,384]{2,1,0:T(8,128)(2,1)S(1)}, u32[]{:S(2)}, u32[]{:S(2)}) collective-permute-start(bf16[4,224,384]{2,1,0:T(8,128)(2,1)} %collective-permute-done.3), channel_id=1, source_target_pairs={{0,8},{8,0},{1,9},{9,1},{2,10},{10,2},{3,11},{11,3},{4,12},{12,4},... | collective-permute-start | bytes 2064392 | tf_op jit(solution)/shard_map/ppermute | solution.py:41
  94.3 0.9 copy-start.3
  95.2 0.9 copy-start.4
  129.2 6.0 %collective-permute-start.11 = (bf16[320,2048]{1,0:T(8,128)(2,1)}, bf16[320,2048]{1,0:T(8,128)(2,1)S(1)}, u32[]{:S(2)}, u32[]{:S(2)}) collective-permute-start(bf16[320,2048]{1,0:T(8,128)(2,1)} %get-tuple-element.43), channel_id=1, source_target_pairs={{0,8},{8,0},{1,9},{9,1},{2,10},{10,2},{3,11},{11,3},{4,12},{12,4},... | collective-permute-start | bytes 3932168 | tf_op jit(solution)/shard_map/ppermute | solution.py:41
  135.2 3.0 %copy-start.1 = (bf16[2048,384]{1,0:T(8,128)(2,1)S(1)}, bf16[2048,384]{1,0:T(8,128)(2,1)}, u32[]{:S(2)}) copy-start(bf16[2048,384]{1,0:T(8,128)(2,1)} %get-tuple-element.41) | copy-start | bytes 4718596
Sparse Core Ops, SparseCore 0:
  10.1 57.2 all-gather.3
  138.4 33.3 reduce-scatter.1

commit v8 on v7

--- a/solution.py
+++ b/solution.py
@@ -11,7 +11,7 @@
 NX, NZ, NC, NY = 4, 8, 2, 8
 epsilon = 1e-06
 HEAD_ROWS = 16
-LSE_ROWS = 8
+LSE_ROWS = 2
 GRANT = 60 << 20
 HBM = pl.BlockSpec(memory_space=pltpu.HBM)
 VMEM = pl.BlockSpec(memory_space=pltpu.VMEM)
@@ -24,6 +24,17 @@
     middle = rest.astype(BF16)
     low = (rest - middle.astype(F32)).astype(BF16)
     return high, middle, low
+
+
+def scaled_kernel(rows_ref, gain_ref, out_ref):
+    values = rows_ref[...].astype(F32)
+    wide = values.shape[0]
+    gain = jnp.broadcast_to(gain_ref[...].astype(F32), (128, wide)).T[:, :1]
+    out_ref[pl.ds(0, wide), :] = (values * gain).astype(BF16)
+    terms = split3(jnp.sum(values * values, axis=0, keepdims=True))
+    rest = jnp.zeros((HEAD_ROWS - len(terms), values.shape[1]), F32)
+    terms = jnp.concatenate([term.astype(F32) for term in terms] + [rest], axis=0)
+    out_ref[pl.ds(wide, HEAD_ROWS), :] = terms.astype(BF16)
 
 
 def normalize(rows, gain):
@@ -331,6 +342,23 @@
     )(which, student, teacher, lse, weights, normed)
 
 
+def added_kernel(left_ref, right_ref, out_ref):
+    out_ref[...] = (left_ref[...].astype(F32) + right_ref[...].astype(F32)).astype(BF16)
+
+
+def added(left, right):
+    rows, columns = left.shape
+    spec = pl.BlockSpec((rows // NX, columns), lambda i: (i, 0))
+    return pl.pallas_call(
+        added_kernel,
+        out_shape=jax.ShapeDtypeStruct(left.shape, BF16),
+        grid=(NX,),
+        in_specs=[spec, spec],
+        out_specs=spec,
+        compiler_params=pltpu.CompilerParams(vmem_limit_bytes=16 << 20),
+    )(left, right)
+
+
 def squares_kernel(parts_ref, row_ref, head_ref, out_ref):
     head = jnp.sum(parts_ref[...].astype(F32), axis=0)
     head_ref[...] = head
@@ -359,12 +387,11 @@
     z = lax.axis_index("z")
     c = lax.axis_index("core")
 
-    block = teacher_rows.T
-    wide = block.shape[0]
-    values = block.astype(F32)
-    scaled = (values * teacher_gain.astype(F32)[:, None]).astype(BF16)
-    squares = jnp.stack(split3(jnp.sum(values * values, axis=0)), axis=0)
-    sent = jnp.concatenate([scaled, jnp.pad(squares, ((0, HEAD_ROWS - 3), (0, 0)))], axis=0)
+    wide = teacher_rows.shape[1]
+    sent = pl.pallas_call(
+        scaled_kernel,
+        out_shape=jax.ShapeDtypeStruct((wide + HEAD_ROWS, teacher_rows.shape[0]), BF16),
+    )(teacher_rows.T, teacher_gain[None])
     rows = lax.all_gather(sent, ("core", "y"), axis=0, tiled=False)
 
     heads = jnp.concatenate([student_head.T, teacher_head.T], axis=0)
@@ -412,7 +439,7 @@
     )
 
     other = swapped(other)
-    mine = (mine.astype(F32) + other.astype(F32)).astype(BF16)
+    mine = added(mine, other)
     row_grad = lax.psum_scatter(mine, "y", scatter_dimension=0, tiled=True)
 
     head_part = lax.all_to_all(head_part.reshape(NX, NZ * fs, vocab), "x", 0, 0, tiled=True)

time: 221 us -> 219 us (level)
  other arithmetic: 11.1 us -> 6.08 us
  Pallas kernels: 28.5 us -> 32.1 us
  blocking collectives: 100 us -> 97.3 us
  local copies, waits for them, and re-layouts: 4.26 us -> 6.73 us
    convert_element_type x4 -> x0, other arithmetic: 4.82 us -> none  [the longest x1 3 us: body(): mine = (mine.astype(F32) + other.astype(F32)).astype(BF16)]
    pallas_call x0 -> x2, Pallas kernels: none -> 3.78 us  [the longest x1 2.01 us: body(): pl.pallas_call(scaled_kernel, out_shape=jax.ShapeDtypeStruct((wide + HEAD...]
    all_to_all x1, blocking collectives: 18.1 us -> 14.8 us  [body(): lse = lax.all_to_all(lse, ('core', 'y'), 0, 0, tiled=True)]
where the time goes in v8:
time: 219 us; the launch traced here: 218 us
  blocking collectives  97.3 us (44%)
  starting transfers between devices  49.5 us (23%)
  Pallas kernels  32.1 us (15%)
  between operations  14.9 us (7%)
  waiting for transfers between devices  11.5 us (5%)
  local copies, waits for them, and re-layouts  6.73 us (3%)
  other arithmetic  6.08 us (3%)
    all_to_all x1, blocking collectives, body(): squares = lax.all_to_all(squares, ('x', 'z', 'core', 'y'), 0, 0, tiled=True)  31.6 us
    ppermute x7, starting transfers between devices, along(): return lax.ppermute(values, ('z', 'core'), pairs)  28.3 us
    all_to_all x1, blocking collectives, body(): lax.all_to_all(head_part.reshape(NX, NZ * fs, vocab), 'x', 0, 0, tiled=True)  23.8 us
    ppermute x5, starting transfers between devices, swapped(): return lax.ppermute(values, 'core', [(0, 1), (1, 0)])  21.2 us
    all_to_all x1, blocking collectives, body(): lax.all_to_all(head_part.reshape(NZ, fs, vocab), 'z', 0, 0, tiled=True)  15.8 us
    all_to_all x1, blocking collectives, body(): lse = lax.all_to_all(lse, ('core', 'y'), 0, 0, tiled=True)  14.8 us
    all_gather x1, blocking collectives, body(): own = lax.all_gather(heads, 'x', axis=0, tiled=False)  11.4 us
    pallas_call x1, Pallas kernels, most(): pl.pallas_call(kernel, out_shape=(jax.ShapeDtypeStruct((vocab, tokens), F...  9.44 us
  transfers between devices with their start and end apart: 14, of which 5 were waited for; matrix products, arithmetic and copies ran while one was open for 4% of the time, Pallas kernels for 4%

profile of v8, /device:TPU:1, one launch (start us, length us, event | category | flops | bytes accessed | tf_op | source)
XLA Modules:
  0.0 218.1 jit_solution(306815787453747627)
XLA Ops:
  7.2 0.0 all-gather.4.cloned.1.call-start
  7.2 1.2 broadcast_in_dim.2.gain_ref
  8.5 2.0 shard_map.86
  10.5 0.0 all-gather.4.cloned.1.call-update
  10.5 0.0 reduce-scatter.2.cloned.1.call-start
  10.5 0.9 pad_maximum_fusion
  11.5 11.4 %all-gather.1 = bf16[896,384]{1,0:T(8,128)(2,1)S(1)} all-gather(bf16[224,384]{1,0:T(8,128)(2,1)S(1)} %pad_maximum_fusion), channel_id=3, replica_groups=mesh['x'=4,'z'=8,'core'=2,'y'=8] {'x'}, dimensions={0}, use_global_device_ids=true | all-gather | bytes 860160 | tf_op jit(solution)/shard_map/all_gather | solution.py:398
  22.9 0.0 copy-start.1
  22.9 10.5 %collective-permute-start = (bf16[4,224,384]{2,1,0:T(8,128)(2,1)S(1)}, bf16[4,224,384]{2,1,0:T(8,128)(2,1)S(1)}, u32[]{:S(2)}, u32[]{:S(2)}) collective-permute-start(bf16[4,224,384]{2,1,0:T(8,128)(2,1)S(1)} %bitcast.20), channel_id=1, source_target_pairs={{0,8},{8,0},{1,9},{9,1},{2,10},{10,2},{3,11},{11,3},{4,12},{12,4},... | collective-permute-start | bytes 2064392 | tf_op jit(solution)/shard_map/ppermute | solution.py:52
  33.4 5.6 %collective-permute-start.4 = (bf16[4,224,384]{2,1,0:T(8,128)(2,1)S(1)}, bf16[4,224,384]{2,1,0:T(8,128)(2,1)}, u32[]{:S(2)}, u32[]{:S(2)}) collective-permute-start(bf16[4,224,384]{2,1,0:T(8,128)(2,1)S(1)} %bitcast.21), channel_id=1, source_target_pairs={{0,16},{8,120},{16,32},{24,8},{32,48},{40,24},{48,64},{56,40},{64,... | collective-permute-start | bytes 2064392 | tf_op jit(solution)/shard_map/ppermute | solution.py:48
  39.0 0.0 collective-permute-done
  39.0 2.2 %collective-permute-start.1 = (bf16[4,224,384]{2,1,0:T(8,128)(2,1)S(1)}, bf16[4,224,384]{2,1,0:T(8,128)(2,1)}, u32[]{:S(2)}, u32[]{:S(2)}) collective-permute-start(bf16[4,224,384]{2,1,0:T(8,128)(2,1)S(1)} %collective-permute-done), channel_id=1, source_target_pairs={{0,16},{8,120},{16,32},{24,8},{32,48},{40,24},{48,64},{56,40},{64,... | collective-permute-start | bytes 2064392 | tf_op jit(solution)/shard_map/ppermute | solution.py:48
  41.2 5.7 %collective-permute-done.4.refs_4_ = bf16[4,224,384]{2,1,0:T(8,128)(2,1)} collective-permute-done((bf16[4,224,384]{2,1,0:T(8,128)(2,1)S(1)}, bf16[4,224,384]{2,1,0:T(8,128)(2,1)}, u32[]{:S(2)}, u32[]{:S(2)}) %collective-permute-start.4) | collective-permute-done | bytes 688160 | tf_op jit(solution)/shard_map/ppermute | solution.py:48
  46.9 5.4 %collective-permute-start.6 = (bf16[4,224,384]{2,1,0:T(8,128)(2,1)}, bf16[4,224,384]{2,1,0:T(8,128)(2,1)}, u32[]{:S(2)}, u32[]{:S(2)}) collective-permute-start(bf16[4,224,384]{2,1,0:T(8,128)(2,1)} %collective-permute-done.4.refs_4_), channel_id=1, source_target_pairs={{0,16},{8,120},{16,32},{24,8},{32,48},{40,24},{48,64},{56,40},{64,... | collective-permute-start | bytes 2064392 | tf_op jit(solution)/shard_map/ppermute | solution.py:48
  52.3 2.0 collective-permute-done.1
  54.3 5.4 %collective-permute-start.2 = (bf16[4,224,384]{2,1,0:T(8,128)(2,1)}, bf16[4,224,384]{2,1,0:T(8,128)(2,1)}, u32[]{:S(2)}, u32[]{:S(2)}) collective-permute-start(bf16[4,224,384]{2,1,0:T(8,128)(2,1)} %collective-permute-done.1), channel_id=1, source_target_pairs={{0,16},{8,120},{16,32},{24,8},{32,48},{40,24},{48,64},{56,40},{64,... | collective-permute-start | bytes 2064392 | tf_op jit(solution)/shard_map/ppermute | solution.py:48
  59.7 0.7 convert_element_type.12
  60.4 3.1 %copy.11 = bf16[640,2048]{0,1:T(8,128)(2,1)S(1)} copy(bf16[640,2048]{1,0:T(8,128)(2,1)} %param.10) | data formatting | bytes 5242880 | tf_op args[3]
  63.5 0.0 copy-done.1
  63.5 0.6 fusion
  64.1 1.9 collective-permute-start.5
  66.1 0.0 collective-permute-done.6.refs_6_
  66.1 2.8 %collective-permute-start.8 = (bf16[4,224,384]{2,1,0:T(8,128)(2,1)}, bf16[4,224,384]{2,1,0:T(8,128)(2,1)S(1)}, u32[]{:S(2)}, u32[]{:S(2)}) collective-permute-start(bf16[4,224,384]{2,1,0:T(8,128)(2,1)} %collective-permute-done.6.refs_6_), channel_id=1, source_target_pairs={{0,16},{8,120},{16,32},{24,8},{32,48},{40,24},{48,64},{56,40},{64,... | collective-permute-start | bytes 2064392 | tf_op jit(solution)/shard_map/ppermute | solution.py:48
  68.9 0.2 collective-permute-done.2
  69.1 3.2 %collective-permute-start.7 = (bf16[4,224,384]{2,1,0:T(8,128)(2,1)}, bf16[4,224,384]{2,1,0:T(8,128)(2,1)}, u32[]{:S(2)}, u32[]{:S(2)}) collective-permute-start(bf16[4,224,384]{2,1,0:T(8,128)(2,1)} %collective-permute-done.2), channel_id=1, source_target_pairs={{0,8},{8,0},{1,9},{9,1},{2,10},{10,2},{3,11},{11,3},{4,12},{12,4},... | collective-permute-start | bytes 2064392 | tf_op jit(solution)/shard_map/ppermute | solution.py:52
  72.3 0.6 pad_add_fusion.refs_0_
  73.0 3.7 %collective-permute-start.3 = (bf16[4,224,384]{2,1,0:T(8,128)(2,1)}, bf16[4,224,384]{2,1,0:T(8,128)(2,1)}, u32[]{:S(2)}, u32[]{:S(2)}) collective-permute-start(bf16[4,224,384]{2,1,0:T(8,128)(2,1)} %collective-permute-done.2), channel_id=1, source_target_pairs={{0,16},{8,120},{16,32},{24,8},{32,48},{40,24},{48,64},{56,40},{64,... | collective-permute-start | bytes 2064392 | tf_op jit(solution)/shard_map/ppermute | solution.py:48
  76.7 2.2 %fusion.3.refs_2_.normed_hbm = bf16[2048,640]{1,0:T(8,128)(2,1)} fusion(bf16[640,2048]{0,1:T(8,128)(2,1)S(1)} %copy.11, f32[2048]{0:T(1024)S(1)} %convert_element_type.12, f32[640]{0:T(1024)S(1)} %add_rsqrt_fusion), kind=kLoop, calls=%fused_computation.5 | loop fusion | flops 5242880 | bytes 5253632 | tf_op jit(solution)/shard_map/transpose | solution.py:407
  78.9 0.0 collective-permute-done.8.refs_7_
  78.9 0.0 copy-start.3
  78.9 3.1 %collective-permute-start.9 = (bf16[4,224,384]{2,1,0:T(8,128)(2,1)S(1)}, bf16[4,224,384]{2,1,0:T(8,128)(2,1)S(1)}, u32[]{:S(2)}, u32[]{:S(2)}) collective-permute-start(bf16[4,224,384]{2,1,0:T(8,128)(2,1)S(1)} %collective-permute-done.8.refs_7_), channel_id=1, source_target_pairs={{0,16},{8,120},{16,32},{24,8},{32,48},{40,24},{48,64},{56,40},{64,... | collective-permute-start | bytes 2064392 | tf_op jit(solution)/shard_map/ppermute | solution.py:48
  82.0 0.0 collective-permute-done.5.refs_5_
  82.0 0.0 collective-permute-done.7.refs_7_
  82.0 0.0 all-gather.4.cloned.1.call-done
  82.0 9.4 %shard_map.87 = (f32[384,640]{1,0:T(8,128)}, f32[384,640]{1,0:T(8,128)}, f32[1,640]{1,0:T(1,128)}, bf16[4,8,64,384]{3,2,1,0:T(8,128)(2,1)}) custom-call(s32[2]{0:T(128)} %pad_add_fusion.refs_0_, bf16[16,336,640]{2,1,0:T(8,128)(2,1)} %bitcast.18, bf16[2048,640]{1,0:T(8,128)(2,1)} %fusion.3.refs_2_.normed_hbm, bf16[4,224,384]{2,1,0:T(8,128)(2,1)} %bitcast.22, ...), custom_call_target="tpu_custom_call" | custom-call | flops 2202009600 | bytes 12582912 | tf_op jit(solution)/shard_map/pallas_call | solution.py:183
  91.5 0.0 copy-done.3
  91.5 0.0 collective-permute-done.3
  91.5 2.7 %collective-permute-start.10 = (bf16[4,224,384]{2,1,0:T(8,128)(2,1)}, bf16[4,224,384]{2,1,0:T(8,128)(2,1)S(1)}, u32[]{:S(2)}, u32[]{:S(2)}) collective-permute-start(bf16[4,224,384]{2,1,0:T(8,128)(2,1)} %collective-permute-done.3), channel_id=1, source_target_pairs={{0,8},{8,0},{1,9},{9,1},{2,10},{10,2},{3,11},{11,3},{4,12},{12,4},... | collective-permute-start | bytes 2064392 | tf_op jit(solution)/shard_map/ppermute | solution.py:52
  94.8 0.6 pad_add_fusion.1.which_ref
  95.4 0.0 collective-permute-done.9.refs_8_
  95.4 0.0 copy-start.4
  95.4 0.7 collective-permute-done.10.refs_9_
  96.1 0.1 copy-done.4
  96.3 0.0 copy-start.5
  96.3 0.9 copy-done.5
  97.2 7.9 %shard_map.88 = (f32[384,640]{1,0:T(8,128)}, f32[384,640]{1,0:T(8,128)}, f32[16,2,640]{2,1,0:T(2,128)}, bf16[4,8,64,384]{3,2,1,0:T(8,128)(2,1)}) custom-call(s32[2]{0:T(128)} %pad_add_fusion.refs_0_, bf16[16,336,640]{2,1,0:T(8,128)(2,1)} %bitcast.19, bf16[2048,640]{1,0:T(8,128)(2,1)} %fusion.3.refs_2_.normed_hbm, ...), custom_call_target="tpu_custom_call", output_to_operand_aliasing={{3}: (6, {})} | custom-call | flops 1321205760 | bytes 8388608 | tf_op jit(solution)/shard_map/pallas_call | solution.py:240
  105.1 14.8 %all_to_all.26.lse_ref = f32[16,2,640]{2,1,0:T(2,128)} all-to-all(f32[16,2,640]{2,1,0:T(2,128)} %get-tuple-element.38), channel_id=1, replica_groups=mesh['x'=4,'z'=8,'core'=2,'y'=8] {'core','y'}, dimensions={0} | all-to-all | bytes 163840 | tf_op jit(solution)/shard_map/all_to_all | solution.py:436
  119.9 7.0 %shard_map.89 = (bf16[320,2048]{1,0:T(8,128)(2,1)}, bf16[320,2048]{1,0:T(8,128)(2,1)}, bf16[2048,384]{1,0:T(8,128)(2,1)}) custom-call(s32[2]{0:T(128)} %pad_add_fusion.1.which_ref, f32[384,640]{1,0:T(8,128)} %get-tuple-element.36.student_hbm, f32[384,640]{1,0:T(8,128)} %get-tuple-element.37.teacher_hbm, f32[16,2,640]{2,1,0:T(2,128)} %all_to_all.26.lse_ref, ...), custom_call_target="tpu_custom_call" | custom-call | flops 2013265920 | bytes 10485760 | tf_op jit(solution)/shard_map/pallas_call | solution.py:314
  126.9 2.9 %collective-permute-start.11 = (bf16[320,2048]{1,0:T(8,128)(2,1)}, bf16[320,2048]{1,0:T(8,128)(2,1)S(1)}, u32[]{:S(2)}, u32[]{:S(2)}) collective-permute-start(bf16[320,2048]{1,0:T(8,128)(2,1)} %get-tuple-element.43), channel_id=1, source_target_pairs={{0,8},{8,0},{1,9},{9,1},{2,10},{10,2},{3,11},{11,3},{4,12},{12,4},... | collective-permute-start | bytes 3932168 | tf_op jit(solution)/shard_map/ppermute | solution.py:52
  129.8 2.9 %collective-permute-done.11.right_ref = bf16[320,2048]{1,0:T(8,128)(2,1)S(1)} collective-permute-done((bf16[320,2048]{1,0:T(8,128)(2,1)}, bf16[320,2048]{1,0:T(8,128)(2,1)S(1)}, u32[]{:S(2)}, u32[]{:S(2)}) %collective-permute-start.11) | collective-permute-done | bytes 1310752 | tf_op jit(solution)/shard_map/ppermute | solution.py:52
  132.6 0.0 copy-start
  132.6 1.3 copy-done
  134.0 0.0 copy-start.2
  134.0 1.8 shard_map.90
  135.7 0.0 reduce-scatter.2.cloned.1.call-update
  135.8 0.0 copy-done.2
  135.8 23.8 %all_to_all.27 = bf16[4,512,384]{2,1,0:T(8,128)(2,1)S(1)} all-to-all(bf16[4,512,384]{2,1,0:T(8,128)(2,1)S(1)} %bitcast.23), channel_id=1, replica_groups=mesh['x'=4,'z'=8,'core'=2,'y'=8] {'x'}, dimensions={0} | all-to-all | bytes 3145728 | tf_op jit(solution)/shard_map/all_to_all | solution.py:445
  159.5 0.4 reduce_sum.22
  160.0 15.8 %all_to_all.28.parts_ref = bf16[8,64,384]{2,1,0:T(8,128)(2,1)} all-to-all(bf16[8,64,384]{2,1,0:T(8,128)(2,1)S(1)} %bitcast.24), channel_id=1, replica_groups=mesh['x'=4,'z'=8,'core'=2,'y'=8] {'z'}, dimensions={0} | all-to-all | bytes 786432 | tf_op jit(solution)/shard_map/all_to_all | solution.py:447
  175.7 0.0 reduce-scatter.2.cloned.1.call-done.row_ref.refs_2_
  175.7 2.0 shard_map.91
  177.7 31.6 %all_to_all.29 = f32[512,1,128]{2,1,0:T(1,128)} all-to-all(f32[512,1,128]{2,1,0:T(1,128)} %bitcast.28), channel_id=1, replica_groups=mesh['x'=4,'z'=8,'core'=2,'y'=8] {'x','z','core','y'}, dimensions={0} | all-to-all | bytes 524288 | tf_op jit(solution)/shard_map/all_to_all | solution.py:457
  209.4 1.9 shard_map.92
  (1 shorter events, 0.0 us)
Async XLA Ops:
  7.2 74.9 %all-gather.4.cloned.1.call-start = ((), (), s32[]{:S(2)}) async-start(), calls=%async_computation.6 | async-start | bytes 7311360 | tf_op jit(solution)/shard_map/all_gather | solution.py:395
  10.5 165.2 %reduce-scatter.2.cloned.1.call-start = ((), (), s32[]{:S(2)}) async-start(), calls=%async_computation.5 | async-start | bytes 1474560 | tf_op jit(solution)/shard_map/reduce_scatter | solution.py:443
  22.9 40.7 %copy-start.1 = (bf16[896,384]{1,0:T(8,128)(2,1)}, bf16[896,384]{1,0:T(8,128)(2,1)S(1)}, u32[]{:S(2)}) copy-start(bf16[896,384]{1,0:T(8,128)(2,1)S(1)} %all-gather.1) | copy-start | bytes 2064388
  22.9 16.1 %collective-permute-start = (bf16[4,224,384]{2,1,0:T(8,128)(2,1)S(1)}, bf16[4,224,384]{2,1,0:T(8,128)(2,1)S(1)}, u32[]{:S(2)}, u32[]{:S(2)}) collective-permute-start(bf16[4,224,384]{2,1,0:T(8,128)(2,1)S(1)} %bitcast.20), channel_id=1, source_target_pairs={{0,8},{8,0},{1,9},{9,1},{2,10},{10,2},{3,11},{11,3},{4,12},{12,4},... | collective-permute-start | bytes 2064392 | tf_op jit(solution)/shard_map/ppermute | solution.py:52
  33.4 13.5 %collective-permute-start.4 = (bf16[4,224,384]{2,1,0:T(8,128)(2,1)S(1)}, bf16[4,224,384]{2,1,0:T(8,128)(2,1)}, u32[]{:S(2)}, u32[]{:S(2)}) collective-permute-start(bf16[4,224,384]{2,1,0:T(8,128)(2,1)S(1)} %bitcast.21), channel_id=1, source_target_pairs={{0,16},{8,120},{16,32},{24,8},{32,48},{40,24},{48,64},{56,40},{64,... | collective-permute-start | bytes 2064392 | tf_op jit(solution)/shard_map/ppermute | solution.py:48
  39.0 15.2 %collective-permute-start.1 = (bf16[4,224,384]{2,1,0:T(8,128)(2,1)S(1)}, bf16[4,224,384]{2,1,0:T(8,128)(2,1)}, u32[]{:S(2)}, u32[]{:S(2)}) collective-permute-start(bf16[4,224,384]{2,1,0:T(8,128)(2,1)S(1)} %collective-permute-done), channel_id=1, source_target_pairs={{0,16},{8,120},{16,32},{24,8},{32,48},{40,24},{48,64},{56,40},{64,... | collective-permute-start | bytes 2064392 | tf_op jit(solution)/shard_map/ppermute | solution.py:48
  46.9 19.2 %collective-permute-start.6 = (bf16[4,224,384]{2,1,0:T(8,128)(2,1)}, bf16[4,224,384]{2,1,0:T(8,128)(2,1)}, u32[]{:S(2)}, u32[]{:S(2)}) collective-permute-start(bf16[4,224,384]{2,1,0:T(8,128)(2,1)} %collective-permute-done.4.refs_4_), channel_id=1, source_target_pairs={{0,16},{8,120},{16,32},{24,8},{32,48},{40,24},{48,64},{56,40},{64,... | collective-permute-start | bytes 2064392 | tf_op jit(solution)/shard_map/ppermute | solution.py:48
  54.3 14.9 %collective-permute-start.2 = (bf16[4,224,384]{2,1,0:T(8,128)(2,1)}, bf16[4,224,384]{2,1,0:T(8,128)(2,1)}, u32[]{:S(2)}, u32[]{:S(2)}) collective-permute-start(bf16[4,224,384]{2,1,0:T(8,128)(2,1)} %collective-permute-done.1), channel_id=1, source_target_pairs={{0,16},{8,120},{16,32},{24,8},{32,48},{40,24},{48,64},{56,40},{64,... | collective-permute-start | bytes 2064392 | tf_op jit(solution)/shard_map/ppermute | solution.py:48
  64.1 17.9 %collective-permute-start.5 = (bf16[4,224,384]{2,1,0:T(8,128)(2,1)}, bf16[4,224,384]{2,1,0:T(8,128)(2,1)}, u32[]{:S(2)}, u32[]{:S(2)}) collective-permute-start(bf16[4,224,384]{2,1,0:T(8,128)(2,1)} %collective-permute-done.1), channel_id=1, source_target_pairs={{0,8},{8,0},{1,9},{9,1},{2,10},{10,2},{3,11},{11,3},{4,12},{12,4},... | collective-permute-start | bytes 2064392 | tf_op jit(solution)/shard_map/ppermute | solution.py:52
  66.1 12.8 %collective-permute-start.8 = (bf16[4,224,384]{2,1,0:T(8,128)(2,1)}, bf16[4,224,384]{2,1,0:T(8,128)(2,1)S(1)}, u32[]{:S(2)}, u32[]{:S(2)}) collective-permute-start(bf16[4,224,384]{2,1,0:T(8,128)(2,1)} %collective-permute-done.6.refs_6_), channel_id=1, source_target_pairs={{0,16},{8,120},{16,32},{24,8},{32,48},{40,24},{48,64},{56,40},{64,... | collective-permute-start | bytes 2064392 | tf_op jit(solution)/shard_map/ppermute | solution.py:48
  69.1 12.9 %collective-permute-start.7 = (bf16[4,224,384]{2,1,0:T(8,128)(2,1)}, bf16[4,224,384]{2,1,0:T(8,128)(2,1)}, u32[]{:S(2)}, u32[]{:S(2)}) collective-permute-start(bf16[4,224,384]{2,1,0:T(8,128)(2,1)} %collective-permute-done.2), channel_id=1, source_target_pairs={{0,8},{8,0},{1,9},{9,1},{2,10},{10,2},{3,11},{11,3},{4,12},{12,4},... | collective-permute-start | bytes 2064392 | tf_op jit(solution)/shard_map/ppermute | solution.py:52
  73.0 18.5 %collective-permute-start.3 = (bf16[4,224,384]{2,1,0:T(8,128)(2,1)}, bf16[4,224,384]{2,1,0:T(8,128)(2,1)}, u32[]{:S(2)}, u32[]{:S(2)}) collective-permute-start(bf16[4,224,384]{2,1,0:T(8,128)(2,1)} %collective-permute-done.2), channel_id=1, source_target_pairs={{0,16},{8,120},{16,32},{24,8},{32,48},{40,24},{48,64},{56,40},{64,... | collective-permute-start | bytes 2064392 | tf_op jit(solution)/shard_map/ppermute | solution.py:48
  78.9 12.6 %copy-start.3 = (bf16[4,224,384]{2,1,0:T(8,128)(2,1)}, bf16[4,224,384]{2,1,0:T(8,128)(2,1)S(1)}, u32[]{:S(2)}) copy-start(bf16[4,224,384]{2,1,0:T(8,128)(2,1)S(1)} %collective-permute-done.8.refs_7_) | copy-start | bytes 2064388
  78.9 16.5 %collective-permute-start.9 = (bf16[4,224,384]{2,1,0:T(8,128)(2,1)S(1)}, bf16[4,224,384]{2,1,0:T(8,128)(2,1)S(1)}, u32[]{:S(2)}, u32[]{:S(2)}) collective-permute-start(bf16[4,224,384]{2,1,0:T(8,128)(2,1)S(1)} %collective-permute-done.8.refs_7_), channel_id=1, source_target_pairs={{0,16},{8,120},{16,32},{24,8},{32,48},{40,24},{48,64},{56,40},{64,... | collective-permute-start | bytes 2064392 | tf_op jit(solution)/shard_map/ppermute | solution.py:48
  91.5 4.6 %collective-permute-start.10 = (bf16[4,224,384]{2,1,0:T(8,128)(2,1)}, bf16[4,224,384]{2,1,0:T(8,128)(2,1)S(1)}, u32[]{:S(2)}, u32[]{:S(2)}) collective-permute-start(bf16[4,224,384]{2,1,0:T(8,128)(2,1)} %collective-permute-done.3), channel_id=1, source_target_pairs={{0,8},{8,0},{1,9},{9,1},{2,10},{10,2},{3,11},{11,3},{4,12},{12,4},... | collective-permute-start | bytes 2064392 | tf_op jit(solution)/shard_map/ppermute | solution.py:52
  95.4 0.9 copy-start.4
  96.3 0.9 copy-start.5
  126.9 5.8 %collective-permute-start.11 = (bf16[320,2048]{1,0:T(8,128)(2,1)}, bf16[320,2048]{1,0:T(8,128)(2,1)S(1)}, u32[]{:S(2)}, u32[]{:S(2)}) collective-permute-start(bf16[320,2048]{1,0:T(8,128)(2,1)} %get-tuple-element.43), channel_id=1, source_target_pairs={{0,8},{8,0},{1,9},{9,1},{2,10},{10,2},{3,11},{11,3},{4,12},{12,4},... | collective-permute-start | bytes 3932168 | tf_op jit(solution)/shard_map/ppermute | solution.py:52
  132.6 1.3 copy-start
  134.0 1.8 copy-start.2
Sparse Core Ops, SparseCore 0:
  10.6 57.8 all-gather.3
  135.9 31.7 reduce-scatter.1

commit v9 on v7

--- a/solution.py
+++ b/solution.py
@@ -11,7 +11,7 @@
 NX, NZ, NC, NY = 4, 8, 2, 8
 epsilon = 1e-06
 HEAD_ROWS = 16
-LSE_ROWS = 8
+LSE_ROWS = 2
 GRANT = 60 << 20
 HBM = pl.BlockSpec(memory_space=pltpu.HBM)
 VMEM = pl.BlockSpec(memory_space=pltpu.VMEM)
@@ -32,8 +32,12 @@
     return (values * lax.rsqrt(mean_square + epsilon) * gain.astype(F32)).astype(BF16)
 
 
-def along(values):
-    pairs = [(i * NC + c, (i + 1 - 2 * c) % NZ * NC + c) for i in range(NZ) for c in range(NC)]
+def along(values, cross_in=False, cross_out=False):
+    pairs = []
+    for i in range(NZ):
+        for c in range(NC):
+            near, far = i, (i + 1 - 2 * c) % NZ
+            pairs.append((near * NC + (c ^ cross_in), far * NC + (c ^ cross_out)))
     return lax.ppermute(values, ("z", "core"), pairs)
 
 
@@ -331,6 +335,23 @@
     )(which, student, teacher, lse, weights, normed)
 
 
+def added_kernel(left_ref, right_ref, out_ref):
+    out_ref[...] = (left_ref[...].astype(F32) + right_ref[...].astype(F32)).astype(BF16)
+
+
+def added(left, right):
+    rows, columns = left.shape
+    spec = pl.BlockSpec((rows // NX, columns), lambda i: (i, 0))
+    return pl.pallas_call(
+        added_kernel,
+        out_shape=jax.ShapeDtypeStruct(left.shape, BF16),
+        grid=(NX,),
+        in_specs=[spec, spec],
+        out_specs=spec,
+        compiler_params=pltpu.CompilerParams(vmem_limit_bytes=16 << 20),
+    )(left, right)
+
+
 def squares_kernel(parts_ref, row_ref, head_ref, out_ref):
     head = jnp.sum(parts_ref[...].astype(F32), axis=0)
     head_ref[...] = head
@@ -370,26 +391,24 @@
     heads = jnp.concatenate([student_head.T, teacher_head.T], axis=0)
     own = lax.all_gather(heads, "x", axis=0, tiled=False)
     blocks, offsets = [own], [0]
-    mine, theirs = own, swapped(own)
+    mine = theirs = own
     for step in range(1, NZ // 2):
-        mine, theirs = along(mine), along(theirs)
-        if step < NZ // 2 - 1:
-            blocks += [mine, swapped(theirs)]
-            offsets += [-step, step]
+        final = step == NZ // 2 - 1
+        mine, theirs = along(mine), along(theirs, cross_in=step == 1, cross_out=final)
+        blocks.append(mine)
+        offsets.append(-step)
+        if not final:
+            blocks.append(swapped(theirs))
+            offsets.append(step)
 
     normed = normalize(student_rows, student_gain).T
     early = len(blocks)
-    blocks += [mine, along(mine)]
-    offsets += [1 - NZ // 2, -NZ // 2]
+    blocks += [theirs, along(mine)]
+    offsets += [NZ // 2 - 1, -NZ // 2]
     where = jnp.stack([z, 1 - 2 * c])
     student_logits, teacher_logits, scale, weights = most(
         where, rows, normed, blocks[:early], offsets[:early], wide, fs
     )
-    theirs, student_logits, teacher_logits, scale, weights = lax.optimization_barrier(
-        (theirs, student_logits, teacher_logits, scale, weights)
-    )
-    blocks.append(swapped(theirs))
-    offsets.append(NZ // 2 - 1)
     student_logits, teacher_logits, lse, weights = last(
         where,
         rows,
@@ -412,7 +431,7 @@
     )
 
     other = swapped(other)
-    mine = (mine.astype(F32) + other.astype(F32)).astype(BF16)
+    mine = added(mine, other)
     row_grad = lax.psum_scatter(mine, "y", scatter_dimension=0, tiled=True)
 
     head_part = lax.all_to_all(head_part.reshape(NX, NZ * fs, vocab), "x", 0, 0, tiled=True)

time: 221 us -> 218 us (0.986)
  starting transfers between devices: 49.1 us -> 44.7 us
  waiting for transfers between devices: 12.1 us -> 15.6 us
  other arithmetic: 11.1 us -> 8.05 us
  blocking collectives: 100 us -> 97.6 us
    ppermute x5 -> x3, starting transfers between devices: 21.4 us -> 12.3 us  [swapped(): return lax.ppermute(values, 'core', [(0, 1), (1, 0)])]
    ppermute x7, starting transfers between devices: 27.6 us -> 32.3 us  [along(): return lax.ppermute(values, ('z', 'core'), pairs)]
    ppermute x7, waiting for transfers between devices: 8.53 us -> 12.7 us  [along(): return lax.ppermute(values, ('z', 'core'), pairs)]
    convert_element_type x1 -> x0, other arithmetic: 3 us -> none  [body(): mine = (mine.astype(F32) + other.astype(F32)).astype(BF16)]
  transfers between devices with their start and end apart: 14 -> 12, of which waited for: 5 -> 4; matrix products, arithmetic and copies ran while one was open for 4% -> 4% of each run, Pallas kernels for 4% -> 5%
where the time goes in v9:
time: 218 us; the launch traced here: 217 us
  blocking collectives  97.6 us (45%)
  starting transfers between devices  44.7 us (21%)
  Pallas kernels  30.6 us (14%)
  waiting for transfers between devices  15.6 us (7%)
  between operations  14.9 us (7%)
  other arithmetic  8.05 us (4%)
  local copies, waits for them, and re-layouts  5.35 us (2%)
    ppermute x7, starting transfers between devices, along(): return lax.ppermute(values, ('z', 'core'), pairs)  32.3 us
    all_to_all x1, blocking collectives, body(): squares = lax.all_to_all(squares, ('x', 'z', 'core', 'y'), 0, 0, tiled=True)  30.1 us
    all_to_all x1, blocking collectives, body(): lax.all_to_all(head_part.reshape(NX, NZ * fs, vocab), 'x', 0, 0, tiled=True)  22.8 us
    all_to_all x1, blocking collectives, body(): lse = lax.all_to_all(lse, ('core', 'y'), 0, 0, tiled=True)  17.1 us
    all_to_all x1, blocking collectives, body(): lax.all_to_all(head_part.reshape(NZ, fs, vocab), 'z', 0, 0, tiled=True)  16.2 us
    ppermute x7, waiting for transfers between devices, along(): return lax.ppermute(values, ('z', 'core'), pairs)  12.7 us
    ppermute x3, starting transfers between devices, swapped(): return lax.ppermute(values, 'core', [(0, 1), (1, 0)])  12.3 us
    all_gather x1, blocking collectives, body(): own = lax.all_gather(heads, 'x', axis=0, tiled=False)  11.4 us
  transfers between devices with their start and end apart: 12, of which 4 were waited for; matrix products, arithmetic and copies ran while one was open for 4% of the time, Pallas kernels for 5%

profile of v9, /device:TPU:1, one launch (start us, length us, event | category | flops | bytes accessed | tf_op | source)
XLA Modules:
  0.0 216.8 jit_solution(4296412034933623125)
XLA Ops:
  7.2 0.0 all-gather.4.cloned.1.call-start
  7.2 0.7 convert_element_type.93
  7.9 1.1 fusion.6
  9.1 0.8 pad_maximum_fusion
  9.9 0.0 all-gather.4.cloned.1.call-update
  9.9 0.0 reduce-scatter.2.cloned.1.call-start
  10.0 0.9 pad_maximum_fusion.1
  10.9 11.4 %all-gather.1 = bf16[896,384]{1,0:T(8,128)(2,1)S(1)} all-gather(bf16[224,384]{1,0:T(8,128)(2,1)S(1)} %pad_maximum_fusion.1), channel_id=3, replica_groups=mesh['x'=4,'z'=8,'core'=2,'y'=8] {'x'}, dimensions={0}, use_global_device_ids=true | all-gather | bytes 860160 | tf_op jit(solution)/shard_map/all_gather | solution.py:392
  22.3 0.0 copy-start.1
  22.3 12.0 %collective-permute-start = (bf16[4,224,384]{2,1,0:T(8,128)(2,1)S(1)}, bf16[4,224,384]{2,1,0:T(8,128)(2,1)}, u32[]{:S(2)}, u32[]{:S(2)}) collective-permute-start(bf16[4,224,384]{2,1,0:T(8,128)(2,1)S(1)} %bitcast.21), channel_id=1, source_target_pairs={{0,16},{8,120},{16,32},{24,8},{32,48},{40,24},{48,64},{56,40},{64,... | collective-permute-start | bytes 2064392 | tf_op jit(solution)/shard_map/ppermute | solution.py:41
  34.3 1.9 collective-permute-start.1
  36.2 10.5 %collective-permute-done.refs_4_ = bf16[4,224,384]{2,1,0:T(8,128)(2,1)} collective-permute-done((bf16[4,224,384]{2,1,0:T(8,128)(2,1)S(1)}, bf16[4,224,384]{2,1,0:T(8,128)(2,1)}, u32[]{:S(2)}, u32[]{:S(2)}) %collective-permute-start) | collective-permute-done | bytes 688160 | tf_op jit(solution)/shard_map/ppermute | solution.py:41
  46.7 5.4 %collective-permute-start.3 = (bf16[4,224,384]{2,1,0:T(8,128)(2,1)}, bf16[4,224,384]{2,1,0:T(8,128)(2,1)}, u32[]{:S(2)}, u32[]{:S(2)}) collective-permute-start(bf16[4,224,384]{2,1,0:T(8,128)(2,1)} %collective-permute-done.refs_4_), channel_id=1, source_target_pairs={{0,16},{8,120},{16,32},{24,8},{32,48},{40,24},{48,64},{56,40},{64,... | collective-permute-start | bytes 2064392 | tf_op jit(solution)/shard_map/ppermute | solution.py:41
  52.1 0.0 collective-permute-done.1
  52.1 2.8 %collective-permute-start.4 = (bf16[4,224,384]{2,1,0:T(8,128)(2,1)}, bf16[4,224,384]{2,1,0:T(8,128)(2,1)}, u32[]{:S(2)}, u32[]{:S(2)}) collective-permute-start(bf16[4,224,384]{2,1,0:T(8,128)(2,1)} %collective-permute-done.1), channel_id=1, source_target_pairs={{0,16},{8,120},{16,32},{24,8},{32,48},{40,24},{48,64},{56,40},{64,... | collective-permute-start | bytes 2064392 | tf_op jit(solution)/shard_map/ppermute | solution.py:41
  54.9 0.0 copy-start.5
  54.9 3.1 %copy.11 = bf16[640,2048]{0,1:T(8,128)(2,1)S(1)} copy(bf16[640,2048]{1,0:T(8,128)(2,1)} %param.10) | data formatting | bytes 5242880 | tf_op args[3]
  58.1 0.0 copy-done.1
  58.1 0.0 copy-done.5
  58.8 1.5 collective-permute-done.3.refs_6_
  60.3 5.3 %collective-permute-start.6 = (bf16[4,224,384]{2,1,0:T(8,128)(2,1)}, bf16[4,224,384]{2,1,0:T(8,128)(2,1)S(1)}, u32[]{:S(2)}, u32[]{:S(2)}) collective-permute-start(bf16[4,224,384]{2,1,0:T(8,128)(2,1)} %collective-permute-done.3.refs_6_), channel_id=1, source_target_pairs={{0,16},{8,120},{16,32},{24,8},{32,48},{40,24},{48,64},{56,40},{64,... | collective-permute-start | bytes 2064392 | tf_op jit(solution)/shard_map/ppermute | solution.py:41
  65.6 0.6 pad_add_fusion.refs_0_
  66.2 0.6 fusion
  66.8 5.3 %collective-permute-start.2 = (bf16[4,224,384]{2,1,0:T(8,128)(2,1)}, bf16[4,224,384]{2,1,0:T(8,128)(2,1)S(1)}, u32[]{:S(2)}, u32[]{:S(2)}) collective-permute-start(bf16[4,224,384]{2,1,0:T(8,128)(2,1)} %collective-permute-done.1), channel_id=1, source_target_pairs={{0,8},{8,0},{1,9},{9,1},{2,10},{10,2},{3,11},{11,3},{4,12},{12,4},... | collective-permute-start | bytes 2064392 | tf_op jit(solution)/shard_map/ppermute | solution.py:45
  72.1 0.0 collective-permute-done.4
  72.1 4.2 %collective-permute-start.5 = (bf16[4,224,384]{2,1,0:T(8,128)(2,1)}, bf16[4,224,384]{2,1,0:T(8,128)(2,1)}, u32[]{:S(2)}, u32[]{:S(2)}) collective-permute-start(bf16[4,224,384]{2,1,0:T(8,128)(2,1)} %collective-permute-done.4), channel_id=1, source_target_pairs={{0,8},{8,0},{1,9},{9,1},{2,10},{10,2},{3,11},{11,3},{4,12},{12,4},... | collective-permute-start | bytes 2064392 | tf_op jit(solution)/shard_map/ppermute | solution.py:45
  76.3 0.6 pad_add_fusion.1.which_ref
  76.9 3.0 %collective-permute-start.7 = (bf16[4,224,384]{2,1,0:T(8,128)(2,1)}, bf16[4,224,384]{2,1,0:T(8,128)(2,1)}, u32[]{:S(2)}, u32[]{:S(2)}) collective-permute-start(bf16[4,224,384]{2,1,0:T(8,128)(2,1)} %collective-permute-done.4), channel_id=1, source_target_pairs={{0,24},{8,112},{16,40},{24,0},{32,56},{40,16},{48,72},{56,32},{64,... | collective-permute-start | bytes 2064392 | tf_op jit(solution)/shard_map/ppermute | solution.py:41
  79.8 0.0 collective-permute-done.6.refs_8_
  79.8 0.0 copy-start.3
  79.9 1.9 collective-permute-start.8
  81.8 2.2 %fusion.3.refs_2_.normed_hbm = bf16[2048,640]{1,0:T(8,128)(2,1)} fusion(bf16[640,2048]{0,1:T(8,128)(2,1)S(1)} %copy.11, f32[2048]{0:T(1024)S(1)} %convert_element_type.102, f32[640]{0:T(1024)S(1)} %add_rsqrt_fusion), kind=kLoop, calls=%fused_computation.5 | loop fusion | flops 5242880 | bytes 5253632 | tf_op jit(solution)/shard_map/transpose | solution.py:404
  84.0 0.0 copy-done.3
  84.0 0.0 collective-permute-done.2.refs_5_
  84.0 0.0 copy-start.4
  84.0 0.9 copy-done.4
  84.9 0.0 collective-permute-done.5.refs_7_
  84.9 0.0 all-gather.4.cloned.1.call-done
  84.9 10.8 %shard_map.86 = (f32[384,640]{1,0:T(8,128)}, f32[384,640]{1,0:T(8,128)}, f32[1,640]{1,0:T(1,128)}, bf16[4,8,64,384]{3,2,1,0:T(8,128)(2,1)}) custom-call(s32[2]{0:T(128)} %pad_add_fusion.refs_0_, bf16[16,336,640]{2,1,0:T(8,128)(2,1)} %bitcast.19, bf16[2048,640]{1,0:T(8,128)(2,1)} %fusion.3.refs_2_.normed_hbm, bf16[4,224,384]{2,1,0:T(8,128)(2,1)} %bitcast.23, ...), custom_call_target="tpu_custom_call" | custom-call | flops 2642411520 | bytes 12582912 | tf_op jit(solution)/shard_map/pallas_call | solution.py:176
  95.7 0.0 collective-permute-done.7.refs_7_
  95.7 0.7 collective-permute-done.8.refs_8_
  96.4 7.1 %shard_map.87 = (f32[384,640]{1,0:T(8,128)}, f32[384,640]{1,0:T(8,128)}, f32[16,2,640]{2,1,0:T(2,128)}, bf16[4,8,64,384]{3,2,1,0:T(8,128)(2,1)}) custom-call(s32[2]{0:T(128)} %pad_add_fusion.refs_0_, bf16[16,336,640]{2,1,0:T(8,128)(2,1)} %bitcast.20, bf16[2048,640]{1,0:T(8,128)(2,1)} %fusion.3.refs_2_.normed_hbm, ...), custom_call_target="tpu_custom_call", output_to_operand_aliasing={{3}: (6, {})} | custom-call | flops 880803840 | bytes 8388608 | tf_op jit(solution)/shard_map/pallas_call | solution.py:233
  103.6 17.1 %all_to_all.26.lse_ref = f32[16,2,640]{2,1,0:T(2,128)} all-to-all(f32[16,2,640]{2,1,0:T(2,128)} %get-tuple-element.28), channel_id=1, replica_groups=mesh['x'=4,'z'=8,'core'=2,'y'=8] {'core','y'}, dimensions={0} | all-to-all | bytes 163840 | tf_op jit(solution)/shard_map/all_to_all | solution.py:428
  120.6 7.0 %shard_map.88 = (bf16[320,2048]{1,0:T(8,128)(2,1)}, bf16[320,2048]{1,0:T(8,128)(2,1)}, bf16[2048,384]{1,0:T(8,128)(2,1)}) custom-call(s32[2]{0:T(128)} %pad_add_fusion.1.which_ref, f32[384,640]{1,0:T(8,128)} %get-tuple-element.26.student_hbm, f32[384,640]{1,0:T(8,128)} %get-tuple-element.27.teacher_hbm, f32[16,2,640]{2,1,0:T(2,128)} %all_to_all.26.lse_ref, ...), custom_call_target="tpu_custom_call" | custom-call | flops 2013265920 | bytes 10485760 | tf_op jit(solution)/shard_map/pallas_call | solution.py:307
  127.6 2.9 %collective-permute-start.9 = (bf16[320,2048]{1,0:T(8,128)(2,1)}, bf16[320,2048]{1,0:T(8,128)(2,1)S(1)}, u32[]{:S(2)}, u32[]{:S(2)}) collective-permute-start(bf16[320,2048]{1,0:T(8,128)(2,1)} %get-tuple-element.33), channel_id=1, source_target_pairs={{0,8},{8,0},{1,9},{9,1},{2,10},{10,2},{3,11},{11,3},{4,12},{12,4},... | collective-permute-start | bytes 3932168 | tf_op jit(solution)/shard_map/ppermute | solution.py:45
  130.5 2.9 %collective-permute-done.9.right_ref = bf16[320,2048]{1,0:T(8,128)(2,1)S(1)} collective-permute-done((bf16[320,2048]{1,0:T(8,128)(2,1)}, bf16[320,2048]{1,0:T(8,128)(2,1)S(1)}, u32[]{:S(2)}, u32[]{:S(2)}) %collective-permute-start.9) | collective-permute-done | bytes 1310752 | tf_op jit(solution)/shard_map/ppermute | solution.py:45
  133.4 0.0 copy-start
  133.4 1.3 copy-done
  134.7 0.0 copy-start.2
  134.7 1.7 shard_map.89
  136.5 0.0 reduce-scatter.2.cloned.1.call-update
  136.5 0.0 copy-done.2
  136.5 22.8 %all_to_all.27 = bf16[4,512,384]{2,1,0:T(8,128)(2,1)S(1)} all-to-all(bf16[4,512,384]{2,1,0:T(8,128)(2,1)S(1)} %bitcast.24), channel_id=1, replica_groups=mesh['x'=4,'z'=8,'core'=2,'y'=8] {'x'}, dimensions={0} | all-to-all | bytes 3145728 | tf_op jit(solution)/shard_map/all_to_all | solution.py:437
  159.3 0.4 reduce_sum.35
  159.7 16.2 %all_to_all.28.parts_ref = bf16[8,64,384]{2,1,0:T(8,128)(2,1)} all-to-all(bf16[8,64,384]{2,1,0:T(8,128)(2,1)S(1)} %bitcast.25), channel_id=1, replica_groups=mesh['x'=4,'z'=8,'core'=2,'y'=8] {'z'}, dimensions={0} | all-to-all | bytes 786432 | tf_op jit(solution)/shard_map/all_to_all | solution.py:439
  175.9 0.0 reduce-scatter.2.cloned.1.call-done.row_ref.refs_2_
  175.9 2.0 shard_map.90
  177.9 30.1 %all_to_all.29 = f32[512,1,128]{2,1,0:T(1,128)} all-to-all(f32[512,1,128]{2,1,0:T(1,128)} %bitcast.28), channel_id=1, replica_groups=mesh['x'=4,'z'=8,'core'=2,'y'=8] {'x','z','core','y'}, dimensions={0} | all-to-all | bytes 524288 | tf_op jit(solution)/shard_map/all_to_all | solution.py:449
  208.1 1.9 shard_map.91
  (5 shorter events, 0.0 us)
Async XLA Ops:
  7.2 77.7 %all-gather.4.cloned.1.call-start = ((), (), s32[]{:S(2)}) async-start(), calls=%async_computation.6 | async-start | bytes 7311360 | tf_op jit(solution)/shard_map/all_gather | solution.py:389
  9.9 166.0 %reduce-scatter.2.cloned.1.call-start = ((), (), s32[]{:S(2)}) async-start(), calls=%async_computation.5 | async-start | bytes 1474560 | tf_op jit(solution)/shard_map/reduce_scatter | solution.py:435
  22.3 35.8 %copy-start.1 = (bf16[896,384]{1,0:T(8,128)(2,1)}, bf16[896,384]{1,0:T(8,128)(2,1)S(1)}, u32[]{:S(2)}) copy-start(bf16[896,384]{1,0:T(8,128)(2,1)S(1)} %all-gather.1) | copy-start | bytes 2064388
  22.3 24.4 %collective-permute-start = (bf16[4,224,384]{2,1,0:T(8,128)(2,1)S(1)}, bf16[4,224,384]{2,1,0:T(8,128)(2,1)}, u32[]{:S(2)}, u32[]{:S(2)}) collective-permute-start(bf16[4,224,384]{2,1,0:T(8,128)(2,1)S(1)} %bitcast.21), channel_id=1, source_target_pairs={{0,16},{8,120},{16,32},{24,8},{32,48},{40,24},{48,64},{56,40},{64,... | collective-permute-start | bytes 2064392 | tf_op jit(solution)/shard_map/ppermute | solution.py:41
  34.3 17.8 %collective-permute-start.1 = (bf16[4,224,384]{2,1,0:T(8,128)(2,1)S(1)}, bf16[4,224,384]{2,1,0:T(8,128)(2,1)}, u32[]{:S(2)}, u32[]{:S(2)}) collective-permute-start(bf16[4,224,384]{2,1,0:T(8,128)(2,1)S(1)} %bitcast.22), channel_id=1, source_target_pairs={{8,16},{0,120},{24,32},{16,8},{40,48},{32,24},{56,64},{48,40},{72,... | collective-permute-start | bytes 2064392 | tf_op jit(solution)/shard_map/ppermute | solution.py:41
  46.7 13.6 %collective-permute-start.3 = (bf16[4,224,384]{2,1,0:T(8,128)(2,1)}, bf16[4,224,384]{2,1,0:T(8,128)(2,1)}, u32[]{:S(2)}, u32[]{:S(2)}) collective-permute-start(bf16[4,224,384]{2,1,0:T(8,128)(2,1)} %collective-permute-done.refs_4_), channel_id=1, source_target_pairs={{0,16},{8,120},{16,32},{24,8},{32,48},{40,24},{48,64},{56,40},{64,... | collective-permute-start | bytes 2064392 | tf_op jit(solution)/shard_map/ppermute | solution.py:41
  52.1 20.0 %collective-permute-start.4 = (bf16[4,224,384]{2,1,0:T(8,128)(2,1)}, bf16[4,224,384]{2,1,0:T(8,128)(2,1)}, u32[]{:S(2)}, u32[]{:S(2)}) collective-permute-start(bf16[4,224,384]{2,1,0:T(8,128)(2,1)} %collective-permute-done.1), channel_id=1, source_target_pairs={{0,16},{8,120},{16,32},{24,8},{32,48},{40,24},{48,64},{56,40},{64,... | collective-permute-start | bytes 2064392 | tf_op jit(solution)/shard_map/ppermute | solution.py:41
  54.9 3.2 %copy-start.5 = (bf16[2048]{0:T(1024)(128)(2,1)S(1)}, bf16[2048]{0:T(1024)(128)(2,1)}, u32[]{:S(2)}) copy-start(bf16[2048]{0:T(1024)(128)(2,1)} %param.11) | copy-start | bytes 12292
  60.3 19.6 %collective-permute-start.6 = (bf16[4,224,384]{2,1,0:T(8,128)(2,1)}, bf16[4,224,384]{2,1,0:T(8,128)(2,1)S(1)}, u32[]{:S(2)}, u32[]{:S(2)}) collective-permute-start(bf16[4,224,384]{2,1,0:T(8,128)(2,1)} %collective-permute-done.3.refs_6_), channel_id=1, source_target_pairs={{0,16},{8,120},{16,32},{24,8},{32,48},{40,24},{48,64},{56,40},{64,... | collective-permute-start | bytes 2064392 | tf_op jit(solution)/shard_map/ppermute | solution.py:41
  66.8 17.2 %collective-permute-start.2 = (bf16[4,224,384]{2,1,0:T(8,128)(2,1)}, bf16[4,224,384]{2,1,0:T(8,128)(2,1)S(1)}, u32[]{:S(2)}, u32[]{:S(2)}) collective-permute-start(bf16[4,224,384]{2,1,0:T(8,128)(2,1)} %collective-permute-done.1), channel_id=1, source_target_pairs={{0,8},{8,0},{1,9},{9,1},{2,10},{10,2},{3,11},{11,3},{4,12},{12,4},... | collective-permute-start | bytes 2064392 | tf_op jit(solution)/shard_map/ppermute | solution.py:45
  72.1 12.8 %collective-permute-start.5 = (bf16[4,224,384]{2,1,0:T(8,128)(2,1)}, bf16[4,224,384]{2,1,0:T(8,128)(2,1)}, u32[]{:S(2)}, u32[]{:S(2)}) collective-permute-start(bf16[4,224,384]{2,1,0:T(8,128)(2,1)} %collective-permute-done.4), channel_id=1, source_target_pairs={{0,8},{8,0},{1,9},{9,1},{2,10},{10,2},{3,11},{11,3},{4,12},{12,4},... | collective-permute-start | bytes 2064392 | tf_op jit(solution)/shard_map/ppermute | solution.py:45
  76.9 18.8 %collective-permute-start.7 = (bf16[4,224,384]{2,1,0:T(8,128)(2,1)}, bf16[4,224,384]{2,1,0:T(8,128)(2,1)}, u32[]{:S(2)}, u32[]{:S(2)}) collective-permute-start(bf16[4,224,384]{2,1,0:T(8,128)(2,1)} %collective-permute-done.4), channel_id=1, source_target_pairs={{0,24},{8,112},{16,40},{24,0},{32,56},{40,16},{48,72},{56,32},{64,... | collective-permute-start | bytes 2064392 | tf_op jit(solution)/shard_map/ppermute | solution.py:41
  79.8 4.2 %copy-start.3 = (bf16[4,224,384]{2,1,0:T(8,128)(2,1)}, bf16[4,224,384]{2,1,0:T(8,128)(2,1)S(1)}, u32[]{:S(2)}) copy-start(bf16[4,224,384]{2,1,0:T(8,128)(2,1)S(1)} %collective-permute-done.6.refs_8_) | copy-start | bytes 2064388
  79.9 16.6 %collective-permute-start.8 = (bf16[4,224,384]{2,1,0:T(8,128)(2,1)S(1)}, bf16[4,224,384]{2,1,0:T(8,128)(2,1)}, u32[]{:S(2)}, u32[]{:S(2)}) collective-permute-start(bf16[4,224,384]{2,1,0:T(8,128)(2,1)S(1)} %collective-permute-done.6.refs_8_), channel_id=1, source_target_pairs={{0,16},{8,120},{16,32},{24,8},{32,48},{40,24},{48,64},{56,40},{64,... | collective-permute-start | bytes 2064392 | tf_op jit(solution)/shard_map/ppermute | solution.py:41
  84.0 0.9 copy-start.4
  127.6 5.8 %collective-permute-start.9 = (bf16[320,2048]{1,0:T(8,128)(2,1)}, bf16[320,2048]{1,0:T(8,128)(2,1)S(1)}, u32[]{:S(2)}, u32[]{:S(2)}) collective-permute-start(bf16[320,2048]{1,0:T(8,128)(2,1)} %get-tuple-element.33), channel_id=1, source_target_pairs={{0,8},{8,0},{1,9},{9,1},{2,10},{10,2},{3,11},{11,3},{4,12},{12,4},... | collective-permute-start | bytes 3932168 | tf_op jit(solution)/shard_map/ppermute | solution.py:45
  133.4 1.3 copy-start
  134.7 1.8 copy-start.2
Sparse Core Ops, SparseCore 0:
  10.1 57.0 all-gather.3
  136.6 29.0 reduce-scatter.1

commit v10 on v9

--- a/solution.py
+++ b/solution.py
@@ -391,7 +391,8 @@
     heads = jnp.concatenate([student_head.T, teacher_head.T], axis=0)
     own = lax.all_gather(heads, "x", axis=0, tiled=False)
     blocks, offsets = [own], [0]
-    mine = theirs = own
+    normed = normalize(student_rows, student_gain).T
+    mine, (theirs, normed) = own, lax.optimization_barrier((own, normed))
     for step in range(1, NZ // 2):
         final = step == NZ // 2 - 1
         mine, theirs = along(mine), along(theirs, cross_in=step == 1, cross_out=final)
@@ -401,7 +402,6 @@
             blocks.append(swapped(theirs))
             offsets.append(step)
 
-    normed = normalize(student_rows, student_gain).T
     early = len(blocks)
     blocks += [theirs, along(mine)]
     offsets += [NZ // 2 - 1, -NZ // 2]

time: 218 us -> 216 us (level)
  starting transfers between devices: 44.7 us -> 37.5 us
  waiting for transfers between devices: 15.6 us -> 21.1 us
    ppermute x3, starting transfers between devices: 12.3 us -> 6.72 us  [swapped(): return lax.ppermute(values, 'core', [(0, 1), (1, 0)])]
    ppermute x7, waiting for transfers between devices: 12.7 us -> 18.2 us  [along(): return lax.ppermute(values, ('z', 'core'), pairs)]
    all_to_all x1, blocking collectives: 17.1 us -> 14.6 us  [body(): lse = lax.all_to_all(lse, ('core', 'y'), 0, 0, tiled=True)]
    unnamed x13 -> x19, local copies, waits for them, and re-layouts: 5.34 us -> 6.41 us
where the time goes in v10:
time: 216 us; the launch traced here: 215 us
  blocking collectives  96.3 us (45%)
  starting transfers between devices  37.5 us (17%)
  Pallas kernels  30.6 us (14%)
  waiting for transfers between devices  21.1 us (10%)
  between operations  15 us (7%)
  other arithmetic  8.08 us (4%)
  local copies, waits for them, and re-layouts  6.41 us (3%)
    all_to_all x1, blocking collectives, body(): squares = lax.all_to_all(squares, ('x', 'z', 'core', 'y'), 0, 0, tiled=True)  31.4 us
    ppermute x7, starting transfers between devices, along(): return lax.ppermute(values, ('z', 'core'), pairs)  30.7 us
    all_to_all x1, blocking collectives, body(): lax.all_to_all(head_part.reshape(NX, NZ * fs, vocab), 'x', 0, 0, tiled=True)  23.4 us
    ppermute x7, waiting for transfers between devices, along(): return lax.ppermute(values, ('z', 'core'), pairs)  18.2 us
    all_to_all x1, blocking collectives, body(): lax.all_to_all(head_part.reshape(NZ, fs, vocab), 'z', 0, 0, tiled=True)  15.5 us
    all_to_all x1, blocking collectives, body(): lse = lax.all_to_all(lse, ('core', 'y'), 0, 0, tiled=True)  14.6 us
    all_gather x1, blocking collectives, body(): own = lax.all_gather(heads, 'x', axis=0, tiled=False)  11.4 us
    pallas_call x1, Pallas kernels, most(): pl.pallas_call(kernel, out_shape=(jax.ShapeDtypeStruct((vocab, tokens), F...  10.8 us
  transfers between devices with their start and end apart: 12, of which 4 were waited for; matrix products, arithmetic and copies ran while one was open for 4% of the time, Pallas kernels for 5%

profile of v10, /device:TPU:1, one launch (start us, length us, event | category | flops | bytes accessed | tf_op | source)
XLA Modules:
  0.0 215.0 jit_solution(1019974176146046467)
XLA Ops:
  7.2 0.0 all-gather.4.cloned.1.call-start
  7.2 0.7 convert_element_type.93
  7.9 1.1 fusion.6
  9.1 0.8 pad_maximum_fusion
  9.9 0.0 all-gather.4.cloned.1.call-update
  9.9 0.0 reduce-scatter.2.cloned.1.call-start
  10.0 0.9 pad_maximum_fusion.1
  10.9 11.4 %all-gather.1 = bf16[896,384]{1,0:T(8,128)(2,1)S(1)} all-gather(bf16[224,384]{1,0:T(8,128)(2,1)S(1)} %pad_maximum_fusion.1), channel_id=3, replica_groups=mesh['x'=4,'z'=8,'core'=2,'y'=8] {'x'}, dimensions={0}, use_global_device_ids=true | all-gather | bytes 860160 | tf_op jit(solution)/shard_map/all_gather | solution.py:392
  22.3 0.0 copy-start.1
  22.3 0.0 copy-start.8
  22.3 12.1 %collective-permute-start = (bf16[4,224,384]{2,1,0:T(8,128)(2,1)S(1)}, bf16[4,224,384]{2,1,0:T(8,128)(2,1)}, u32[]{:S(2)}, u32[]{:S(2)}) collective-permute-start(bf16[4,224,384]{2,1,0:T(8,128)(2,1)S(1)} %bitcast.21), channel_id=1, source_target_pairs={{0,16},{8,120},{16,32},{24,8},{32,48},{40,24},{48,64},{56,40},{64,... | collective-permute-start | bytes 2064392 | tf_op jit(solution)/shard_map/ppermute | solution.py:41
  34.4 3.2 %copy.11 = bf16[640,2048]{0,1:T(8,128)(2,1)S(1)} copy(bf16[640,2048]{1,0:T(8,128)(2,1)} %param.10) | data formatting | bytes 5242880 | tf_op args[3]
  37.6 0.0 copy-done.8
  37.6 0.6 fusion
  38.2 2.2 %fusion.3.refs_2_.normed_hbm = bf16[2048,640]{1,0:T(8,128)(2,1)} fusion(bf16[640,2048]{0,1:T(8,128)(2,1)S(1)} %copy.11, f32[2048]{0:T(1024)S(1)} %convert_element_type.102, f32[640]{0:T(1024)S(1)} %add_rsqrt_fusion), kind=kLoop, calls=%fused_computation.5 | loop fusion | flops 5242880 | bytes 5253632 | tf_op jit(solution)/shard_map/transpose | solution.py:394
  40.5 0.0 copy-done.1
  40.5 1.9 collective-permute-start.1
  42.4 0.0 collective-permute-done.refs_4_
  42.4 5.3 %collective-permute-start.3 = (bf16[4,224,384]{2,1,0:T(8,128)(2,1)}, bf16[4,224,384]{2,1,0:T(8,128)(2,1)S(1)}, u32[]{:S(2)}, u32[]{:S(2)}) collective-permute-start(bf16[4,224,384]{2,1,0:T(8,128)(2,1)} %collective-permute-done.refs_4_), channel_id=1, source_target_pairs={{0,16},{8,120},{16,32},{24,8},{32,48},{40,24},{48,64},{56,40},{64,... | collective-permute-start | bytes 2064392 | tf_op jit(solution)/shard_map/ppermute | solution.py:41
  47.7 11.1 %collective-permute-done.1 = bf16[4,224,384]{2,1,0:T(8,128)(2,1)} collective-permute-done((bf16[4,224,384]{2,1,0:T(8,128)(2,1)S(1)}, bf16[4,224,384]{2,1,0:T(8,128)(2,1)}, u32[]{:S(2)}, u32[]{:S(2)}) %collective-permute-start.1) | collective-permute-done | bytes 688160 | tf_op jit(solution)/shard_map/ppermute | solution.py:41
  58.8 1.9 collective-permute-start.4
  60.8 0.0 collective-permute-done.3.refs_6_
  60.8 0.0 copy-start.3
  60.8 3.0 %collective-permute-start.6 = (bf16[4,224,384]{2,1,0:T(8,128)(2,1)S(1)}, bf16[4,224,384]{2,1,0:T(8,128)(2,1)S(1)}, u32[]{:S(2)}, u32[]{:S(2)}) collective-permute-start(bf16[4,224,384]{2,1,0:T(8,128)(2,1)S(1)} %collective-permute-done.3.refs_6_), channel_id=1, source_target_pairs={{0,16},{8,120},{16,32},{24,8},{32,48},{40,24},{48,64},{56,40},{64,... | collective-permute-start | bytes 2064392 | tf_op jit(solution)/shard_map/ppermute | solution.py:41
  63.8 1.9 collective-permute-start.2
  65.8 5.3 %collective-permute-done.4 = bf16[4,224,384]{2,1,0:T(8,128)(2,1)} collective-permute-done((bf16[4,224,384]{2,1,0:T(8,128)(2,1)}, bf16[4,224,384]{2,1,0:T(8,128)(2,1)}, u32[]{:S(2)}, u32[]{:S(2)}) %collective-permute-start.4) | collective-permute-done | bytes 688160 | tf_op jit(solution)/shard_map/ppermute | solution.py:41
  71.0 1.9 collective-permute-start.5
  72.9 3.3 %collective-permute-start.7 = (bf16[4,224,384]{2,1,0:T(8,128)(2,1)}, bf16[4,224,384]{2,1,0:T(8,128)(2,1)S(1)}, u32[]{:S(2)}, u32[]{:S(2)}) collective-permute-start(bf16[4,224,384]{2,1,0:T(8,128)(2,1)} %collective-permute-done.4), channel_id=1, source_target_pairs={{0,24},{8,112},{16,40},{24,0},{32,56},{40,16},{48,72},{56,32},{64,... | collective-permute-start | bytes 2064392 | tf_op jit(solution)/shard_map/ppermute | solution.py:41
  76.3 1.8 collective-permute-done.6.refs_8_
  78.1 0.0 copy-start.4
  78.1 3.1 %collective-permute-start.8 = (bf16[4,224,384]{2,1,0:T(8,128)(2,1)S(1)}, bf16[4,224,384]{2,1,0:T(8,128)(2,1)S(1)}, u32[]{:S(2)}, u32[]{:S(2)}) collective-permute-start(bf16[4,224,384]{2,1,0:T(8,128)(2,1)S(1)} %collective-permute-done.6.refs_8_), channel_id=1, source_target_pairs={{0,16},{8,120},{16,32},{24,8},{32,48},{40,24},{48,64},{56,40},{64,... | collective-permute-start | bytes 2064392 | tf_op jit(solution)/shard_map/ppermute | solution.py:41
  81.9 0.7 pad_add_fusion.refs_0_
  82.5 0.6 pad_add_fusion.1.which_ref
  83.1 0.0 collective-permute-done.2.refs_5_
  83.1 0.0 copy-start.6
  83.1 0.0 collective-permute-done.5.refs_7_
  83.1 0.0 all-gather.4.cloned.1.call-done
  83.1 0.0 copy-done.3
  83.1 0.0 copy-done.4
  83.2 0.8 copy-done.6
  84.0 10.8 %shard_map.86 = (f32[384,640]{1,0:T(8,128)}, f32[384,640]{1,0:T(8,128)}, f32[1,640]{1,0:T(1,128)}, bf16[4,8,64,384]{3,2,1,0:T(8,128)(2,1)}) custom-call(s32[2]{0:T(128)} %pad_add_fusion.refs_0_, bf16[16,336,640]{2,1,0:T(8,128)(2,1)} %bitcast.19, bf16[2048,640]{1,0:T(8,128)(2,1)} %fusion.3.refs_2_.normed_hbm, bf16[4,224,384]{2,1,0:T(8,128)(2,1)} %bitcast.23, ...), custom_call_target="tpu_custom_call" | custom-call | flops 2642411520 | bytes 12582912 | tf_op jit(solution)/shard_map/pallas_call | solution.py:176
  94.8 0.0 collective-permute-done.7.refs_7_
  94.8 0.0 copy-start.5
  94.8 0.0 collective-permute-done.8.refs_8_
  94.8 0.0 copy-start.7
  94.8 0.8 copy-done.5
  95.7 0.3 copy-done.7
  95.9 7.1 %shard_map.87 = (f32[384,640]{1,0:T(8,128)}, f32[384,640]{1,0:T(8,128)}, f32[16,2,640]{2,1,0:T(2,128)}, bf16[4,8,64,384]{3,2,1,0:T(8,128)(2,1)}) custom-call(s32[2]{0:T(128)} %pad_add_fusion.refs_0_, bf16[16,336,640]{2,1,0:T(8,128)(2,1)} %bitcast.20, bf16[2048,640]{1,0:T(8,128)(2,1)} %fusion.3.refs_2_.normed_hbm, ...), custom_call_target="tpu_custom_call", output_to_operand_aliasing={{3}: (6, {})} | custom-call | flops 880803840 | bytes 8388608 | tf_op jit(solution)/shard_map/pallas_call | solution.py:233
  103.1 14.6 %all_to_all.26.lse_ref = f32[16,2,640]{2,1,0:T(2,128)} all-to-all(f32[16,2,640]{2,1,0:T(2,128)} %get-tuple-element.32), channel_id=1, replica_groups=mesh['x'=4,'z'=8,'core'=2,'y'=8] {'core','y'}, dimensions={0} | all-to-all | bytes 163840 | tf_op jit(solution)/shard_map/all_to_all | solution.py:428
  117.7 7.0 %shard_map.88 = (bf16[320,2048]{1,0:T(8,128)(2,1)}, bf16[320,2048]{1,0:T(8,128)(2,1)}, bf16[2048,384]{1,0:T(8,128)(2,1)}) custom-call(s32[2]{0:T(128)} %pad_add_fusion.1.which_ref, f32[384,640]{1,0:T(8,128)} %get-tuple-element.30.student_hbm, f32[384,640]{1,0:T(8,128)} %get-tuple-element.31.teacher_hbm, f32[16,2,640]{2,1,0:T(2,128)} %all_to_all.26.lse_ref, ...), custom_call_target="tpu_custom_call" | custom-call | flops 2013265920 | bytes 10485760 | tf_op jit(solution)/shard_map/pallas_call | solution.py:307
  124.7 2.9 %collective-permute-start.9 = (bf16[320,2048]{1,0:T(8,128)(2,1)}, bf16[320,2048]{1,0:T(8,128)(2,1)S(1)}, u32[]{:S(2)}, u32[]{:S(2)}) collective-permute-start(bf16[320,2048]{1,0:T(8,128)(2,1)} %get-tuple-element.37), channel_id=1, source_target_pairs={{0,8},{8,0},{1,9},{9,1},{2,10},{10,2},{3,11},{11,3},{4,12},{12,4},... | collective-permute-start | bytes 3932168 | tf_op jit(solution)/shard_map/ppermute | solution.py:45
  127.6 2.9 %collective-permute-done.9.right_ref = bf16[320,2048]{1,0:T(8,128)(2,1)S(1)} collective-permute-done((bf16[320,2048]{1,0:T(8,128)(2,1)}, bf16[320,2048]{1,0:T(8,128)(2,1)S(1)}, u32[]{:S(2)}, u32[]{:S(2)}) %collective-permute-start.9) | collective-permute-done | bytes 1310752 | tf_op jit(solution)/shard_map/ppermute | solution.py:45
  130.5 0.0 copy-start
  130.5 1.3 copy-done
  131.8 0.0 copy-start.2
  131.8 1.7 shard_map.89
  133.5 0.0 reduce-scatter.2.cloned.1.call-update
  133.5 0.0 copy-done.2
  133.5 23.4 %all_to_all.27 = bf16[4,512,384]{2,1,0:T(8,128)(2,1)S(1)} all-to-all(bf16[4,512,384]{2,1,0:T(8,128)(2,1)S(1)} %bitcast.24), channel_id=1, replica_groups=mesh['x'=4,'z'=8,'core'=2,'y'=8] {'x'}, dimensions={0} | all-to-all | bytes 3145728 | tf_op jit(solution)/shard_map/all_to_all | solution.py:437
  156.9 0.4 reduce_sum.35
  157.4 15.5 %all_to_all.28.parts_ref = bf16[8,64,384]{2,1,0:T(8,128)(2,1)} all-to-all(bf16[8,64,384]{2,1,0:T(8,128)(2,1)S(1)} %bitcast.25), channel_id=1, replica_groups=mesh['x'=4,'z'=8,'core'=2,'y'=8] {'z'}, dimensions={0} | all-to-all | bytes 786432 | tf_op jit(solution)/shard_map/all_to_all | solution.py:439
  172.9 2.0 shard_map.90
  174.9 31.4 %all_to_all.29 = f32[512,1,128]{2,1,0:T(1,128)} all-to-all(f32[512,1,128]{2,1,0:T(1,128)} %bitcast.28), channel_id=1, replica_groups=mesh['x'=4,'z'=8,'core'=2,'y'=8] {'x','z','core','y'}, dimensions={0} | all-to-all | bytes 524288 | tf_op jit(solution)/shard_map/all_to_all | solution.py:449
  206.3 1.9 shard_map.91
  (6 shorter events, 0.0 us)
Async XLA Ops:
  7.2 76.0 %all-gather.4.cloned.1.call-start = ((), (), s32[]{:S(2)}) async-start(), calls=%async_computation.6 | async-start | bytes 7311360 | tf_op jit(solution)/shard_map/all_gather | solution.py:389
  9.9 163.0 %reduce-scatter.2.cloned.1.call-start = ((), (), s32[]{:S(2)}) async-start(), calls=%async_computation.5 | async-start | bytes 1474560 | tf_op jit(solution)/shard_map/reduce_scatter | solution.py:435
  22.3 18.1 %copy-start.1 = (bf16[896,384]{1,0:T(8,128)(2,1)}, bf16[896,384]{1,0:T(8,128)(2,1)S(1)}, u32[]{:S(2)}) copy-start(bf16[896,384]{1,0:T(8,128)(2,1)S(1)} %all-gather.1) | copy-start | bytes 2064388
  22.3 15.3 %copy-start.8 = (bf16[2048]{0:T(1024)(128)(2,1)S(1)}, bf16[2048]{0:T(1024)(128)(2,1)}, u32[]{:S(2)}) copy-start(bf16[2048]{0:T(1024)(128)(2,1)} %param.11) | copy-start | bytes 12292
  22.3 20.1 %collective-permute-start = (bf16[4,224,384]{2,1,0:T(8,128)(2,1)S(1)}, bf16[4,224,384]{2,1,0:T(8,128)(2,1)}, u32[]{:S(2)}, u32[]{:S(2)}) collective-permute-start(bf16[4,224,384]{2,1,0:T(8,128)(2,1)S(1)} %bitcast.21), channel_id=1, source_target_pairs={{0,16},{8,120},{16,32},{24,8},{32,48},{40,24},{48,64},{56,40},{64,... | collective-permute-start | bytes 2064392 | tf_op jit(solution)/shard_map/ppermute | solution.py:41
  40.5 18.4 %collective-permute-start.1 = (bf16[4,224,384]{2,1,0:T(8,128)(2,1)S(1)}, bf16[4,224,384]{2,1,0:T(8,128)(2,1)}, u32[]{:S(2)}, u32[]{:S(2)}) collective-permute-start(bf16[4,224,384]{2,1,0:T(8,128)(2,1)S(1)} %bitcast.22), channel_id=1, source_target_pairs={{8,16},{0,120},{24,32},{16,8},{40,48},{32,24},{56,64},{48,40},{72,... | collective-permute-start | bytes 2064392 | tf_op jit(solution)/shard_map/ppermute | solution.py:41
  42.4 18.4 %collective-permute-start.3 = (bf16[4,224,384]{2,1,0:T(8,128)(2,1)}, bf16[4,224,384]{2,1,0:T(8,128)(2,1)S(1)}, u32[]{:S(2)}, u32[]{:S(2)}) collective-permute-start(bf16[4,224,384]{2,1,0:T(8,128)(2,1)} %collective-permute-done.refs_4_), channel_id=1, source_target_pairs={{0,16},{8,120},{16,32},{24,8},{32,48},{40,24},{48,64},{56,40},{64,... | collective-permute-start | bytes 2064392 | tf_op jit(solution)/shard_map/ppermute | solution.py:41
  58.8 12.2 %collective-permute-start.4 = (bf16[4,224,384]{2,1,0:T(8,128)(2,1)}, bf16[4,224,384]{2,1,0:T(8,128)(2,1)}, u32[]{:S(2)}, u32[]{:S(2)}) collective-permute-start(bf16[4,224,384]{2,1,0:T(8,128)(2,1)} %collective-permute-done.1), channel_id=1, source_target_pairs={{0,16},{8,120},{16,32},{24,8},{32,48},{40,24},{48,64},{56,40},{64,... | collective-permute-start | bytes 2064392 | tf_op jit(solution)/shard_map/ppermute | solution.py:41
  60.8 22.4 %copy-start.3 = (bf16[4,224,384]{2,1,0:T(8,128)(2,1)}, bf16[4,224,384]{2,1,0:T(8,128)(2,1)S(1)}, u32[]{:S(2)}) copy-start(bf16[4,224,384]{2,1,0:T(8,128)(2,1)S(1)} %collective-permute-done.3.refs_6_) | copy-start | bytes 2064388
  60.8 17.3 %collective-permute-start.6 = (bf16[4,224,384]{2,1,0:T(8,128)(2,1)S(1)}, bf16[4,224,384]{2,1,0:T(8,128)(2,1)S(1)}, u32[]{:S(2)}, u32[]{:S(2)}) collective-permute-start(bf16[4,224,384]{2,1,0:T(8,128)(2,1)S(1)} %collective-permute-done.3.refs_6_), channel_id=1, source_target_pairs={{0,16},{8,120},{16,32},{24,8},{32,48},{40,24},{48,64},{56,40},{64,... | collective-permute-start | bytes 2064392 | tf_op jit(solution)/shard_map/ppermute | solution.py:41
  63.8 19.3 %collective-permute-start.2 = (bf16[4,224,384]{2,1,0:T(8,128)(2,1)}, bf16[4,224,384]{2,1,0:T(8,128)(2,1)S(1)}, u32[]{:S(2)}, u32[]{:S(2)}) collective-permute-start(bf16[4,224,384]{2,1,0:T(8,128)(2,1)} %collective-permute-done.1), channel_id=1, source_target_pairs={{0,8},{8,0},{1,9},{9,1},{2,10},{10,2},{3,11},{11,3},{4,12},{12,4},... | collective-permute-start | bytes 2064392 | tf_op jit(solution)/shard_map/ppermute | solution.py:45
  71.0 12.1 %collective-permute-start.5 = (bf16[4,224,384]{2,1,0:T(8,128)(2,1)}, bf16[4,224,384]{2,1,0:T(8,128)(2,1)}, u32[]{:S(2)}, u32[]{:S(2)}) collective-permute-start(bf16[4,224,384]{2,1,0:T(8,128)(2,1)} %collective-permute-done.4), channel_id=1, source_target_pairs={{0,8},{8,0},{1,9},{9,1},{2,10},{10,2},{3,11},{11,3},{4,12},{12,4},... | collective-permute-start | bytes 2064392 | tf_op jit(solution)/shard_map/ppermute | solution.py:45
  72.9 21.9 %collective-permute-start.7 = (bf16[4,224,384]{2,1,0:T(8,128)(2,1)}, bf16[4,224,384]{2,1,0:T(8,128)(2,1)S(1)}, u32[]{:S(2)}, u32[]{:S(2)}) collective-permute-start(bf16[4,224,384]{2,1,0:T(8,128)(2,1)} %collective-permute-done.4), channel_id=1, source_target_pairs={{0,24},{8,112},{16,40},{24,0},{32,56},{40,16},{48,72},{56,32},{64,... | collective-permute-start | bytes 2064392 | tf_op jit(solution)/shard_map/ppermute | solution.py:41
  78.1 5.0 %copy-start.4 = (bf16[4,224,384]{2,1,0:T(8,128)(2,1)}, bf16[4,224,384]{2,1,0:T(8,128)(2,1)S(1)}, u32[]{:S(2)}) copy-start(bf16[4,224,384]{2,1,0:T(8,128)(2,1)S(1)} %collective-permute-done.6.refs_8_) | copy-start | bytes 2064388
  78.1 16.7 %collective-permute-start.8 = (bf16[4,224,384]{2,1,0:T(8,128)(2,1)S(1)}, bf16[4,224,384]{2,1,0:T(8,128)(2,1)S(1)}, u32[]{:S(2)}, u32[]{:S(2)}) collective-permute-start(bf16[4,224,384]{2,1,0:T(8,128)(2,1)S(1)} %collective-permute-done.6.refs_8_), channel_id=1, source_target_pairs={{0,16},{8,120},{16,32},{24,8},{32,48},{40,24},{48,64},{56,40},{64,... | collective-permute-start | bytes 2064392 | tf_op jit(solution)/shard_map/ppermute | solution.py:41
  83.1 0.9 copy-start.6
  94.8 0.9 copy-start.5
  94.8 1.1 copy-start.7
  124.7 5.8 %collective-permute-start.9 = (bf16[320,2048]{1,0:T(8,128)(2,1)}, bf16[320,2048]{1,0:T(8,128)(2,1)S(1)}, u32[]{:S(2)}, u32[]{:S(2)}) collective-permute-start(bf16[320,2048]{1,0:T(8,128)(2,1)} %get-tuple-element.37), channel_id=1, source_target_pairs={{0,8},{8,0},{1,9},{9,1},{2,10},{10,2},{3,11},{11,3},{4,12},{12,4},... | collective-permute-start | bytes 3932168 | tf_op jit(solution)/shard_map/ppermute | solution.py:45
  130.5 1.3 copy-start
  131.8 1.8 copy-start.2
Sparse Core Ops, SparseCore 0:
  10.1 57.1 all-gather.3
  133.7 30.9 reduce-scatter.1
